TPU v7x, 256 devices: a whole 4x4x8 slice. The times are simulated.
256 devices in a mesh: tm: 32 (over x, z_lo, y), batch: 8 (over z_hi, core).
Axes of the slice: x: 4, y: 4, z: 8 (z_hi: 4, z_lo: 2; z = z_hi * 2 + z_lo), core: 2. Of those that a mesh axis runs over, the one named last changes fastest.
Arguments:
- inputs: bfloat16 [8, 8192, 512], P('batch', 'tm'), may hold values from -6 to 6
- cotangent: bfloat16 [8, 8192, 512], P('batch', 'tm'), may hold values from -6 to 6
- w_pos: float32 [64, 64], replicated, may hold values from -0.75 to 0.75
- w_filt: float32 [64, 512], replicated, may hold values from -0.75 to 0.75
- log_rates: float32 [512], replicated, may hold values from -9.5 to -3.5
- skip_gain: float32 [512], replicated, may hold values from 0.5 to 1.5
- w_conv: bfloat16 [512, 5, 512], replicated, may hold values from -0.125 to 0.125
Outputs:
- mixed: bfloat16 [8, 8192, 512], P('batch', 'tm')
- input_grad: bfloat16 [8, 8192, 512], P('batch', 'tm')
- conv_grad: float32 [512, 5, 512], P('tm')
- pos_grad: float32 [64, 64], replicated
- filt_grad: float32 [64, 512], replicated
- rates_grad: float32 [512], replicated
- skip_grad: float32 [512], replicated
All inputs are finite; a program needn't handle non-finite values.
Results may differ from a plain program's by a relative error of at most 0.0051.
Values may be sent and summed in bfloat16 or wider, within the bound.
No kernel may reach another device: no remote copies, remote signals or barrier semaphores. Data moves between devices by JAX's collectives and lax.ppermute only.
A program may use at most 64 MiB of HBM per device.

v0:
```python
import math

import jax
import jax.numpy as jnp
import numpy as np
from jax import lax
from jax.sharding import PartitionSpec as P

PRECISE = lax.Precision.HIGHEST


def from_behind(block, axis, distance):
    devices = range(lax.axis_size(axis))
    route = [(i - distance, i) for i in devices if i - distance in devices]
    return lax.ppermute(block, axis, route)


def multipliers(half_width, length):
    return np.array(
        [
            1 + index * index * length // (2 * half_width * half_width)
            for index in range(half_width)
        ],
        dtype=np.int32,
    )


def features(positions, length, width):
    half_width = width // 2
    factor = jnp.asarray(multipliers(half_width, length))
    phase_int = positions[:, None] * factor[None, :] % length
    angles = 2.0 * math.pi / length * phase_int.astype(jnp.float32)
    return jnp.concatenate([jnp.sin(angles), jnp.cos(angles)], axis=1)


def filter_taps(w_pos, w_filt, log_rates, positions, length):
    hidden = jnp.sin(jnp.dot(features(positions, length, w_pos.shape[0]), w_pos, precision=PRECISE))
    shaped = jnp.dot(hidden, w_filt, precision=PRECISE)
    decay_rates = jnp.exp(log_rates)
    step_times = positions.astype(jnp.float32)
    return (
        shaped
        * jnp.sqrt(decay_rates)[None, :]
        * jnp.exp(-step_times[:, None] * decay_rates[None, :])
    )


def gelu_value(values):
    return jax.nn.gelu(values, approximate=True)


def spectral_tables(num_parts, num_rows, my_rank):
    block_rows = num_rows // num_parts
    length = 2 * num_parts * num_rows
    freq_index = jnp.arange(2 * num_parts, dtype=jnp.int32)
    part_index = jnp.arange(num_parts, dtype=jnp.int32)
    outer_angle = (
        2.0
        * math.pi
        / (2 * num_parts)
        * (freq_index[:, None] * part_index[None, :] % (2 * num_parts)).astype(jnp.float32)
    )
    inner_index = jnp.arange(num_rows, dtype=jnp.int32)
    inner_angle = (
        2.0
        * math.pi
        / num_rows
        * (inner_index[:, None] * inner_index[None, :] % num_rows).astype(jnp.float32)
    )
    global_rows = my_rank * block_rows + jnp.arange(block_rows, dtype=jnp.int32)
    twist_angle = (
        2.0
        * math.pi
        / length
        * (freq_index[:, None] * global_rows[None, :] % length).astype(jnp.float32)
    )
    return (
        jnp.cos(outer_angle),
        jnp.sin(outer_angle),
        jnp.cos(inner_angle),
        jnp.sin(inner_angle),
        jnp.cos(twist_angle)[None, :, :, None],
        jnp.sin(twist_angle)[None, :, :, None],
    )


def to_spectrum(signals, tables):
    outer_cos, outer_sin, inner_cos, inner_sin, twist_cos, twist_sin = tables
    num_sig, num_rows, width = signals.shape
    columns = lax.all_to_all(
        signals.reshape(num_sig, 1, num_rows, width), "tm", split_axis=2, concat_axis=1, tiled=True
    )
    columns = columns.astype(jnp.float32)
    real_part = jnp.einsum("ap,spjc->sajc", outer_cos, columns, precision=PRECISE)
    imag_part = -jnp.einsum("ap,spjc->sajc", outer_sin, columns, precision=PRECISE)
    twisted_real = real_part * twist_cos + imag_part * twist_sin
    twisted_imag = imag_part * twist_cos - real_part * twist_sin
    spread = lax.all_to_all(
        jnp.stack([twisted_real, twisted_imag]), "tm", split_axis=2, concat_axis=3, tiled=True
    )
    bins_real = jnp.einsum("bj,sajc->sabc", inner_cos, spread[0], precision=PRECISE) + jnp.einsum(
        "bj,sajc->sabc", inner_sin, spread[1], precision=PRECISE
    )
    bins_imag = jnp.einsum("bj,sajc->sabc", inner_cos, spread[1], precision=PRECISE) - jnp.einsum(
        "bj,sajc->sabc", inner_sin, spread[0], precision=PRECISE
    )
    return (bins_real, bins_imag)


def from_spectrum(bins_real, bins_imag, tables):
    outer_cos, outer_sin, inner_cos, inner_sin, twist_cos, twist_sin = tables
    length = 2 * outer_cos.shape[1] * inner_cos.shape[0]
    mixed_real = jnp.einsum("jb,sabc->sajc", inner_cos, bins_real, precision=PRECISE) - jnp.einsum(
        "jb,sabc->sajc", inner_sin, bins_imag, precision=PRECISE
    )
    mixed_imag = jnp.einsum("jb,sabc->sajc", inner_cos, bins_imag, precision=PRECISE) + jnp.einsum(
        "jb,sabc->sajc", inner_sin, bins_real, precision=PRECISE
    )
    gathered = lax.all_to_all(
        jnp.stack([mixed_real, mixed_imag]), "tm", split_axis=3, concat_axis=2, tiled=True
    )
    back_real = gathered[0] * twist_cos - gathered[1] * twist_sin
    back_imag = gathered[1] * twist_cos + gathered[0] * twist_sin
    values = (
        jnp.einsum("ap,sajc->spjc", outer_cos, back_real, precision=PRECISE)
        - jnp.einsum("ap,sajc->spjc", outer_sin, back_imag, precision=PRECISE)
    ) / length
    result = lax.all_to_all(values, "tm", split_axis=1, concat_axis=2, tiled=True)
    return result[:, 0]


def on_device(inputs, cotangent, w_pos, w_filt, log_rates, skip_gain, w_conv):
    num_parts = lax.axis_size("tm")
    my_rank = lax.axis_index("tm")
    signal = inputs[0]
    upstream = cotangent[0]
    num_rows, width = signal.shape
    kernel = w_conv.shape[1]
    length = num_rows * num_parts
    positions = my_rank * num_rows + jnp.arange(num_rows, dtype=jnp.int32)
    tables = spectral_tables(num_parts, num_rows, my_rank)
    tap_values = filter_taps(w_pos, w_filt, log_rates, positions, length).astype(jnp.bfloat16)
    bins_real, bins_imag = to_spectrum(jnp.stack([signal, tap_values]), tables)
    sig_real, tap_real = (bins_real[0], bins_real[1])
    sig_imag, tap_imag = (bins_imag[0], bins_imag[1])
    prod_real = sig_real * tap_real - sig_imag * tap_imag
    prod_imag = sig_real * tap_imag + sig_imag * tap_real
    long_part = from_spectrum(prod_real[None], prod_imag[None], tables)[0]
    signal_wide = signal.astype(jnp.float32)
    before = long_part + skip_gain[None, :] * signal_wide
    active = gelu_value(before).astype(jnp.bfloat16)
    earlier = from_behind(active[num_rows - (kernel - 1) :], "tm", 1)
    extended = jnp.concatenate([earlier, active], axis=0)
    later = from_behind(upstream[: kernel - 1], "tm", -1)
    reaching = jnp.concatenate([upstream, later], axis=0)
    mixed = jnp.zeros((num_rows, width), jnp.float32)
    grad_active = jnp.zeros((num_rows, width), jnp.float32)
    for offset in range(kernel):
        window = extended[kernel - 1 - offset : kernel - 1 - offset + num_rows]
        mixed = mixed + jnp.dot(window, w_conv[:, offset, :], preferred_element_type=jnp.float32)
        grad_active = grad_active + jnp.einsum(
            "td,cd->tc",
            reaching[offset : offset + num_rows],
            w_conv[:, offset, :],
            preferred_element_type=jnp.float32,
        )
    grad_before = jax.vjp(gelu_value, before)[1](grad_active)[0].astype(jnp.bfloat16)
    grad_wide = grad_before.astype(jnp.float32)
    grad_real, grad_imag = to_spectrum(grad_before[None], tables)
    grad_real, grad_imag = (grad_real[0], grad_imag[0])
    back_real = tap_real * grad_real + tap_imag * grad_imag
    back_imag = tap_real * grad_imag - tap_imag * grad_real
    corr_real = sig_real * grad_real + sig_imag * grad_imag
    corr_imag = sig_real * grad_imag - sig_imag * grad_real
    joined = from_spectrum(
        jnp.stack([back_real, corr_real]), jnp.stack([back_imag, corr_imag]), tables
    )
    long_grad = joined[0]
    grad_taps = joined[1]
    input_grad = (long_grad + skip_gain[None, :] * grad_wide).astype(jnp.bfloat16)

    def taps_of(pos_weight, filt_weight, rate_logs):
        return filter_taps(pos_weight, filt_weight, rate_logs, positions, length)

    pullback = jax.vjp(taps_of, w_pos, w_filt, log_rates)[1]
    local_pos, local_filt, local_rates = pullback(grad_taps)
    local_skip = jnp.sum(grad_wide * signal_wide, axis=0)
    total_pos, total_filt, total_rates, total_skip = lax.psum(
        (local_pos, local_filt, local_rates, local_skip), ("tm", "batch")
    )
    pieces = [
        jnp.einsum(
            "tc,td->cd",
            extended[kernel - 1 - offset : kernel - 1 - offset + num_rows],
            upstream,
            preferred_element_type=jnp.float32,
        )
        for offset in range(kernel)
    ]
    conv_part = lax.psum_scatter(jnp.stack(pieces, axis=1), "tm", scatter_dimension=0, tiled=True)
    conv_total = lax.psum(conv_part, "batch")
    scale = 1.0 / math.sqrt(lax.axis_size("batch") * length)
    return (
        mixed.astype(jnp.bfloat16)[None],
        input_grad[None],
        conv_total * scale,
        total_pos * scale,
        total_filt * scale,
        total_rates * scale,
        total_skip * scale,
    )


def solution(mesh):
    in_specs = (P("batch", "tm", None), P("batch", "tm", None), P(), P(), P(), P(), P())
    out_specs = (
        P("batch", "tm", None),
        P("batch", "tm", None),
        P("tm", None, None),
        P(),
        P(),
        P(),
        P(),
    )
    return jax.shard_map(
        on_device, mesh=mesh, in_specs=in_specs, out_specs=out_specs, check_vma=False
    )
```

profile of v0, /device:TPU:1, one launch (start us, length us, event | category | flops | bytes accessed | tf_op | source)
XLA Modules:
  0.0 789.5 jit_solution(2728428579427719830)
XLA Ops:
  9.7 1.8 fusion.378
  14.7 9.2 %all-to-all-start = ((bf16[2,1,256,512]{3,0,1,2:T(2,128)(2,1)}), bf16[2,1,256,512]{3,0,1,2:T(2,128)(2,1)S(1)}, u32[]{:S(2)}, u32[]{:S(2)}) async-start(bf16[2,1,256,512]{3,0,1,2:T(2,128)(2,1)} %copy.146), calls=%async_computation | async-start | bytes 1048576 | tf_op jit(solution)/shard_map/all_to_all | solution.py:90
  24.0 9.7 %all-to-all-done = bf16[2,1,256,512]{3,0,1,2:T(2,128)(2,1)S(1)} async-done(((bf16[2,1,256,512]{3,0,1,2:T(2,128)(2,1)}), bf16[2,1,256,512]{3,0,1,2:T(2,128)(2,1)S(1)}, u32[]{:S(2)}, u32[]{:S(2)}) %all-to-all-start) | async-done | bytes 524320 | tf_op jit(solution)/shard_map/all_to_all | solution.py:90
  35.0 1.9 fusion.9
  37.6 2.4 copy.150
  40.0 51.8 %all_to_all.99 = f32[2,2,64,8,512]{4,3,1,0,2:T(8,128)S(1)} all-to-all(f32[2,2,64,8,512]{4,3,1,0,2:T(8,128)S(1)} %copy.150), channel_id=1, replica_groups=mesh['tm'=32,'batch'=8] {'tm'}, dimensions={2} | all-to-all | bytes 8388608 | tf_op jit(solution)/shard_map/all_to_all | solution.py:98
  93.2 4.4 fusion
  97.7 4.4 fusion.2
  102.1 4.7 subtract_bitcast_fusion.1
  106.8 4.5 add_bitcast_fusion.1
  112.6 2.0 fusion.71
  114.6 2.0 fusion.67
  116.6 2.2 fusion.44
  118.8 2.0 fusion.43
  120.8 1.5 pad_maximum_fusion.2
  122.3 4.2 copy.158
  126.5 5.1 all-to-all-start.2
  133.7 22.3 %all-to-all-done.2 = f32[2,1,2,256,512]{4,2,1,0,3:T(2,128)} async-done(((f32[2,1,2,256,512]{4,2,1,0,3:T(2,128)}), f32[2,1,2,256,512]{4,2,1,0,3:T(2,128)}, u32[]{:S(2)}, u32[]{:S(2)}) %all-to-all-start.2) | async-done | bytes 2097184 | tf_op jit(solution)/shard_map/all_to_all | solution.py:119
  155.9 2.3 copy.257
  162.7 7.7 all-to-all-start.3
  170.3 1.4 fusion.119
  171.7 2.2 fusion.107
  173.9 2.2 fusion.111
  176.1 2.2 convolution_add_fusion.3
  179.5 2.3 fusion.98
  184.2 3.8 reduce
  188.0 1.8 reshape.244
  189.7 14.8 %all_to_all.100 = bf16[32,2,2048]{2,1,0:T(2,128)(2,1)} all-to-all(bf16[32,2,2048]{2,1,0:T(2,128)(2,1)} %reshape.244), channel_id=1, replica_groups=mesh['tm'=32,'batch'=8] {'tm'}, dimensions={0} | all-to-all | bytes 524288 | tf_op jit(solution)/shard_map/all_to_all | solution.py:90
  204.5 2.8 reshape.245
  211.7 26.6 %all_to_all.101 = f32[2,1,64,8,512]{4,3,1,0,2:T(8,128)S(1)} all-to-all(f32[2,1,64,8,512]{4,3,1,0,2:T(8,128)S(1)} %copy.171), channel_id=1, replica_groups=mesh['tm'=32,'batch'=8] {'tm'}, dimensions={2} | all-to-all | bytes 4194304 | tf_op jit(solution)/shard_map/all_to_all | solution.py:98
  238.7 2.7 fusion.59
  241.3 2.7 fusion.63
  244.0 2.7 fusion.42
  246.7 3.1 multiply_add_fusion.1
  249.9 3.0 fusion.24
  252.9 2.8 fusion.25
  255.7 2.9 subtract_bitcast_fusion
  258.6 2.9 add_bitcast_fusion
  261.5 2.4 pad_maximum_fusion.1
  263.9 7.3 copy.179
  271.2 49.0 %all_to_all.102 = f32[2,2,2,256,512]{4,2,1,0,3:T(2,128)S(1)} all-to-all(f32[2,2,2,256,512]{4,2,1,0,3:T(2,128)} %copy.179), channel_id=1, replica_groups=mesh['tm'=32,'batch'=8] {'tm'}, dimensions={3} | all-to-all | bytes 8388608 | tf_op jit(solution)/shard_map/all_to_all | solution.py:119
  320.2 2.4 copy.256
  322.6 2.0 fusion.374
  324.6 2.9 copy.182
  327.5 2.7 squeeze.76
  330.2 4.5 copy.181
  334.8 3.9 squeeze.75
  338.6 3.3 fusion.12
  342.0 1.7 fusion.48
  343.7 1.6 copy.183
  345.3 8.9 %all-to-all-start.7 = ((f32[2,32,8,512]{3,2,0,1:T(8,128)}), f32[2,32,8,512]{3,2,0,1:T(8,128)S(1)}, u32[]{:S(2)}, u32[]{:S(2)}) async-start(f32[2,32,8,512]{3,2,0,1:T(8,128)} %copy.183), calls=%async_computation.7 | async-start | bytes 2097152 | tf_op jit(solution)/shard_map/all_to_all | solution.py:128
  354.6 13.0 %all-to-all-done.7 = f32[2,32,8,512]{3,2,0,1:T(8,128)S(1)} async-done(((f32[2,32,8,512]{3,2,0,1:T(8,128)}), f32[2,32,8,512]{3,2,0,1:T(8,128)S(1)}, u32[]{:S(2)}, u32[]{:S(2)}) %all-to-all-start.7) | async-done | bytes 1048608 | tf_op jit(solution)/shard_map/all_to_all | solution.py:128
  367.6 1.8 multiply_reduce_fusion
  369.4 3.0 collective-permute-start
  377.6 1.4 fusion.35
  379.1 1.4 fusion.121
  381.7 86.2 %all-reduce = (f32[64,64]{1,0:T(8,128)S(1)}, f32[512]{0:T(512)S(1)}, f32[512]{0:T(512)S(1)}) all-reduce(f32[64,64]{1,0:T(8,128)S(1)} %fusion.213, f32[512]{0:T(512)S(1)} %fusion.251, f32[512]{0:T(512)S(1)} %copy-done.19), channel_id=1, replica_groups=mesh['tm'=32,'batch'=8] {'tm','batch'}, use_global_device_ids=true, to_apply=%region_2.3 | all-reduce | flops 5120 | bytes 40960 | tf_op jit(solution)/shard_map/psum | solution.py:188
  473.1 1.4 convolution_add_fusion.5
  474.5 2.1 fusion.58
  476.6 60.2 %reduce-scatter.2.cloned.1.call-done = f32[16,5,512]{2,0,1:T(8,128)} async-done(((f32[512,5,512]{2,0,1:T(8,128)}), f32[16,5,512]{2,0,1:T(8,128)}) %reduce-scatter.2.cloned.1.call-update) | async-done | bytes 163856 | tf_op jit(solution)/shard_map/reduce_scatter | solution.py:200
  536.8 171.8 %all-reduce.6.cloned.1.call-done = f32[64,512]{1,0:T(8,128)} async-done(((f32[64,512]{1,0:T(8,128)}), f32[64,512]{1,0:T(8,128)}) %all-reduce.6.cloned.1.call-update) | async-done | bytes 131088 | tf_op jit(solution)/shard_map/psum | solution.py:188
  708.7 1.6 broadcast_multiply_fusion.1
  710.2 69.8 %all-reduce.4.cloned.1.call-done = f32[16,5,512]{2,0,1:T(8,128)} async-done(((f32[16,5,512]{2,0,1:T(8,128)}), f32[16,5,512]{2,0,1:T(8,128)}) %all-reduce.4.cloned.1.call-update) | async-done | bytes 163856 | tf_op jit(solution)/shard_map/psum | solution.py:201
  780.0 1.6 broadcast_multiply_fusion
  (103 shorter events, 36.4 us)
Async XLA Ops:
  8.0 3.5 copy-start
  8.0 6.6 copy-start.15
  9.7 2.5 copy-start.8
  9.7 2.5 copy-start.10
  11.5 0.7 copy-start.13
  14.7 19.1 %all-to-all-start = ((bf16[2,1,256,512]{3,0,1,2:T(2,128)(2,1)}), bf16[2,1,256,512]{3,0,1,2:T(2,128)(2,1)S(1)}, u32[]{:S(2)}, u32[]{:S(2)}) async-start(bf16[2,1,256,512]{3,0,1,2:T(2,128)(2,1)} %copy.146), calls=%async_computation | async-start | bytes 1048576 | tf_op jit(solution)/shard_map/all_to_all | solution.py:90
  111.3 1.4 copy-start.3
  126.5 5.1 copy-start.2
  126.5 29.5 %all-to-all-start.2 = ((f32[2,1,2,256,512]{4,2,1,0,3:T(2,128)}), f32[2,1,2,256,512]{4,2,1,0,3:T(2,128)}, u32[]{:S(2)}, u32[]{:S(2)}) async-start(f32[2,1,2,256,512]{4,2,1,0,3:T(2,128)} %copy.158), calls=%async_computation.2 | async-start | bytes 4194304 | tf_op jit(solution)/shard_map/all_to_all | solution.py:119
  132.2 39.5 %collective-permute-start.1 = (bf16[4,512]{1,0:T(4,128)(2,1)}, bf16[4,512]{1,0:T(4,128)(2,1)}, u32[]{:S(2)}, u32[]{:S(2)}) collective-permute-start(bf16[4,512]{1,0:T(4,128)(2,1)} %slice_bitcast_fusion.2), channel_id=1, source_target_pairs={{8,0},{16,8},{24,16},{32,24},{40,32},{48,40},{56,48},{64,56},{72,6... | collective-permute-start | bytes 12296 | tf_op jit(solution)/shard_map/ppermute | solution.py:15
  162.7 16.8 %all-to-all-start.3 = ((f32[1,32,8,512]{3,2,0,1:T(8,128)}), f32[1,32,8,512]{3,2,0,1:T(8,128)S(1)}, u32[]{:S(2)}, u32[]{:S(2)}) async-start(f32[1,32,8,512]{3,2,0,1:T(8,128)} %copy.166), calls=%async_computation.3 | async-start | bytes 1048576 | tf_op jit(solution)/shard_map/all_to_all | solution.py:128
  181.7 0.7 copy-start.6
  244.0 2.7 copy-start.4
  338.6 3.3 copy-start.1
  343.7 10.6 %copy-start.5 = (bf16[1,256,512]{2,1,0:T(8,128)(2,1)S(1)}, bf16[1,256,512]{2,1,0:T(8,128)(2,1)}, u32[]{:S(2)}) copy-start(bf16[1,256,512]{2,1,0:T(8,128)(2,1)} %param.9) | copy-start | bytes 786436
  343.7 10.6 %copy-start.18 = (f32[512]{0:T(512)S(1)}, f32[512]{0:T(512)}, u32[]{:S(2)}) copy-start(f32[512]{0:T(512)} %param.14) | copy-start | bytes 6148
  345.3 22.3 %copy-start.7 = (bf16[256,512]{1,0:T(8,128)(2,1)S(1)}, bf16[256,512]{1,0:T(8,128)(2,1)}, u32[]{:S(2)}) copy-start(bf16[256,512]{1,0:T(8,128)(2,1)} %copy-done.6) | copy-start | bytes 786436
  345.3 22.3 %copy-start.16 = (f32[256]{0:T(256)S(1)}, f32[256]{0:T(256)}, u32[]{:S(2)}) copy-start(f32[256]{0:T(256)} %copy-done.15) | copy-start | bytes 3076
  345.3 22.3 %all-to-all-start.7 = ((f32[2,32,8,512]{3,2,0,1:T(8,128)}), f32[2,32,8,512]{3,2,0,1:T(8,128)S(1)}, u32[]{:S(2)}, u32[]{:S(2)}) async-start(f32[2,32,8,512]{3,2,0,1:T(8,128)} %copy.183), calls=%async_computation.7 | async-start | bytes 2097152 | tf_op jit(solution)/shard_map/all_to_all | solution.py:128
  354.3 182.5 %reduce-scatter.2.cloned.1.call-start = ((), (), s32[]{:S(2)}) async-start(), calls=%async_computation.9 | async-start | bytes 5406720 | tf_op jit(solution)/shard_map/reduce_scatter | solution.py:200
  369.4 4.3 collective-permute-start
  379.0 1.5 copy-start.17
  379.0 1.5 copy-start.20
  379.0 1.5 copy-start.21
  379.0 1.6 copy-start.12
  379.0 2.4 copy-start.9
  379.0 2.4 copy-start.11
  379.1 2.6 copy-start.19
  379.1 89.5 %copy-start.14 = (f32[256,64]{0,1:T(8,128)S(1)}, f32[256,64]{0,1:T(8,128)}, u32[]{:S(2)}) copy-start(f32[256,64]{0,1:T(8,128)} %copy-done.13) | copy-start | bytes 196612
  379.1 329.6 %all-reduce.6.cloned.1.call-start = ((), (), s32[]{:S(2)}) async-start(), calls=%async_computation.11 | async-start | bytes 262144 | tf_op jit(solution)/shard_map/psum | solution.py:188
  469.8 310.2 %all-reduce.4.cloned.1.call-start = ((), (), s32[]{:S(2)}) async-start(), calls=%async_computation.10 | async-start | bytes 327680 | tf_op jit(solution)/shard_map/psum | solution.py:201
Sparse Core Ops, SparseCore 0:
  379.2 157.5 reduce-scatter.1
Sparse Core Ops, SparseCore 1:
  469.9 238.7 all-reduce.5
  711.2 68.8 all-reduce.3
where the time goes:
time: 798 us; the launch traced here: 790 us
  waiting for transfers between devices  348 us (44%)
  blocking collectives  228 us (29%)
  matrix products  90.4 us (11%)
  local copies, waits for them, and re-layouts  52.8 us (7%)
  starting transfers between devices  35.4 us (4%)
  other arithmetic  17.9 us (2%)
  between operations  16.7 us (2%)
    psum x1, waiting for transfers between devices, on_device(): lax.psum((local_pos, local_filt, local_rates, local_skip), ('tm', 'batch'))  172 us
    psum x1, blocking collectives, on_device(): lax.psum((local_pos, local_filt, local_rates, local_skip), ('tm', 'batch'))  86.2 us
    all_to_all x2, blocking collectives, to_spectrum(): lax.all_to_all(jnp.stack([twisted_real, twisted_imag]), 'tm', split_axis=...  78.3 us
    psum x1, waiting for transfers between devices, on_device(): conv_total = lax.psum(conv_part, 'batch')  69.8 us
    reduce_scatter x1, waiting for transfers between devices, on_device(): lax.psum_scatter(jnp.stack(pieces, axis=1), 'tm', scatter_dimension=0, ti...  60.2 us
    all_to_all x1, blocking collectives, from_spectrum(): lax.all_to_all(jnp.stack([mixed_real, mixed_imag]), 'tm', split_axis=3, c...  49 us
    all_to_all x1, waiting for transfers between devices, from_spectrum(): lax.all_to_all(jnp.stack([mixed_real, mixed_imag]), 'tm', split_axis=3, c...  22.3 us
    all_to_all x2, starting transfers between devices, from_spectrum(): lax.all_to_all(values, 'tm', split_axis=1, concat_axis=2, tiled=True)  16.6 us
  transfers between devices with their start and end apart: 9, of which 7 were waited for; matrix products, arithmetic and copies ran while one was open for 4% of the time, Pallas kernels for 0%

commit v1 on v0

v1 whole, which is shorter than its diff:
```python
import math

import jax
import jax.numpy as jnp
import ml_dtypes
import numpy as np
from jax import lax
from jax.experimental import pallas as pl
from jax.experimental.pallas import tpu as pltpu
from jax.sharding import PartitionSpec as P

F32 = jnp.float32
BF16 = jnp.bfloat16

SHARDS = 32
ROWS = 256
LENGTH = SHARDS * ROWS
WIDTH = 512
KERNEL = 5
FEAT = 64
OWN = WIDTH // SHARDS
LANES = 128
STEPS = LENGTH // LANES
STACK = STEPS * OWN
HALO = LANES
SPAN = ROWS + HALO
HALF = WIDTH // 2
CONV = KERNEL * HALF
BLOCK = 1024


def split_table(values):
    high = values.astype(ml_dtypes.bfloat16)
    low = (values - high.astype(np.float64)).astype(ml_dtypes.bfloat16)
    return high, low


def feature_tables():
    half = FEAT // 2
    factor = np.array([1 + i * i * LENGTH // (2 * half * half) for i in range(half)], dtype=np.int64)
    steps = np.arange(LENGTH, dtype=np.int64)
    angles = 2.0 * np.pi * ((factor[:, None] * steps[None, :]) % LENGTH) / LENGTH
    return split_table(np.concatenate([np.sin(angles), np.cos(angles)], axis=0))


def transform_tables():
    order = np.array([2 * p + h for h in range(2) for p in range(STEPS // 2)])
    k1 = np.arange(STEPS)
    alpha = np.pi * order[None, :] / STEPS / 2 - 2.0 * np.pi * ((order[None, :] * k1[:, None]) % STEPS) / STEPS
    outer = np.concatenate([np.cos(alpha), np.sin(alpha)], axis=0)
    outer_high, outer_low = split_table(outer)
    first = np.concatenate([outer_high, outer_low], axis=1)
    back_high, back_low = split_table(outer.T / LENGTH)
    last = np.concatenate([back_high, back_low, back_high], axis=1)
    b = np.arange(LANES)
    beta = np.pi * b[None, :] / (2 * LENGTH) - 2.0 * np.pi * ((b[None, :] * k1[:, None]) % LENGTH) / LENGTH
    twist_cos = np.cos(beta).astype(np.float32)
    twist_sin = np.sin(beta).astype(np.float32)
    gamma = 2.0 * np.pi * ((b[:, None] * b[None, :]) % LANES) / LANES
    cos, sin = np.cos(gamma), np.sin(gamma)
    ahead = split_table(np.block([[cos, -sin], [sin, cos]]))
    behind = split_table(np.block([[cos, sin], [-sin, cos]]))
    return (first, last, twist_cos, twist_sin, *ahead, *behind)


def split(values):
    high = values.astype(BF16)
    return high, (values - high.astype(F32)).astype(BF16)


def mul(left, right, dims=((1,), (0,))):
    return lax.dot_general(left, right, (dims, ((), ())), preferred_element_type=F32)


def mul3(left, right, dims=((1,), (0,))):
    lh, ll = left
    rh, rl = right
    return mul(lh, rh, dims) + mul(ll, rh, dims) + mul(lh, rl, dims)


def spectrum(stack_ref, high_ref, low_ref, tabs):
    first, _, tc_ref, ts_ref, ahead_high, ahead_low, _, _ = tabs
    tc, ts = tc_ref[...], ts_ref[...]
    for c in range(0, OWN, 2):
        pair = [stack_ref[pl.ds(c + k, STEPS, stride=OWN), :] for k in range(2)]
        wide = jnp.concatenate(pair, axis=1).astype(BF16)
        u = mul(first[...], jnp.concatenate([wide, wide], axis=0))
        for k in range(2):
            ur = u[:STEPS, k * LANES : (k + 1) * LANES]
            ui = u[STEPS:, k * LANES : (k + 1) * LANES]
            v = jnp.concatenate([ur * tc - ui * ts, ur * ts + ui * tc], axis=1)
            high, low = split(v)
            high_ref[(c + k) * STEPS : (c + k + 1) * STEPS, :] = high
            low_ref[(c + k) * STEPS : (c + k + 1) * STEPS, :] = low
    return mul3((high_ref[...], low_ref[...]), (ahead_high[...], ahead_low[...]))


def from_spectrum(values, stack_ref, tabs):
    _, last, tc_ref, ts_ref, _, _, behind_high, behind_low = tabs
    tc, ts = tc_ref[...], ts_ref[...]
    q = mul3(split(values), (behind_high[...], behind_low[...]))
    for c in range(0, OWN, 2):
        pair = []
        for k in range(2):
            rows = q[(c + k) * STEPS : (c + k + 1) * STEPS]
            qr, qi = rows[:, :LANES], rows[:, LANES:]
            pair.append(jnp.concatenate([qr * tc + qi * ts, qi * tc - qr * ts], axis=0))
        high, low = split(jnp.concatenate(pair, axis=1))
        y = mul(last[...], jnp.concatenate([high, high, low], axis=0))
        for k in range(2):
            stack_ref[pl.ds(c + k, STEPS, stride=OWN), :] = y[:, k * LANES : (k + 1) * LANES]


def product(left, right, conjugate):
    lr, li = left[:, :LANES], left[:, LANES:]
    rr, ri = right[:, :LANES], right[:, LANES:]
    if conjugate:
        return jnp.concatenate([lr * rr + li * ri, lr * ri - li * rr], axis=1)
    return jnp.concatenate([lr * rr - li * ri, lr * ri + li * rr], axis=1)


def sin_cos(x):
    turns = jnp.floor(x * (2.0 / math.pi) + 0.5)
    r = x - turns * 1.5703125
    r = r - turns * 4.837512969970703125e-4
    r = r - turns * 7.549789948768648e-8
    z = r * r
    s = r + r * z * (-1.6666654611e-1 + z * (8.3321608736e-3 - z * 1.9515295891e-4))
    c = 1.0 - 0.5 * z + z * z * (4.166664568298827e-2 + z * (-1.388731625493765e-3 + z * 2.443315711809948e-5))
    quad = turns.astype(jnp.int32)
    odd = (quad & 1) == 1
    sin = jnp.where(odd, c, s)
    cos = jnp.where(odd, s, c)
    sin = jnp.where((quad & 2) == 2, -sin, sin)
    cos = jnp.where(((quad + 1) & 2) == 2, -cos, cos)
    return sin, cos


def envelope(rates, start, size):
    steps = (start + lax.broadcasted_iota(jnp.int32, (OWN, size), 1)).astype(F32)
    return jnp.sqrt(rates) * jnp.exp(-steps * rates), steps


def prep_kernel(x_ref, cot_ref, w_ref, out_ref, pad_ref, shift_ref):
    out_ref[:, :ROWS] = jnp.transpose(x_ref[...].astype(F32)).astype(BF16)
    pad_ref[:HALO, :] = jnp.zeros((HALO, WIDTH), F32)
    pad_ref[HALO + ROWS :, :] = jnp.zeros((8, WIDTH), F32)
    pad_ref[HALO : HALO + ROWS, :] = cot_ref[...].astype(F32)
    for i in range(KERNEL):
        shift_ref[i] = pad_ref[i : i + SPAN, :].astype(BF16)
    for c in range(0, WIDTH, 128):
        total = jnp.zeros((128, SPAN), F32)
        for i in range(KERNEL):
            total = total + mul(w_ref[i, c : c + 128, :], shift_ref[i], ((1,), (1,)))
        out_ref[c : c + 128, ROWS:] = total.astype(BF16)


def taps_kernel(
    wp_ref, wf_ref, lr_ref, fh_ref, fl_ref, *rest
):
    tabs = rest[:8]
    hh_ref, hl_ref, cos_ref, taps_ref, spec_ref, stack_ref, vh_ref, vl_ref = rest[8:]
    wp = split(wp_ref[...])
    wf = split(wf_ref[...])
    rates = jnp.exp(lr_ref[...])
    for start in range(0, LENGTH, BLOCK):
        cut = slice(start, start + BLOCK)
        sin, cos = sin_cos(mul3(wp, (fh_ref[:, cut], fl_ref[:, cut])))
        high, low = split(sin)
        hh_ref[:, cut] = high
        hl_ref[:, cut] = low
        cos_ref[:, cut] = cos
        decay, _ = envelope(rates, start, BLOCK)
        taps = mul3(wf, (high, low)) * decay
        taps_ref[:, cut] = taps
        rounded = taps.astype(BF16).astype(F32)
        for j in range(BLOCK // LANES):
            a = start // LANES + j
            row = ((a % 2) * SHARDS + a // 2) * OWN
            stack_ref[row : row + OWN, :] = rounded[:, j * LANES : (j + 1) * LANES]
    spec_ref[...] = spectrum(stack_ref, vh_ref, vl_ref, tabs)


def forward_kernel(recv_ref, tspec_ref, gain_ref, *rest):
    tabs = rest[:8]
    act_ref, gb_ref, xspec_ref, skip_ref, x_ref, y_ref, vh_ref, vl_ref = rest[8:]
    for h in range(2):
        part = recv_ref[:, :, h * LANES : (h + 1) * LANES].astype(F32)
        x_ref[h * STACK // 2 : (h + 1) * STACK // 2, :] = part.reshape(STACK // 2, LANES)
    spec = spectrum(x_ref, vh_ref, vl_ref, tabs)
    xspec_ref[...] = spec
    from_spectrum(product(tspec_ref[...], spec, False), y_ref, tabs)
    gain = gain_ref[...][None]
    x = x_ref[...].reshape(STEPS, OWN, LANES)
    before = y_ref[...].reshape(STEPS, OWN, LANES) + gain * x
    root = math.sqrt(2.0 / math.pi)
    square = before * before
    th = jnp.tanh(root * (before + 0.044715 * square * before))
    half_cdf = 0.5 * (1.0 + th)
    active = (before * half_cdf).astype(BF16)
    slope = half_cdf + 0.5 * before * (1.0 - th * th) * (root * (1.0 + 3.0 * 0.044715 * square))
    early = recv_ref[:, :, ROWS + HALO : ROWS + HALO + LANES].astype(F32)
    late = recv_ref[:, :, ROWS + HALO + LANES : ROWS + HALO + 2 * LANES].astype(F32)
    edge = recv_ref[:, :, ROWS : ROWS + HALO].astype(F32)
    edge = jnp.concatenate([edge[1:], jnp.zeros((1, OWN, LANES), F32)], axis=0)
    grad_active = jnp.concatenate([early, late + edge], axis=0)
    grad_before = (grad_active * slope).astype(BF16).astype(F32)
    gb_ref[...] = grad_before.reshape(STACK, LANES)
    skip_ref[...] = jnp.sum(grad_before * x, axis=0)
    first, second = active[:SHARDS], active[SHARDS:]
    act_ref[:, :, HALO : HALO + LANES] = first
    act_ref[:, :, HALO + LANES :] = second
    act_ref[:, :, :HALO] = jnp.concatenate([jnp.zeros((1, OWN, LANES), BF16), second[:-1]], axis=0)


def backward_kernel(
    gb_ref, xspec_ref, tspec_ref, gain_ref, skip_ref, hh_ref, hl_ref, cos_ref, fh_ref, fl_ref, taps_ref, wf_ref, lr_ref, *rest
):
    tabs = rest[:8]
    ig_ref, small_ref, y_ref, vh_ref, vl_ref, g_ref = rest[8:]
    spec = spectrum(gb_ref, vh_ref, vl_ref, tabs)
    from_spectrum(product(tspec_ref[...], spec, True), y_ref, tabs)
    gain = gain_ref[...][None]
    grad = gb_ref[...].reshape(STEPS, OWN, LANES)
    result = (y_ref[...].reshape(STEPS, OWN, LANES) + gain * grad).astype(BF16)
    ig_ref[:, :, :LANES] = result[:SHARDS]
    ig_ref[:, :, LANES:] = result[SHARDS:]
    from_spectrum(product(xspec_ref[...], spec, True), y_ref, tabs)
    for a in range(STEPS):
        row = ((a % 2) * SHARDS + a // 2) * OWN
        g_ref[:, a * LANES : (a + 1) * LANES] = y_ref[row : row + OWN, :]
    wf = split(wf_ref[...])
    rates = jnp.exp(lr_ref[...])
    filt = jnp.zeros((OWN, FEAT), F32)
    pos = jnp.zeros((FEAT, FEAT), F32)
    rate = jnp.zeros((OWN, 1), F32)
    for start in range(0, LENGTH, BLOCK):
        cut = slice(start, start + BLOCK)
        grad_taps = g_ref[:, cut]
        decay, steps = envelope(rates, start, BLOCK)
        shaped = split(grad_taps * decay)
        rate = rate + jnp.sum(grad_taps * taps_ref[:, cut] * (0.5 - rates * steps), axis=1, keepdims=True)
        filt = filt + mul3(shaped, (hh_ref[:, cut], hl_ref[:, cut]), ((1,), (1,)))
        inner = split(mul3(wf, shaped, ((0,), (0,))) * cos_ref[:, cut])
        pos = pos + mul3((fh_ref[:, cut], fl_ref[:, cut]), inner, ((1,), (1,)))
    small_ref[...] = jnp.zeros((48, LANES), F32)
    small_ref[:32, :FEAT] = pos[:32]
    small_ref[:32, FEAT:] = pos[32:]
    small_ref[32:, :FEAT] = filt
    small_ref[32:, 64:65] = rate
    small_ref[32:, 65:66] = jnp.sum(skip_ref[...], axis=1, keepdims=True)


def conv_kernel(act_ref, peer_act_ref, cot_ref, peer_cot_ref, ig_ref, small_ref, out_ref, pad_ref):
    pad_ref[:, :HALO, :] = jnp.zeros((2, HALO, HALF), F32)
    pad_ref[:, HALO + ROWS :, :] = jnp.zeros((2, 8, HALF), F32)
    pad_ref[0, HALO : HALO + ROWS, :] = cot_ref[...].astype(F32)
    pad_ref[1, HALO : HALO + ROWS, :] = peer_cot_ref[...].astype(F32)
    for i in range(KERNEL):
        own = pad_ref[0, i : i + SPAN, :].astype(BF16)
        peer = pad_ref[1, i : i + SPAN, :].astype(BF16)
        part = mul(act_ref[...], own) + mul(peer_act_ref[...], peer)
        out_ref[:, i * HALF : (i + 1) * HALF] = part.astype(BF16)
    out_ref[:, CONV : CONV + ROWS] = ig_ref[...]
    small = small_ref[...]
    pos = jnp.concatenate(split(small[:16]), axis=1)
    filt = jnp.concatenate([v.astype(F32) for v in split(small[16:])], axis=0).astype(BF16)
    tile = jnp.concatenate([pos, filt], axis=1)
    for p in range(SHARDS):
        out_ref[p * OWN : (p + 1) * OWN, CONV + ROWS :] = tile


def mixed_kernel(act_ref, w_ref, out_ref, part_ref):
    act = jnp.transpose(act_ref[...].astype(F32)).astype(BF16)[HALO - 16 :]
    total = jnp.zeros((ROWS, WIDTH), F32)
    for i in range(KERNEL):
        part_ref[...] = mul(act, w_ref[i])
        total = total + part_ref[16 - i : 16 - i + ROWS, :]
    out_ref[...] = total.astype(BF16)


def gather_kernel(recv_ref, ig_ref, out_ref):
    conv = jnp.sum(recv_ref[:, :, :CONV].astype(F32), axis=0)
    out_ref[:, :CONV] = conv.astype(BF16)
    ig = recv_ref[:, :, CONV : CONV + ROWS].astype(F32).reshape(WIDTH, ROWS)
    ig_ref[...] = jnp.transpose(ig).astype(BF16)
    base = CONV + ROWS
    pos = jnp.sum(
        recv_ref[:, :, base : base + LANES].astype(F32) + recv_ref[:, :, base + LANES : base + 2 * LANES].astype(F32), axis=0
    )
    pos_high, pos_low = split(pos)
    out_ref[:, CONV : CONV + LANES] = pos_high
    out_ref[:, CONV + LANES : CONV + 2 * LANES] = pos_low
    both = recv_ref[:, :, base + 2 * LANES : base + 3 * LANES].astype(F32)
    filt = both[:, :8] + both[:, 8:]
    for j in range(16):
        block = filt[2 * j : 2 * j + 2].reshape(16, LANES)
        out_ref[:, CONV + (2 + j) * LANES : CONV + (3 + j) * LANES] = block.astype(BF16)


def final_kernel(recv_ref, conv_ref, rest_ref):
    scale = 1.0 / math.sqrt(8 * LENGTH)
    total = jnp.sum(recv_ref[...].astype(F32), axis=0) * scale
    conv_ref[...] = total[:, :CONV]
    rest_ref[:16, :] = total[:, CONV : CONV + LANES] + total[:, CONV + LANES : CONV + 2 * LANES]
    for j in range(16):
        rest_ref[16 + 16 * j : 32 + 16 * j, :] = total[:, CONV + (2 + j) * LANES : CONV + (3 + j) * LANES]


def call(kernel, out_shape, args, scratch=(), flops=0, name=None):
    vmem = pl.BlockSpec(memory_space=pltpu.VMEM)
    single = not isinstance(out_shape, (list, tuple))
    outs = [out_shape] if single else out_shape
    moved = sum(math.prod(a.shape) * a.dtype.itemsize for a in (*args, *outs))
    return pl.pallas_call(
        kernel,
        out_shape=out_shape,
        in_specs=[vmem] * len(args),
        out_specs=vmem if single else [vmem] * len(outs),
        scratch_shapes=list(scratch),
        compiler_params=pltpu.CompilerParams(vmem_limit_bytes=48 * 1024 * 1024),
        cost_estimate=pl.CostEstimate(flops=flops, bytes_accessed=moved, transcendentals=0),
        name=name,
    )(*args)


def shape(dims, kind=F32):
    return jax.ShapeDtypeStruct(dims, kind)


def on_device(inputs, cotangent, w_pos, w_filt, log_rates, skip_gain, w_conv):
    rank = lax.axis_index("tm")
    core = lax.axis_index("batch") % 2
    swap = [(i, i ^ 1) for i in range(lax.axis_size("batch"))]
    signal, upstream = inputs[0], cotangent[0]
    w_taps = jnp.transpose(w_conv, (1, 0, 2))
    tabs = tuple(jnp.asarray(t) for t in transform_tables())
    feat = tuple(jnp.asarray(t) for t in feature_tables())

    def exchange(low, high):
        mine = jnp.where(core == 0, low, high)
        theirs = jnp.where(core == 0, high, low)
        return mine, lax.ppermute(theirs, "batch", swap)

    message = call(
        prep_kernel,
        shape((WIDTH, ROWS + SPAN), BF16),
        (signal, upstream, w_taps),
        [pltpu.VMEM((HALO + ROWS + 8, WIDTH), F32), pltpu.VMEM((KERNEL, SPAN, WIDTH), BF16)],
        flops=2 * KERNEL * WIDTH * WIDTH * SPAN,
        name="prep",
    )
    received = lax.all_to_all(
        message.reshape(SHARDS, OWN, ROWS + SPAN), "tm", split_axis=0, concat_axis=0, tiled=True
    )
    cot_mine, cot_peer = exchange(upstream[:, :HALF], upstream[:, HALF:])

    own = rank * OWN
    wf_own = lax.dynamic_slice(w_filt, (0, own), (FEAT, OWN)).T
    lr_own = lax.dynamic_slice(log_rates, (own,), (OWN,))[:, None]
    gain_own = lax.dynamic_slice(skip_gain, (own,), (OWN,))[:, None]
    stack = pltpu.VMEM((STACK, LANES), F32)
    wide = pltpu.VMEM((STACK, 2 * LANES), BF16)
    flops = 2 * 3 * (2 * STACK * LANES * LANES + STACK * 4 * LANES * LANES)
    hid_high, hid_low, cosines, taps, tap_spec = call(
        taps_kernel,
        [
            shape((FEAT, LENGTH), BF16),
            shape((FEAT, LENGTH), BF16),
            shape((FEAT, LENGTH)),
            shape((OWN, LENGTH)),
            shape((STACK, 2 * LANES)),
        ],
        (w_pos.T, wf_own, lr_own, *feat, *tabs),
        [stack, wide, wide],
        flops=flops * 2,
        name="taps",
    )
    act_message, grad_before, sig_spec, skip_part = call(
        forward_kernel,
        [
            shape((SHARDS, OWN, SPAN), BF16),
            shape((STACK, LANES)),
            shape((STACK, 2 * LANES)),
            shape((OWN, LANES)),
        ],
        (received, tap_spec, gain_own, *tabs),
        [stack, stack, wide, wide],
        flops=flops * 2,
        name="forward",
    )
    act = lax.all_to_all(act_message, "tm", split_axis=0, concat_axis=0, tiled=True).reshape(WIDTH, SPAN)
    ig_message, small = call(
        backward_kernel,
        [shape((SHARDS, OWN, ROWS), BF16), shape((48, LANES))],
        (
            grad_before,
            sig_spec,
            tap_spec,
            gain_own,
            skip_part,
            hid_high,
            hid_low,
            cosines,
            *feat,
            taps,
            wf_own,
            lr_own,
            *tabs,
        ),
        [stack, wide, wide, pltpu.VMEM((OWN, LENGTH), F32)],
        flops=flops * 4,
        name="backward",
    )
    mine, theirs = exchange(
        jnp.concatenate([small[:16], small[32:40]], axis=0), jnp.concatenate([small[16:32], small[40:]], axis=0)
    )
    small_half = mine + theirs
    act_peer = lax.ppermute(act, "batch", swap)
    lanes = CONV + ROWS + 3 * LANES
    sums = call(
        conv_kernel,
        shape((WIDTH, lanes), BF16),
        (act, act_peer, cot_mine, cot_peer, ig_message.reshape(WIDTH, ROWS), small_half),
        [pltpu.VMEM((2, HALO + ROWS + 8, HALF), F32)],
        flops=2 * KERNEL * WIDTH * HALF * 2 * SPAN,
        name="conv_grad",
    )
    sums = lax.all_to_all(sums.reshape(SHARDS, OWN, lanes), "tm", split_axis=0, concat_axis=0, tiled=True)
    mixed = call(
        mixed_kernel,
        shape((ROWS, WIDTH), BF16),
        (act, w_taps),
        [pltpu.VMEM((ROWS + 16, WIDTH), F32)],
        flops=2 * KERNEL * WIDTH * WIDTH * (ROWS + 16),
        name="mixed",
    )
    payload_lanes = CONV + 18 * LANES
    input_grad, payload = call(
        gather_kernel,
        [shape((ROWS, WIDTH), BF16), shape((OWN, payload_lanes), BF16)],
        (sums,),
        name="gather",
    )
    groups = [[2 * z + e for z in range(4)] for e in range(2)]
    spread = lax.all_to_all(
        jnp.broadcast_to(payload[None], (4, OWN, payload_lanes)),
        "batch",
        split_axis=0,
        concat_axis=0,
        tiled=True,
        axis_index_groups=groups,
    )
    conv_half, rest = call(final_kernel, [shape((OWN, CONV)), shape((16 + HALF, LANES))], (spread,), name="final")
    conv_other = lax.ppermute(conv_half, "batch", swap)
    rest_other = lax.ppermute(rest, "batch", swap)

    def ordered(mine, other):
        return jnp.where(core == 0, mine, other), jnp.where(core == 0, other, mine)

    conv_low, conv_high = ordered(conv_half, conv_other)
    conv_grad = jnp.concatenate([v.reshape(OWN, KERNEL, HALF) for v in (conv_low, conv_high)], axis=2)
    rest_low, rest_high = ordered(rest, rest_other)
    pos_grad = jnp.concatenate([rest_low[:16, :FEAT], rest_high[:16, :FEAT], rest_low[:16, FEAT:], rest_high[:16, FEAT:]], axis=0)
    filt = jnp.concatenate([v[16:].reshape(SHARDS, 8, LANES) for v in (rest_low, rest_high)], axis=1).reshape(WIDTH, LANES)
    return (
        mixed[None],
        input_grad[None],
        conv_grad,
        pos_grad,
        filt[:, :FEAT].T,
        filt[:, 64],
        filt[:, 65],
    )


def solution(mesh):
    in_specs = (P("batch", "tm", None), P("batch", "tm", None), P(), P(), P(), P(), P())
    out_specs = (P("batch", "tm", None), P("batch", "tm", None), P("tm", None, None), P(), P(), P(), P())
    return jax.shard_map(on_device, mesh=mesh, in_specs=in_specs, out_specs=out_specs, check_vma=False)
```

time: 798 us -> 136 us (0.17)
  waiting for transfers between devices: 348 us -> 1.74 us
  blocking collectives: 228 us -> 52.3 us
  matrix products: 90.4 us -> 0 us
  Pallas kernels: 0 us -> 27.8 us
  local copies, waits for them, and re-layouts: 52.8 us -> 27.3 us
  other arithmetic: 17.9 us -> 0.74 us
  between operations: 16.7 us -> 0.94 us
  starting transfers between devices: 35.4 us -> 23.9 us
    psum x2 -> x0, waiting for transfers between devices: 242 us -> none  [the longest x1 172 us: on_device(): lax.psum((local_pos, local_filt, local_rates, local_skip), ('tm', 'batch'))]
    dot_general x44 -> x0, matrix products: 90.4 us -> none  [the longest x5 10.2 us: on_device(): jnp.einsum('td,cd->tc', reaching[offset:offset + num_rows], w_conv[:, off...]
    all_to_all x4 -> x2, blocking collectives: 142 us -> 52.3 us  [the longest x1 33.3 us: on_device(): lax.all_to_all(sums.reshape(SHARDS, OWN, lanes), 'tm', split_axis=0, conc...]
    psum x1 -> x0, blocking collectives: 86.2 us -> none  [on_device(): lax.psum((local_pos, local_filt, local_rates, local_skip), ('tm', 'batch'))]
    reduce_scatter x1 -> x0, waiting for transfers between devices: 60.2 us -> none  [on_device(): lax.psum_scatter(jnp.stack(pieces, axis=1), 'tm', scatter_dimension=0, ti...]
    all_to_all x4 -> x2, waiting for transfers between devices: 46.1 us -> 0.01 us  [the longest x1 0.01 us: on_device(): lax.all_to_all(act_message, 'tm', split_axis=0, concat_axis=0, tiled=True)]
    pallas_call x0 -> x8, Pallas kernels: none -> 27.8 us  [call(): pl.pallas_call(kernel, out_shape=out_shape, in_specs=[vmem] * len(args),...]
    unnamed x48 -> x82, local copies, waits for them, and re-layouts: 8.02 us -> 25 us
  transfers between devices with their start and end apart: 9 -> 7, of which waited for: 7 -> 3; matrix products, arithmetic and copies ran while one was open for 4% -> 2% of each run, Pallas kernels for 0% -> 14%
where the time goes in v1:
time: 136 us; the launch traced here: 135 us
  blocking collectives  52.3 us (38%)
  Pallas kernels  27.8 us (20%)
  local copies, waits for them, and re-layouts  27.3 us (20%)
  starting transfers between devices  23.9 us (18%)
  waiting for transfers between devices  1.74 us (1%)
    all_to_all x1, blocking collectives, on_device(): lax.all_to_all(sums.reshape(SHARDS, OWN, lanes), 'tm', split_axis=0, conc...  33.3 us
    pallas_call x8, Pallas kernels, call(): pl.pallas_call(kernel, out_shape=out_shape, in_specs=[vmem] * len(args),...  27.8 us
    unnamed x82, local copies, waits for them, and re-layouts  25 us
    all_to_all x1, blocking collectives, on_device(): lax.all_to_all(jnp.broadcast_to(payload[None], (4, OWN, payload_lanes)),...  19 us
    all_to_all x1, starting transfers between devices, on_device(): lax.all_to_all(message.reshape(SHARDS, OWN, ROWS + SPAN), 'tm', split_axi...  9.21 us
    all_to_all x1, starting transfers between devices, on_device(): lax.all_to_all(act_message, 'tm', split_axis=0, concat_axis=0, tiled=True)  7.92 us
    ppermute x1, starting transfers between devices, on_device(): conv_other = lax.ppermute(conv_half, 'batch', swap)  4.56 us
  transfers between devices with their start and end apart: 7, of which 3 were waited for; matrix products, arithmetic and copies ran while one was open for 2% of the time, Pallas kernels for 14%

profile of v1, /device:TPU:1, one launch (start us, length us, event | category | flops | bytes accessed | tf_op | source)
XLA Modules:
  0.0 134.7 jit_solution(4195364568159330214)
XLA Ops:
  0.6 0.0 copy-start
  0.7 1.8 %copy-done.1 = bf16[512,5,512]{2,0,1:T(8,128)(2,1)S(1)} copy-done((bf16[512,5,512]{2,0,1:T(8,128)(2,1)S(1)}, bf16[512,5,512]{2,0,1:T(8,128)(2,1)}, u32[]{:S(2)}) %copy-start.1) | copy-done | bytes 2621464
  2.4 0.9 copy-done.10
  3.4 0.9 copy-done.17
  4.3 0.0 copy-start.20
  4.4 0.0 copy-start.22
  4.4 0.0 copy-start.24
  4.4 0.0 copy-start.26
  4.4 0.0 copy-start.28
  4.4 3.3 %prep.1 = bf16[512,640]{1,0:T(8,128)(2,1)} custom-call(bf16[256,512]{1,0:T(8,128)(2,1)S(1)} %bitcast.30, bf16[256,512]{1,0:T(8,128)(2,1)S(1)} %bitcast.28, bf16[5,512,512]{2,1,0:T(8,128)(2,1)S(1)} %bitcast.22), custom_call_target="tpu_custom_call" | custom-call | flops 1006632960 | bytes 3801088 | tf_op jit(solution)/shard_map/prep/pallas_call | solution.py:315
  7.7 9.2 %all-to-all-start = ((bf16[32,16,640]{2,1,0:T(8,128)(2,1)}), bf16[32,16,640]{2,1,0:T(8,128)(2,1)S(1)}, u32[]{:S(2)}, u32[]{:S(2)}) async-start(bf16[32,16,640]{2,1,0:T(8,128)(2,1)} %bitcast.3), calls=%async_computation | async-start | bytes 1310720 | tf_op jit(solution)/shard_map/all_to_all | solution.py:353
  17.0 0.8 dynamic-slice_bitcast_fusion
  17.7 0.1 copy.43.lr_ref
  17.8 0.1 constant_dynamic-slice_fusion
  17.9 0.1 copy.49
  18.0 0.7 copy.41
  18.7 0.1 copy.44.gain_ref
  18.8 0.0 copy-start.30
  18.9 0.7 copy-done.30
  19.6 0.8 copy-done.35
  20.4 7.2 %taps.1 = (bf16[64,8192]{1,0:T(8,128)(2,1)S(1)}, bf16[64,8192]{1,0:T(8,128)(2,1)S(1)}, f32[64,8192]{1,0:T(8,128)}, f32[16,8192]{1,0:T(8,128)S(1)}, f32[1024,256]{1,0:T(8,128)S(1)}) custom-call(f32[64,64]{1,0:T(8,128)S(1)} %bitcast.33, f32[16,64]{1,0:T(8,128)S(1)} %bitcast.31, f32[16,1]{1,0:T(8,128)S(1)} %copy.43.lr_ref, bf16[64,8192]{1,0:T(8,128)(2,1)S(1)} %copy-done.3, ...), custom_call_target="tpu_custom_call" | custom-call | flops 1207959552 | bytes 8556608 | tf_op jit(solution)/shard_map/taps/pallas_call | solution.py:315
  27.6 1.0 copy-done.4
  28.6 1.0 copy-done.5
  29.6 0.8 copy-done.12
  30.4 1.2 copy-done.6
  31.6 0.8 copy-done.31
  32.4 2.6 %forward.1 = (bf16[32,16,384]{2,1,0:T(8,128)(2,1)S(1)}, f32[1024,128]{1,0:T(8,128)S(1)}, f32[1024,256]{1,0:T(8,128)S(1)}, f32[16,128]{1,0:T(8,128)S(1)}) custom-call(bf16[32,16,640]{2,1,0:T(8,128)(2,1)S(1)} %all-to-all-done.recv_ref, f32[1024,256]{1,0:T(8,128)S(1)} %copy-done.6, f32[16,1]{1,0:T(8,128)S(1)} %copy.44.gain_ref, ...), custom_call_target="tpu_custom_call" | custom-call | flops 1207959552 | bytes 4350016 | tf_op jit(solution)/shard_map/forward/pallas_call | solution.py:315
  34.9 1.0 copy-done.8
  35.9 0.8 copy-done.14
  36.7 0.7 copy-done.16
  37.5 0.6 copy-done.36
  38.1 7.9 %all-to-all-start.1 = ((bf16[32,16,384]{2,1,0:T(8,128)(2,1)}), bf16[32,16,384]{2,1,0:T(8,128)(2,1)S(1)}, u32[]{:S(2)}, u32[]{:S(2)}) async-start(bf16[32,16,384]{2,1,0:T(8,128)(2,1)} %copy-done.16), calls=%async_computation.1 | async-start | bytes 786432 | tf_op jit(solution)/shard_map/all_to_all | solution.py:392
  46.0 1.2 copy-done.9
  47.2 1.0 copy-done.13
  48.3 1.0 copy-done.15
  49.3 0.9 copy-done.21
  50.2 0.9 copy-done.23
  51.1 0.8 copy-done.25
  51.9 0.8 copy-done.27
  52.7 0.8 copy-done.29
  53.5 0.8 copy-done.32
  54.2 0.7 copy-done.34
  54.9 0.7 copy-done.37
  55.6 10.4 %backward.1 = (bf16[32,16,256]{2,1,0:T(8,128)(2,1)S(1)}, f32[48,128]{1,0:T(8,128)S(1)}) custom-call(f32[1024,128]{1,0:T(8,128)S(1)} %copy-done.15, f32[1024,256]{1,0:T(8,128)S(1)} %copy-done.9, f32[1024,256]{1,0:T(8,128)S(1)} %copy-done.7, f32[16,1]{1,0:T(8,128)S(1)} %copy-done.34, f32[16,128]{1,0:T(8,128)S(1)} %copy-done.37, ...), custom_call_target="tpu_custom_call" | custom-call | flops 2415919104 | bytes 10408064 | tf_op jit(solution)/shard_map/backward/pallas_call | solution.py:315
  66.1 1.6 %collective-permute-start.2 = (f32[24,128]{1,0:T(8,128)S(1)}, f32[24,128]{1,0:T(8,128)S(1)}, u32[]{:S(2)}, u32[]{:S(2)}) collective-permute-start(f32[24,128]{1,0:T(8,128)S(1)} %fusion), channel_id=1, source_target_pairs={{0,1},{1,0},{2,3},{3,2},{4,5},{5,4},{6,7},{7,6},{8,9},{9,8},{10,11... | collective-permute-start | bytes 36872 | tf_op jit(solution)/shard_map/ppermute | solution.py:343
  67.7 0.1 collective-permute-start
  67.9 0.5 collective-permute-start.1
  68.4 0.2 collective-permute-done.2
  68.6 1.1 collective-permute-done.1.peer_cot_ref
  69.6 1.5 %conv_grad.1 = bf16[512,1920]{1,0:T(8,128)(2,1)S(1)} custom-call(bf16[512,384]{1,0:T(8,128)(2,1)S(1)} %bitcast.26, bf16[512,384]{1,0:T(8,128)(2,1)S(1)} %collective-permute-done.peer_act_ref, bf16[256,256]{1,0:T(8,128)(2,1)S(1)} %get-tuple-element.56.cot_ref, bf16[256,256]{1,0:T(8,128)(2,1)S(1)} %collective-permute-done.1.peer_cot_ref, ...), custom_call_target="tpu_custom_call" | custom-call | flops 1006632960 | bytes 3289088 | tf_op jit(solution)/shard_map/conv_grad/pallas_call | solution.py:315
  71.2 33.3 %all_to_all.20.recv_ref = bf16[32,16,1920]{2,1,0:T(8,128)(2,1)S(1)} all-to-all(bf16[32,16,1920]{2,1,0:T(8,128)(2,1)S(1)} %bitcast.24), channel_id=1, replica_groups=mesh['tm'=32,'batch'=8] {'tm'}, dimensions={0} | all-to-all | bytes 3932160 | tf_op jit(solution)/shard_map/all_to_all | solution.py:429
  104.5 0.9 gather.1
  105.4 19.0 %all_to_all.21.recv_ref = bf16[4,16,3584]{2,1,0:T(8,128)(2,1)S(1)} all-to-all(bf16[4,16,3584]{2,1,0:T(8,128)(2,1)S(1)} %broadcast_in_dim.22), channel_id=1, replica_groups={{0,2,4,6},{1,3,5,7},{8,10,12,14},{9,11,13,15},{16,18,20,22},{17,19,21,2..., dimensions={0} | all-to-all | bytes 917504 | tf_op jit(solution)/shard_map/all_to_all | solution.py:446
  124.3 0.1 final.1
  124.4 4.6 %collective-permute-start.3 = (f32[16,1280]{1,0:T(8,128)S(1)}, f32[16,1280]{1,0:T(8,128)S(1)}, u32[]{:S(2)}, u32[]{:S(2)}) collective-permute-start(f32[16,1280]{1,0:T(8,128)S(1)} %get-tuple-element.35), channel_id=1, source_target_pairs={{0,1},{1,0},{2,3},{3,2},{4,5},{5,4},{6,7},{7,6},{8,9},{9,8},{10,11... | collective-permute-start | bytes 245768 | tf_op jit(solution)/shard_map/ppermute | solution.py:455
  129.0 1.8 %mixed.1 = bf16[256,512]{1,0:T(8,128)(2,1)} custom-call(bf16[512,384]{1,0:T(8,128)(2,1)S(1)} %bitcast.27, bf16[5,512,512]{2,1,0:T(8,128)(2,1)S(1)} %bitcast.23), custom_call_target="tpu_custom_call" | custom-call | flops 713031680 | bytes 3276800 | tf_op jit(solution)/shard_map/mixed/pallas_call | solution.py:315
  130.7 0.0 collective-permute-start.4
  130.9 0.8 copy.47
  131.6 0.5 collective-permute-done.4
  132.2 1.0 slice_reduce_fusion
  133.1 0.1 fusion.1
  133.2 0.1 fusion.2
  133.3 0.8 copy.48
  134.1 0.6 pad_maximum_fusion.2
  (65 shorter events, 0.4 us)
Async XLA Ops:
  0.6 17.2 %copy-start = (f32[64,512]{1,0:T(8,128)S(1)}, f32[64,512]{1,0:T(8,128)}, u32[]{:S(2)}) copy-start(f32[64,512]{1,0:T(8,128)} %param.20) | copy-start | bytes 393220
  0.6 1.8 %copy-start.1 = (bf16[512,5,512]{2,0,1:T(8,128)(2,1)S(1)}, bf16[512,5,512]{2,0,1:T(8,128)(2,1)}, u32[]{:S(2)}) copy-start(bf16[512,5,512]{2,0,1:T(8,128)(2,1)} %param.23) | copy-start | bytes 7864324
  2.4 0.9 copy-start.10
  3.4 0.9 copy-start.17
  4.3 13.7 %copy-start.38 = (f32[64,64]{1,0:T(8,128)S(1)}, f32[64,64]{1,0:T(8,128)}, u32[]{:S(2)}) copy-start(f32[64,64]{1,0:T(8,128)} %param.19) | copy-start | bytes 49156
  4.3 14.5 %copy-start.3 = (bf16[64,8192]{1,0:T(8,128)(2,1)S(1)}, bf16[64,8192]{1,0:T(8,128)(2,1)}, u32[]{:S(2)}) copy-start(bf16[64,8192]{1,0:T(8,128)(2,1)} %constant.55.clone.fh_ref) | copy-start | bytes 3145732
  4.3 14.5 %copy-start.18 = (bf16[256,256]{1,0:T(8,128)(2,1)S(1)}, bf16[256,256]{1,0:T(8,128)(2,1)}, u32[]{:S(2)}) copy-start(bf16[256,256]{1,0:T(8,128)(2,1)} %constant.51.clone.rest_4_) | copy-start | bytes 393220
  4.3 14.5 %copy-start.19 = (bf16[256,256]{1,0:T(8,128)(2,1)S(1)}, bf16[256,256]{1,0:T(8,128)(2,1)}, u32[]{:S(2)}) copy-start(bf16[256,256]{1,0:T(8,128)(2,1)} %constant.52.clone.rest_5_) | copy-start | bytes 393220
  4.3 14.5 %copy-start.20 = (bf16[256,256]{1,0:T(8,128)(2,1)S(1)}, bf16[256,256]{1,0:T(8,128)(2,1)}, u32[]{:S(2)}) copy-start(bf16[256,256]{1,0:T(8,128)(2,1)} %constant.53.clone.rest_6_) | copy-start | bytes 393220
  4.4 14.5 %copy-start.22 = (bf16[256,256]{1,0:T(8,128)(2,1)S(1)}, bf16[256,256]{1,0:T(8,128)(2,1)}, u32[]{:S(2)}) copy-start(bf16[256,256]{1,0:T(8,128)(2,1)} %constant.54.clone.rest_7_) | copy-start | bytes 393220
  4.4 14.4 %copy-start.24 = (bf16[64,384]{1,0:T(8,128)(2,1)S(1)}, bf16[64,384]{1,0:T(8,128)(2,1)}, u32[]{:S(2)}) copy-start(bf16[64,384]{1,0:T(8,128)(2,1)} %constant.48.clone.rest_1_) | copy-start | bytes 147460
  4.4 14.4 %copy-start.26 = (bf16[128,128]{1,0:T(8,128)(2,1)S(1)}, bf16[128,128]{1,0:T(8,128)(2,1)}, u32[]{:S(2)}) copy-start(bf16[128,128]{1,0:T(8,128)(2,1)} %constant.47.clone.rest_0_) | copy-start | bytes 98308
  4.4 14.4 %copy-start.28 = (f32[64,128]{1,0:T(8,128)S(1)}, f32[64,128]{1,0:T(8,128)}, u32[]{:S(2)}) copy-start(f32[64,128]{1,0:T(8,128)} %constant.49.clone.rest_2_) | copy-start | bytes 98308
  7.7 22.6 %all-to-all-start = ((bf16[32,16,640]{2,1,0:T(8,128)(2,1)}), bf16[32,16,640]{2,1,0:T(8,128)(2,1)S(1)}, u32[]{:S(2)}, u32[]{:S(2)}) async-start(bf16[32,16,640]{2,1,0:T(8,128)(2,1)} %bitcast.3), calls=%async_computation | async-start | bytes 1310720 | tf_op jit(solution)/shard_map/all_to_all | solution.py:353
  18.8 11.6 %copy-start.33 = (f32[16,1]{1,0:T(8,128)}, f32[16,1]{1,0:T(8,128)S(1)}, u32[]{:S(2)}) copy-start(f32[16,1]{1,0:T(8,128)S(1)} %copy.44.gain_ref) | copy-start | bytes 196
  18.8 0.8 copy-start.30
  19.6 0.8 copy-start.35
  27.6 1.0 copy-start.4
  28.6 1.0 copy-start.5
  29.6 0.8 copy-start.12
  30.4 1.2 copy-start.6
  31.6 0.8 copy-start.31
  32.4 13.6 %copy-start.7 = (f32[1024,256]{1,0:T(8,128)S(1)}, f32[1024,256]{1,0:T(8,128)}, u32[]{:S(2)}) copy-start(f32[1024,256]{1,0:T(8,128)} %copy-done.5) | copy-start | bytes 3145732
  34.9 1.0 copy-start.8
  35.9 0.8 copy-start.14
  36.7 0.7 copy-start.16
  37.5 0.6 copy-start.36
  38.1 29.6 %all-to-all-start.1 = ((bf16[32,16,384]{2,1,0:T(8,128)(2,1)}), bf16[32,16,384]{2,1,0:T(8,128)(2,1)S(1)}, u32[]{:S(2)}, u32[]{:S(2)}) async-start(bf16[32,16,384]{2,1,0:T(8,128)(2,1)} %copy-done.16), calls=%async_computation.1 | async-start | bytes 786432 | tf_op jit(solution)/shard_map/all_to_all | solution.py:392
  46.0 1.2 copy-start.9
  47.2 1.0 copy-start.13
  48.3 1.0 copy-start.15
  49.3 0.9 copy-start.21
  50.2 0.9 copy-start.23
  51.1 0.8 copy-start.25
  51.9 0.8 copy-start.27
  52.7 0.8 copy-start.29
  53.4 0.8 copy-start.32
  54.2 0.7 copy-start.34
  54.9 0.7 copy-start.37
  55.6 12.2 %copy-start.11 = (bf16[1,256,512]{2,1,0:T(8,128)(2,1)S(1)}, bf16[1,256,512]{2,1,0:T(8,128)(2,1)}, u32[]{:S(2)}) copy-start(bf16[1,256,512]{2,1,0:T(8,128)(2,1)} %param.18) | copy-start | bytes 786436
  66.1 2.5 %collective-permute-start.2 = (f32[24,128]{1,0:T(8,128)S(1)}, f32[24,128]{1,0:T(8,128)S(1)}, u32[]{:S(2)}, u32[]{:S(2)}) collective-permute-start(f32[24,128]{1,0:T(8,128)S(1)} %fusion), channel_id=1, source_target_pairs={{0,1},{1,0},{2,3},{3,2},{4,5},{5,4},{6,7},{7,6},{8,9},{9,8},{10,11... | collective-permute-start | bytes 36872 | tf_op jit(solution)/shard_map/ppermute | solution.py:343
  67.7 1.9 %collective-permute-start = (bf16[512,384]{1,0:T(8,128)(2,1)S(1)}, bf16[512,384]{1,0:T(8,128)(2,1)S(1)}, u32[]{:S(2)}, u32[]{:S(2)}) collective-permute-start(bf16[512,384]{1,0:T(8,128)(2,1)S(1)} %bitcast.25), channel_id=1, source_target_pairs={{0,1},{1,0},{2,3},{3,2},{4,5},{5,4},{6,7},{7,6},{8,9},{9,8},{10,11... | collective-permute-start | bytes 1179656 | tf_op jit(solution)/shard_map/ppermute | solution.py:419
  67.9 1.8 %collective-permute-start.1 = (bf16[256,256]{1,0:T(8,128)(2,1)S(1)}, bf16[256,256]{1,0:T(8,128)(2,1)S(1)}, u32[]{:S(2)}, u32[]{:S(2)}) collective-permute-start(bf16[256,256]{1,0:T(8,128)(2,1)S(1)} %get-tuple-element.55), channel_id=1, source_target_pairs={{0,1},{1,0},{2,3},{3,2},{4,5},{5,4},{6,7},{7,6},{8,9},{9,8},{10,11... | collective-permute-start | bytes 393224 | tf_op jit(solution)/shard_map/ppermute | solution.py:343
  104.5 24.5 %copy-start.2 = (bf16[512,5,512]{2,0,1:T(8,128)(2,1)S(1)}, bf16[512,5,512]{2,0,1:T(8,128)(2,1)}, u32[]{:S(2)}) copy-start(bf16[512,5,512]{2,0,1:T(8,128)(2,1)} %param.23) | copy-start | bytes 7864324
  124.4 6.3 %collective-permute-start.3 = (f32[16,1280]{1,0:T(8,128)S(1)}, f32[16,1280]{1,0:T(8,128)S(1)}, u32[]{:S(2)}, u32[]{:S(2)}) collective-permute-start(f32[16,1280]{1,0:T(8,128)S(1)} %get-tuple-element.35), channel_id=1, source_target_pairs={{0,1},{1,0},{2,3},{3,2},{4,5},{5,4},{6,7},{7,6},{8,9},{9,8},{10,11... | collective-permute-start | bytes 245768 | tf_op jit(solution)/shard_map/ppermute | solution.py:455
  130.7 1.4 %collective-permute-start.4 = (f32[272,128]{1,0:T(8,128)S(1)}, f32[272,128]{1,0:T(8,128)S(1)}, u32[]{:S(2)}, u32[]{:S(2)}) collective-permute-start(f32[272,128]{1,0:T(8,128)S(1)} %get-tuple-element.36), channel_id=1, source_target_pairs={{0,1},{1,0},{2,3},{3,2},{4,5},{5,4},{6,7},{7,6},{8,9},{9,8},{10,11... | collective-permute-start | bytes 417800 | tf_op jit(solution)/shard_map/ppermute | solution.py:456

commit v2 on v1

v2 whole, which is shorter than its diff:
```python
import math

import jax
import jax.numpy as jnp
import ml_dtypes
import numpy as np
from jax import lax
from jax.experimental import pallas as pl
from jax.experimental.pallas import tpu as pltpu
from jax.sharding import PartitionSpec as P

F32 = jnp.float32
BF16 = jnp.bfloat16

SHARDS = 32
ROWS = 256
LENGTH = SHARDS * ROWS
WIDTH = 512
KERNEL = 5
FEAT = 64
OWN = WIDTH // SHARDS
LANES = 128
STEPS = LENGTH // LANES
STACK = STEPS * OWN
HALO = LANES
SPAN = ROWS + HALO
HALF = WIDTH // 2
CONV = KERNEL * HALF
BLOCK = 1024


def split_table(values):
    high = values.astype(ml_dtypes.bfloat16)
    low = (values - high.astype(np.float64)).astype(ml_dtypes.bfloat16)
    return high, low


def feature_tables():
    half = FEAT // 2
    factor = np.array([1 + i * i * LENGTH // (2 * half * half) for i in range(half)], dtype=np.int64)
    steps = np.arange(LENGTH, dtype=np.int64)
    angles = 2.0 * np.pi * ((factor[:, None] * steps[None, :]) % LENGTH) / LENGTH
    return split_table(np.concatenate([np.sin(angles), np.cos(angles)], axis=0))


def transform_tables():
    order = np.array([2 * p + h for h in range(2) for p in range(STEPS // 2)])
    k1 = np.arange(STEPS)
    alpha = np.pi * order[None, :] / STEPS / 2 - 2.0 * np.pi * ((order[None, :] * k1[:, None]) % STEPS) / STEPS
    outer = np.concatenate([np.cos(alpha), np.sin(alpha)], axis=0)
    outer_high, outer_low = split_table(outer)
    first = np.concatenate([outer_high, outer_low], axis=1)
    back_high, back_low = split_table(outer.T / LENGTH)
    last = np.concatenate([back_high, back_low, back_high], axis=1)
    b = np.arange(LANES)
    beta = np.pi * b[None, :] / (2 * LENGTH) - 2.0 * np.pi * ((b[None, :] * k1[:, None]) % LENGTH) / LENGTH
    twist_cos = np.cos(beta).astype(np.float32)
    twist_sin = np.sin(beta).astype(np.float32)
    gamma = 2.0 * np.pi * ((b[:, None] * b[None, :]) % LANES) / LANES
    cos, sin = np.cos(gamma), np.sin(gamma)
    ahead = split_table(np.block([[cos, -sin], [sin, cos]]))
    behind = split_table(np.block([[cos, sin], [-sin, cos]]))
    return (first, last, twist_cos, twist_sin, *ahead, *behind)


def split(values):
    high = values.astype(BF16)
    return high, (values - high.astype(F32)).astype(BF16)


def mul(left, right, dims=((1,), (0,))):
    return lax.dot_general(left, right, (dims, ((), ())), preferred_element_type=F32)


def mul3(left, right, dims=((1,), (0,))):
    lh, ll = left
    rh, rl = right
    return mul(lh, rh, dims) + mul(ll, rh, dims) + mul(lh, rl, dims)


def wait_for(loads, *which):
    for k in which:
        if loads is not None:
            loads[k].wait()


def spectrum(stack_ref, high_ref, low_ref, tabs, loads=None):
    first, _, tc_ref, ts_ref, ahead_high, ahead_low, _, _ = tabs
    wait_for(loads, 0, 2, 3)
    tc, ts = tc_ref[...], ts_ref[...]
    for c in range(0, OWN, 2):
        pair = [stack_ref[pl.ds(c + k, STEPS, stride=OWN), :] for k in range(2)]
        wide = jnp.concatenate(pair, axis=1).astype(BF16)
        u = mul(first[...], jnp.concatenate([wide, wide], axis=0))
        for k in range(2):
            ur = u[:STEPS, k * LANES : (k + 1) * LANES]
            ui = u[STEPS:, k * LANES : (k + 1) * LANES]
            v = jnp.concatenate([ur * tc - ui * ts, ur * ts + ui * tc], axis=1)
            high, low = split(v)
            high_ref[(c + k) * STEPS : (c + k + 1) * STEPS, :] = high
            low_ref[(c + k) * STEPS : (c + k + 1) * STEPS, :] = low
    wait_for(loads, 4, 5)
    return mul3((high_ref[...], low_ref[...]), (ahead_high[...], ahead_low[...]))


def from_spectrum(values, stack_ref, tabs, loads=None):
    _, last, tc_ref, ts_ref, _, _, behind_high, behind_low = tabs
    wait_for(loads, 6, 7, 1)
    tc, ts = tc_ref[...], ts_ref[...]
    q = mul3(split(values), (behind_high[...], behind_low[...]))
    for c in range(0, OWN, 2):
        pair = []
        for k in range(2):
            rows = q[(c + k) * STEPS : (c + k + 1) * STEPS]
            qr, qi = rows[:, :LANES], rows[:, LANES:]
            pair.append(jnp.concatenate([qr * tc + qi * ts, qi * tc - qr * ts], axis=0))
        high, low = split(jnp.concatenate(pair, axis=1))
        y = mul(last[...], jnp.concatenate([high, high, low], axis=0))
        for k in range(2):
            stack_ref[pl.ds(c + k, STEPS, stride=OWN), :] = y[:, k * LANES : (k + 1) * LANES]


def product(left, right, conjugate):
    lr, li = left[:, :LANES], left[:, LANES:]
    rr, ri = right[:, :LANES], right[:, LANES:]
    if conjugate:
        return jnp.concatenate([lr * rr + li * ri, lr * ri - li * rr], axis=1)
    return jnp.concatenate([lr * rr - li * ri, lr * ri + li * rr], axis=1)


def sin_cos(x):
    turns = jnp.floor(x * (2.0 / math.pi) + 0.5)
    r = x - turns * 1.5703125
    r = r - turns * 4.837512969970703125e-4
    r = r - turns * 7.549789948768648e-8
    z = r * r
    s = r + r * z * (-1.6666654611e-1 + z * (8.3321608736e-3 - z * 1.9515295891e-4))
    c = 1.0 - 0.5 * z + z * z * (4.166664568298827e-2 + z * (-1.388731625493765e-3 + z * 2.443315711809948e-5))
    quad = turns.astype(jnp.int32)
    odd = (quad & 1) == 1
    sin = jnp.where(odd, c, s)
    cos = jnp.where(odd, s, c)
    sin = jnp.where((quad & 2) == 2, -sin, sin)
    cos = jnp.where(((quad + 1) & 2) == 2, -cos, cos)
    return sin, cos


def envelope(rates, start, size):
    steps = (start + lax.broadcasted_iota(jnp.int32, (OWN, size), 1)).astype(F32)
    return jnp.sqrt(rates) * jnp.exp(-steps * rates), steps


def prep_kernel(x_hbm, cot_hbm, w_hbm, out_hbm, x_ref, cot_ref, w_ref, pad_ref, sum_ref, xt_ref, ga_ref, sems):
    x_copy = pltpu.make_async_copy(x_hbm, x_ref, sems.at[0])
    x_copy.start()
    cot_copy = pltpu.make_async_copy(cot_hbm, cot_ref, sems.at[1])
    cot_copy.start()
    w_copies = [pltpu.make_async_copy(w_hbm.at[i], w_ref.at[i], sems.at[2 + i]) for i in range(KERNEL)]
    for copy in w_copies:
        copy.start()
    pad_ref[:HALO, :] = jnp.zeros((HALO, WIDTH), F32)
    pad_ref[HALO + ROWS :, :] = jnp.zeros((8, WIDTH), F32)
    x_copy.wait()
    xt_ref[...] = jnp.transpose(x_ref[...].astype(F32)).astype(BF16)
    x_out = pltpu.make_async_copy(xt_ref, out_hbm.at[:, pl.ds(0, ROWS)], sems.at[2 + KERNEL])
    x_out.start()
    cot_copy.wait()
    pad_ref[HALO : HALO + ROWS, :] = cot_ref[...].astype(F32)
    for i in range(KERNEL):
        shifted = pad_ref[i : i + SPAN, :].astype(BF16)
        w_copies[i].wait()
        part = mul(w_ref[i], shifted, ((1,), (1,)))
        if i == 0:
            sum_ref[...] = part
        elif i < KERNEL - 1:
            sum_ref[...] += part
        else:
            ga_ref[...] = (sum_ref[...] + part).astype(BF16)
    ga_out = pltpu.make_async_copy(ga_ref, out_hbm.at[:, pl.ds(ROWS, SPAN)], sems.at[3 + KERNEL])
    ga_out.start()
    x_out.wait()
    ga_out.wait()


def taps_kernel(wp_ref, wf_ref, lr_ref, gain_ref, feat_ref, *rest):
    tabs = rest[:8]
    hid_out, cos_out, taps_out, spec_ref, par_ref, hid_ref, cos_ref, taps_ref, stack_ref, vh_ref, vl_ref, sems = rest[8:]
    first = lax.axis_index("tm") * OWN
    lane = lax.broadcasted_iota(jnp.int32, (OWN, WIDTH), 1)
    chosen = lane == first + lax.broadcasted_iota(jnp.int32, (OWN, WIDTH), 0)
    wf_own = lax.dot_general(
        chosen.astype(F32),
        wf_ref[...],
        (((1,), (1,)), ((), ())),
        precision=lax.Precision.HIGHEST,
        preferred_element_type=F32,
    )
    rates = jnp.exp(jnp.sum(jnp.where(chosen, lr_ref[...], 0.0), axis=1, keepdims=True))
    gain = jnp.sum(jnp.where(chosen, gain_ref[...], 0.0), axis=1, keepdims=True)
    spot = lax.broadcasted_iota(jnp.int32, (OWN, LANES), 1)
    par_ref[...] = jnp.where(spot == FEAT, rates, jnp.where(spot == FEAT + 1, gain, 0.0))
    par_ref[:, :FEAT] = wf_own
    wp_high, wp_low = split(wp_ref[...])
    wp = jnp.concatenate([wp_high, wp_low, wp_high], axis=0)
    wf_high, wf_low = split(wf_own)
    for start in range(0, LENGTH, BLOCK):
        cut = slice(start, start + BLOCK)
        feat = feat_ref[:, cut]
        sin, cos = sin_cos(mul(wp, jnp.concatenate([feat[:FEAT], feat], axis=0), ((0,), (0,))))
        high, low = split(sin)
        hid_ref[:FEAT, cut] = high
        hid_ref[FEAT:, cut] = low
        cos_ref[:, cut] = cos
        decay, _ = envelope(rates, start, BLOCK)
        taps = mul3((wf_high, wf_low), (high, low)) * decay
        taps_ref[:, cut] = taps
        rounded = taps.astype(BF16).astype(F32)
        for j in range(BLOCK // LANES):
            a = start // LANES + j
            row = ((a % 2) * SHARDS + a // 2) * OWN
            stack_ref[row : row + OWN, :] = rounded[:, j * LANES : (j + 1) * LANES]
    saves = [
        pltpu.make_async_copy(source, target, sems.at[k])
        for k, (source, target) in enumerate(((hid_ref, hid_out), (cos_ref, cos_out), (taps_ref, taps_out)))
    ]
    for save in saves:
        save.start()
    spec_ref[...] = spectrum(stack_ref, vh_ref, vl_ref, tabs)
    for save in saves:
        save.wait()


def forward_kernel(recv_hbm, tspec_hbm, par_hbm, *rest):
    tabs_hbm = rest[:8]
    act_hbm, gb_hbm, xspec_hbm, skip_ref = rest[8:12]
    xin_ref, gain_ref, tspec_ref, spec_ref, act_ref, gb_ref = rest[12:18]
    tabs = rest[18:26]
    x_ref, y_ref, vh_ref, vl_ref, par_ref, sems = rest[26:]
    par_load = pltpu.make_async_copy(par_hbm, par_ref, sems.at[14])
    par_load.start()
    x_load = pltpu.make_async_copy(recv_hbm.at[:, :, pl.ds(0, ROWS)], xin_ref, sems.at[0])
    x_load.start()
    loads = [pltpu.make_async_copy(tabs_hbm[k], tabs[k], sems.at[1 + k]) for k in range(8)]
    for k in (0, 2, 3, 4, 5, 6, 7, 1):
        loads[k].start()
    tspec_load = pltpu.make_async_copy(tspec_hbm, tspec_ref, sems.at[9])
    tspec_load.start()
    ga_load = pltpu.make_async_copy(recv_hbm.at[:, :, pl.ds(ROWS, SPAN)], gain_ref, sems.at[10])
    ga_load.start()
    x_load.wait()
    for h in range(2):
        part = xin_ref[:, :, h * LANES : (h + 1) * LANES].astype(F32)
        x_ref[h * STACK // 2 : (h + 1) * STACK // 2, :] = part.reshape(STACK // 2, LANES)
    spec = spectrum(x_ref, vh_ref, vl_ref, tabs, loads)
    spec_ref[...] = spec
    spec_save = pltpu.make_async_copy(spec_ref, xspec_hbm, sems.at[11])
    spec_save.start()
    tspec_load.wait()
    from_spectrum(product(tspec_ref[...], spec, False), y_ref, tabs, loads)
    par_load.wait()
    gain = par_ref[:, FEAT + 1 : FEAT + 2][None]
    x = x_ref[...].reshape(STEPS, OWN, LANES)
    before = y_ref[...].reshape(STEPS, OWN, LANES) + gain * x
    root = math.sqrt(2.0 / math.pi)
    square = before * before
    th = jnp.tanh(root * (before + 0.044715 * square * before))
    half_cdf = 0.5 * (1.0 + th)
    active = (before * half_cdf).astype(BF16)
    first, second = active[:SHARDS], active[SHARDS:]
    act_ref[:, :, HALO : HALO + LANES] = first
    act_ref[:, :, HALO + LANES :] = second
    act_ref[:, :, :HALO] = jnp.concatenate([jnp.zeros((1, OWN, LANES), BF16), second[:-1]], axis=0)
    act_save = pltpu.make_async_copy(act_ref, act_hbm, sems.at[12])
    act_save.start()
    slope = half_cdf + 0.5 * before * (1.0 - th * th) * (root * (1.0 + 3.0 * 0.044715 * square))
    ga_load.wait()
    early = gain_ref[:, :, HALO : HALO + LANES].astype(F32)
    late = gain_ref[:, :, HALO + LANES :].astype(F32)
    edge = gain_ref[:, :, :HALO].astype(F32)
    edge = jnp.concatenate([edge[1:], jnp.zeros((1, OWN, LANES), F32)], axis=0)
    grad_active = jnp.concatenate([early, late + edge], axis=0)
    grad_before = (grad_active * slope).astype(BF16).astype(F32)
    gb_ref[...] = grad_before.reshape(STACK, LANES)
    gb_save = pltpu.make_async_copy(gb_ref, gb_hbm, sems.at[13])
    gb_save.start()
    skip_ref[...] = jnp.sum(grad_before * x, axis=0)
    spec_save.wait()
    act_save.wait()
    gb_save.wait()


def backward_kernel(*rest):
    arrays_hbm, tabs_hbm = rest[:9], rest[9:17]
    ig_hbm, small_ref = rest[17:19]
    arrays, tabs = rest[19:28], rest[28:36]
    gb_ref, xspec_ref, tspec_ref, par_ref, skip_ref, hid_ref, cos_ref, feat_ref, taps_ref = arrays
    ig_ref, y_ref, vh_ref, vl_ref, g_ref, sems = rest[36:]
    first = [pltpu.make_async_copy(arrays_hbm[k], arrays[k], sems.at[k]) for k in range(9)]
    table = [pltpu.make_async_copy(tabs_hbm[k], tabs[k], sems.at[9 + k]) for k in range(8)]
    for copy in (first[0], *table, *first[1:]):
        copy.start()
    first[0].wait()
    spec = spectrum(gb_ref, vh_ref, vl_ref, tabs, table)
    wait_for(first, 1, 2, 3, 4)
    from_spectrum(product(tspec_ref[...], spec, True), y_ref, tabs, table)
    gain = par_ref[:, FEAT + 1 : FEAT + 2][None]
    grad = gb_ref[...].reshape(STEPS, OWN, LANES)
    result = (y_ref[...].reshape(STEPS, OWN, LANES) + gain * grad).astype(BF16)
    ig_ref[:, :, :LANES] = result[:SHARDS]
    ig_ref[:, :, LANES:] = result[SHARDS:]
    save = pltpu.make_async_copy(ig_ref, ig_hbm, sems.at[17])
    save.start()
    from_spectrum(product(xspec_ref[...], spec, True), y_ref, tabs)
    for a in range(STEPS):
        row = ((a % 2) * SHARDS + a // 2) * OWN
        g_ref[:, a * LANES : (a + 1) * LANES] = y_ref[row : row + OWN, :]
    wf_high, wf_low = split(par_ref[:, :FEAT])
    wf = jnp.concatenate([wf_high, wf_low, wf_high], axis=0)
    rates = par_ref[:, FEAT : FEAT + 1]
    wait_for(first, 5, 6, 7, 8)
    filt = jnp.zeros((2 * OWN, 2 * FEAT), F32)
    pos = jnp.zeros((2 * FEAT, 2 * FEAT), F32)
    rate = jnp.zeros((OWN, 1), F32)
    for start in range(0, LENGTH, BLOCK):
        cut = slice(start, start + BLOCK)
        grad_taps = g_ref[:, cut]
        decay, steps = envelope(rates, start, BLOCK)
        high, low = split(grad_taps * decay)
        rate = rate + jnp.sum(grad_taps * taps_ref[:, cut] * (0.5 - rates * steps), axis=1, keepdims=True)
        filt = filt + mul(jnp.concatenate([high, low], axis=0), hid_ref[:, cut], ((1,), (1,)))
        inner = mul(wf, jnp.concatenate([high, high, low], axis=0), ((0,), (0,))) * cos_ref[:, cut]
        pos = pos + mul(feat_ref[:, cut], jnp.concatenate(split(inner), axis=0), ((1,), (1,)))
    filt = filt[:OWN, :FEAT] + filt[OWN:, :FEAT] + filt[:OWN, FEAT:]
    pos = pos[:FEAT, :FEAT] + pos[FEAT:, :FEAT] + pos[:FEAT, FEAT:]
    skip = jnp.sum(skip_ref[...], axis=1, keepdims=True)
    small_ref[...] = jnp.zeros((2, 2 * OWN, LANES), F32)
    for e, stat in enumerate((rate, skip)):
        small_ref[e, :OWN, :32] = filt[:, 32 * e : 32 * e + 32]
        small_ref[e, :OWN, 32:33] = stat
        small_ref[e, OWN:, :FEAT] = pos[32 * e : 32 * e + 16]
        small_ref[e, OWN:, FEAT:] = pos[32 * e + 16 : 32 * e + 32]
    save.wait()


def conv_kernel(
    act_hbm, peer_act_hbm, cot_hbm, peer_cot_hbm, ig_hbm, small_hbm, peer_small_hbm, out_hbm,
    act_ref, cot_ref, ig_ref, small_ref, pad_ref, part_ref, tile_ref, sems,
):
    core = lax.axis_index("batch") % 2
    half = pl.ds(pl.multiple_of(core * HALF, HALF), HALF)
    sources = [
        (cot_hbm.at[:, half], cot_ref.at[0]),
        (peer_cot_hbm.at[:, half], cot_ref.at[1]),
        (act_hbm, act_ref.at[0]),
        (ig_hbm, ig_ref),
        (small_hbm.at[core], small_ref.at[0]),
        (peer_act_hbm, act_ref.at[1]),
        (peer_small_hbm.at[core], small_ref.at[1]),
    ]
    loads = [pltpu.make_async_copy(a, b, sems.at[k]) for k, (a, b) in enumerate(sources)]
    for load in loads:
        load.start()
    pad_ref[:, :HALO, :] = jnp.zeros((2, HALO, HALF), F32)
    pad_ref[:, HALO + ROWS :, :] = jnp.zeros((2, 8, HALF), F32)
    wait_for(loads, 0, 1)
    pad_ref[:, HALO : HALO + ROWS, :] = cot_ref[...].astype(F32)
    wait_for(loads, 2, 5)
    copies = []
    for i in range(KERNEL):
        own = pad_ref[0, i : i + SPAN, :].astype(BF16)
        peer = pad_ref[1, i : i + SPAN, :].astype(BF16)
        part_ref[i] = (mul(act_ref[0], own) + mul(act_ref[1], peer)).astype(BF16)
        copy = pltpu.make_async_copy(part_ref.at[i], out_hbm.at[:, pl.ds(i * HALF, HALF)], sems.at[7 + i])
        copy.start()
        copies.append(copy)
        if i == 0:
            wait_for(loads, 3, 4, 6)
            tile_ref[:, :ROWS] = ig_ref[...]
            small = small_ref[0] + small_ref[1]
            high, low = split(small[:OWN])
            filt = high.astype(F32) + pltpu.roll(low.astype(F32), FEAT, 1)
            tile = jnp.concatenate([filt, small[OWN:]], axis=1).astype(BF16)
            for p in range(SHARDS):
                tile_ref[p * OWN : (p + 1) * OWN, ROWS:] = tile
            copy = pltpu.make_async_copy(tile_ref, out_hbm.at[:, pl.ds(CONV, ROWS + 2 * LANES)], sems.at[7 + KERNEL])
            copy.start()
            copies.append(copy)
    for copy in copies:
        copy.wait()


def mixed_kernel(act_ref, w_ref, _, out_ref, part_ref):
    act = jnp.transpose(act_ref[...].astype(F32)).astype(BF16)[HALO - 16 :]
    total = jnp.zeros((ROWS, WIDTH), F32)
    for i in range(KERNEL):
        part_ref[...] = mul(act, w_ref[i])
        total = total + part_ref[16 - i : 16 - i + ROWS, :]
    out_ref[...] = total.astype(BF16)


def gather_kernel(recv_ref, _, out_hbm, out_ref, sems):
    conv = jnp.sum(recv_ref[:, :, :CONV].astype(F32), axis=0).astype(BF16)
    for j in range(2):
        out_ref[16 * j : 16 * j + 16, :] = conv[:, j * WIDTH : (j + 1) * WIDTH]
    out_ref[32:48, :HALF] = conv[:, 2 * WIDTH :]
    base = CONV + ROWS
    both = recv_ref[:, :, base : base + LANES].astype(F32).reshape(WIDTH, LANES)
    filt = jnp.transpose(both + pltpu.roll(both, FEAT, 1))
    out_ref[48:80, :] = filt[:32].astype(BF16)
    pos = jnp.sum(recv_ref[:, :, base + LANES : base + 2 * LANES].astype(F32), axis=0)
    out_ref[32:48, HALF : HALF + LANES] = pos.astype(BF16)
    stat = filt[32:33]
    pieces = [stat[:, j * LANES : (j + 1) * LANES] for j in range(4)]
    stat = jnp.concatenate([*pieces, jnp.zeros((12, LANES), F32)], axis=0)
    out_ref[32:48, HALF + LANES :] = stat.astype(BF16)
    copies = [pltpu.make_async_copy(out_ref, out_hbm.at[z], sems.at[z]) for z in range(4)]
    for copy in copies:
        copy.start()
    for copy in copies:
        copy.wait()


def input_kernel(recv_ref, _, out_ref):
    out_ref[...] = jnp.transpose(recv_ref[:, :, CONV : CONV + ROWS].astype(F32).reshape(WIDTH, ROWS)).astype(BF16)


def final_kernel(recv_ref, _, out_ref):
    out_ref[...] = jnp.sum(recv_ref[...].astype(F32), axis=0) * (1.0 / math.sqrt(8 * LENGTH))


def join_kernel(core_ref, mine_ref, other_ref, conv_ref, pos_ref, filt_ref, rates_ref, skip_ref):
    def write(low, high):
        for e, part in enumerate((low, high)):
            for i in range(KERNEL):
                row, lane = 16 * (i // 2), HALF * (i % 2)
                conv_ref[i, :, e * HALF : (e + 1) * HALF] = part[row : row + 16, lane : lane + HALF]
            pos = part[32:48, HALF : HALF + LANES]
            pos_ref[32 * e : 32 * e + 16, :] = pos[:, :FEAT]
            pos_ref[32 * e + 16 : 32 * e + 32, :] = pos[:, FEAT:]
            filt_ref[32 * e : 32 * e + 32, :] = part[48:80, :]
            stat_ref = (rates_ref, skip_ref)[e]
            for j in range(4):
                stat_ref[:, j * LANES : (j + 1) * LANES] = part[32 + j : 33 + j, HALF + LANES :]

    @pl.when(core_ref[0] == 0)
    def _():
        write(mine_ref, other_ref)

    @pl.when(core_ref[0] == 1)
    def _():
        write(other_ref, mine_ref)


VMEM = pl.BlockSpec(memory_space=pltpu.VMEM)
SMEM = pl.BlockSpec(memory_space=pltpu.SMEM)
ANY = pl.BlockSpec(memory_space=pl.ANY)


def call(kernel, out_shape, args, scratch=(), flops=0, name=None, specs=None, out_specs=None, limit=60):
    single = not isinstance(out_shape, (list, tuple))
    outs = [out_shape] if single else out_shape
    moved = sum(math.prod(a.shape) * a.dtype.itemsize for a in (*args, *outs))
    return pl.pallas_call(
        kernel,
        out_shape=out_shape,
        in_specs=specs or [VMEM] * len(args),
        out_specs=out_specs or (VMEM if single else [VMEM] * len(outs)),
        scratch_shapes=list(scratch),
        compiler_params=pltpu.CompilerParams(vmem_limit_bytes=limit * 1024 * 1024),
        cost_estimate=pl.CostEstimate(flops=flops, bytes_accessed=moved, transcendentals=0),
        name=name,
    )(*args)


def shape(dims, kind=F32):
    return jax.ShapeDtypeStruct(dims, kind)


def regroup(blocks):
    return lax.all_to_all(blocks, "tm", split_axis=0, concat_axis=0, tiled=True)


def on_device(inputs, cotangent, w_pos, w_filt, log_rates, skip_gain, w_conv):
    core = lax.axis_index("batch") % 2
    swap = [(i, i ^ 1) for i in range(lax.axis_size("batch"))]
    signal, upstream = inputs[0], cotangent[0]
    w_taps = jnp.transpose(w_conv, (1, 0, 2))
    tabs = tuple(jnp.asarray(t) for t in transform_tables())
    feat = jnp.asarray(np.concatenate(feature_tables(), axis=0))

    message = call(
        prep_kernel,
        shape((WIDTH, ROWS + SPAN), BF16),
        (signal, upstream, w_taps),
        [
            pltpu.VMEM((ROWS, WIDTH), BF16),
            pltpu.VMEM((ROWS, WIDTH), BF16),
            pltpu.VMEM((KERNEL, WIDTH, WIDTH), BF16),
            pltpu.VMEM((HALO + ROWS + 8, WIDTH), F32),
            pltpu.VMEM((WIDTH, SPAN), F32),
            pltpu.VMEM((WIDTH, ROWS), BF16),
            pltpu.VMEM((WIDTH, SPAN), BF16),
            pltpu.SemaphoreType.DMA((4 + KERNEL,)),
        ],
        flops=2 * KERNEL * WIDTH * WIDTH * SPAN,
        name="prep",
        specs=[ANY] * 3,
        out_specs=ANY,
    )
    received = regroup(message.reshape(SHARDS, OWN, ROWS + SPAN))
    cot_peer = lax.ppermute(upstream, "batch", swap)
    received, cot_peer = lax.optimization_barrier((received, cot_peer))

    stack = pltpu.VMEM((STACK, LANES), F32)
    wide = pltpu.VMEM((STACK, 2 * LANES), BF16)
    saved = [pltpu.VMEM((2 * FEAT, LENGTH), BF16), pltpu.VMEM((FEAT, LENGTH), F32), pltpu.VMEM((OWN, LENGTH), F32)]
    flops = 2 * 3 * (2 * STACK * LANES * LANES + STACK * 4 * LANES * LANES)
    hidden, cosines, taps, tap_spec, par = call(
        taps_kernel,
        [
            shape((2 * FEAT, LENGTH), BF16),
            shape((FEAT, LENGTH)),
            shape((OWN, LENGTH)),
            shape((STACK, 2 * LANES)),
            shape((OWN, LANES)),
        ],
        (w_pos, w_filt, log_rates[None], skip_gain[None], feat, *tabs),
        [*saved, stack, wide, wide, pltpu.SemaphoreType.DMA((3,))],
        flops=flops * 2,
        name="taps",
        out_specs=[ANY, ANY, ANY, VMEM, VMEM],
    )
    act_message, grad_before, sig_spec, skip_part = call(
        forward_kernel,
        [
            shape((SHARDS, OWN, SPAN), BF16),
            shape((STACK, LANES)),
            shape((STACK, 2 * LANES)),
            shape((OWN, LANES)),
        ],
        (received, tap_spec, par, *tabs),
        [
            pltpu.VMEM((SHARDS, OWN, ROWS), BF16),
            pltpu.VMEM((SHARDS, OWN, SPAN), BF16),
            pltpu.VMEM((STACK, 2 * LANES), F32),
            pltpu.VMEM((STACK, 2 * LANES), F32),
            pltpu.VMEM((SHARDS, OWN, SPAN), BF16),
            stack,
            *[pltpu.VMEM(t.shape, t.dtype) for t in tabs],
            stack,
            stack,
            wide,
            wide,
            pltpu.VMEM((OWN, LANES), F32),
            pltpu.SemaphoreType.DMA((15,)),
        ],
        flops=flops * 2,
        name="forward",
        specs=[ANY] * 11,
        out_specs=[ANY, ANY, ANY, VMEM],
    )
    act = regroup(act_message).reshape(WIDTH, SPAN)
    ig_message, small = call(
        backward_kernel,
        [shape((SHARDS, OWN, ROWS), BF16), shape((2, 2 * OWN, LANES))],
        (grad_before, sig_spec, tap_spec, par, skip_part, hidden, cosines, feat, taps, *tabs),
        [
            stack,
            pltpu.VMEM((STACK, 2 * LANES), F32),
            pltpu.VMEM((STACK, 2 * LANES), F32),
            pltpu.VMEM((OWN, LANES), F32),
            pltpu.VMEM((OWN, LANES), F32),
            *saved[:2],
            saved[0],
            saved[2],
            *[pltpu.VMEM(t.shape, t.dtype) for t in tabs],
            pltpu.VMEM((SHARDS, OWN, ROWS), BF16),
            stack,
            wide,
            wide,
            pltpu.VMEM((OWN, LENGTH), F32),
            pltpu.SemaphoreType.DMA((18,)),
        ],
        flops=flops * 4,
        name="backward",
        specs=[ANY] * 17,
        out_specs=[ANY, VMEM],
    )
    act, ig_message, small = lax.optimization_barrier((act, ig_message, small))
    act_peer = lax.ppermute(act, "batch", swap)
    small_peer = lax.ppermute(small, "batch", swap)
    lanes = CONV + ROWS + 2 * LANES
    sums = call(
        conv_kernel,
        shape((WIDTH, lanes), BF16),
        (act, act_peer, upstream, cot_peer, ig_message.reshape(WIDTH, ROWS), small, small_peer),
        [
            pltpu.VMEM((2, WIDTH, SPAN), BF16),
            pltpu.VMEM((2, ROWS, HALF), BF16),
            pltpu.VMEM((WIDTH, ROWS), BF16),
            pltpu.VMEM((2, 2 * OWN, LANES), F32),
            pltpu.VMEM((2, HALO + ROWS + 8, HALF), F32),
            pltpu.VMEM((KERNEL, WIDTH, HALF), BF16),
            pltpu.VMEM((WIDTH, ROWS + 2 * LANES), BF16),
            pltpu.SemaphoreType.DMA((8 + KERNEL,)),
        ],
        flops=2 * KERNEL * WIDTH * HALF * 2 * SPAN,
        name="conv_grad",
        specs=[ANY] * 7,
        out_specs=ANY,
    )
    spread = regroup(sums.reshape(SHARDS, OWN, lanes))
    mixed = call(
        mixed_kernel,
        shape((ROWS, WIDTH), BF16),
        (act, w_taps, sums),
        [pltpu.VMEM((ROWS + 16, WIDTH), F32)],
        flops=2 * KERNEL * WIDTH * WIDTH * (ROWS + 16),
        name="mixed",
        specs=[VMEM, VMEM, ANY],
        limit=16,
    )
    payload = call(
        gather_kernel,
        shape((4, 80, WIDTH), BF16),
        (spread, mixed),
        [pltpu.VMEM((80, WIDTH), BF16), pltpu.SemaphoreType.DMA((4,))],
        name="gather",
        specs=[VMEM, ANY],
        out_specs=ANY,
        limit=12,
    )
    input_grad = call(input_kernel, shape((ROWS, WIDTH), BF16), (spread, payload), name="input", specs=[VMEM, ANY], limit=12)
    groups = [[2 * z + e for z in range(4)] for e in range(2)]
    parts = lax.all_to_all(
        payload,
        "batch",
        split_axis=0,
        concat_axis=0,
        tiled=True,
        axis_index_groups=groups,
    )
    total = call(final_kernel, shape((80, WIDTH)), (parts, input_grad), name="final", specs=[VMEM, ANY], limit=12)
    other = lax.ppermute(total, "batch", swap)
    conv_grad, pos_grad, filt_grad, rates_grad, skip_grad = call(
        join_kernel,
        [
            shape((KERNEL, OWN, WIDTH)),
            shape((FEAT, FEAT)),
            shape((FEAT, WIDTH)),
            shape((1, WIDTH)),
            shape((1, WIDTH)),
        ],
        (core.astype(jnp.int32)[None], total, other),
        name="join",
        specs=[SMEM, VMEM, VMEM],
        limit=12,
    )
    return (
        mixed[None],
        input_grad[None],
        jnp.transpose(conv_grad, (1, 0, 2)),
        pos_grad,
        filt_grad,
        rates_grad[0],
        skip_grad[0],
    )


def solution(mesh):
    in_specs = (P("batch", "tm", None), P("batch", "tm", None), P(), P(), P(), P(), P())
    out_specs = (P("batch", "tm", None), P("batch", "tm", None), P("tm", None, None), P(), P(), P(), P())
    return jax.shard_map(on_device, mesh=mesh, in_specs=in_specs, out_specs=out_specs, check_vma=False)
```

time: 136 us -> 114 us (0.84)
  blocking collectives: 52.3 us -> 0 us
  waiting for transfers between devices: 1.74 us -> 32.7 us
  local copies, waits for them, and re-layouts: 27.3 us -> 6.76 us
  starting transfers between devices: 23.9 us -> 36.8 us
  Pallas kernels: 27.8 us -> 36.5 us
    all_to_all x2 -> x0, blocking collectives: 52.3 us -> none  [the longest x1 33.3 us: on_device(): lax.all_to_all(sums.reshape(SHARDS, OWN, lanes), 'tm', split_axis=0, conc...]
    all_to_all x2 -> x4, waiting for transfers between devices: 0.01 us -> 30.2 us  [the longest x3 21.6 us: regroup(): return lax.all_to_all(blocks, 'tm', split_axis=0, concat_axis=0, tiled=True)]
    unnamed x82 -> x22, local copies, waits for them, and re-layouts: 25 us -> 6.76 us
    all_to_all x2 -> x4, starting transfers between devices: 17.1 us -> 29.7 us  [the longest x3 22.4 us: regroup(): return lax.all_to_all(blocks, 'tm', split_axis=0, concat_axis=0, tiled=True)]
    pallas_call x8 -> x10, Pallas kernels: 27.8 us -> 36.5 us  [call(): pl.pallas_call(kernel, out_shape=out_shape, in_specs=specs or [VMEM] * le...]
    ppermute x1, starting transfers between devices: 0.11 us -> 2.11 us  [on_device(): act_peer = lax.ppermute(act, 'batch', swap)]
    ppermute x4 -> x3, starting transfers between devices: 6.69 us -> 5.06 us  [the longest x1 4.01 us: on_device(): other = lax.ppermute(total, 'batch', swap)]
  transfers between devices with their start and end apart: 7 -> 8, of which waited for: 3 -> 6; matrix products, arithmetic and copies ran while one was open for 2% -> 0% of each run, Pallas kernels for 14% -> 18%
where the time goes in v2:
time: 114 us
  starting transfers between devices  36.8 us (32%)
  Pallas kernels  36.5 us (32%)
  waiting for transfers between devices  32.7 us (29%)
  local copies, waits for them, and re-layouts  6.76 us (6%)
    pallas_call x10, Pallas kernels, call(): pl.pallas_call(kernel, out_shape=out_shape, in_specs=specs or [VMEM] * le...  36.5 us
    all_to_all x3, starting transfers between devices, regroup(): return lax.all_to_all(blocks, 'tm', split_axis=0, concat_axis=0, tiled=True)  22.4 us
    all_to_all x3, waiting for transfers between devices, regroup(): return lax.all_to_all(blocks, 'tm', split_axis=0, concat_axis=0, tiled=True)  21.6 us
    all_to_all x1, waiting for transfers between devices, on_device(): lax.all_to_all(payload, 'batch', split_axis=0, concat_axis=0, tiled=True,...  8.65 us
    all_to_all x1, starting transfers between devices, on_device(): lax.all_to_all(payload, 'batch', split_axis=0, concat_axis=0, tiled=True,...  7.29 us
    unnamed x22, local copies, waits for them, and re-layouts  6.76 us
    ppermute x1, starting transfers between devices, on_device(): other = lax.ppermute(total, 'batch', swap)  4.01 us
  transfers between devices with their start and end apart: 8, of which 6 were waited for; matrix products, arithmetic and copies ran while one was open for 0% of the time, Pallas kernels for 18%

profile of v2, /device:TPU:1, one launch (start us, length us, event | category | flops | bytes accessed | tf_op | source)
XLA Modules:
  0.0 113.6 jit_solution(5037284406289884203)
XLA Ops:
  0.6 0.0 copy-start.7
  0.6 4.0 %prep.1 = bf16[512,640]{1,0:T(8,128)(2,1)} custom-call(bf16[256,512]{1,0:T(8,128)(2,1)} %bitcast.24, bf16[256,512]{1,0:T(8,128)(2,1)} %bitcast.25, bf16[5,512,512]{2,1,0:T(8,128)(2,1)} %bitcast.15), custom_call_target="tpu_custom_call" | custom-call | flops 1006632960 | bytes 3801088 | tf_op jit(solution)/shard_map/prep/pallas_call | solution.py:463
  4.6 9.2 %all-to-all-start = ((bf16[32,16,640]{2,1,0:T(8,128)(2,1)}), bf16[32,16,640]{2,1,0:T(8,128)(2,1)S(1)}, u32[]{:S(2)}, u32[]{:S(2)}) async-start(bf16[32,16,640]{2,1,0:T(8,128)(2,1)} %bitcast.23), calls=%async_computation | async-start | bytes 1310720 | tf_op jit(solution)/shard_map/all_to_all | solution.py:480
  13.9 0.0 copy-done.7
  13.9 1.0 collective-permute-start
  14.9 8.7 %taps.1 = (bf16[128,8192]{1,0:T(8,128)(2,1)}, f32[64,8192]{1,0:T(8,128)}, f32[16,8192]{1,0:T(8,128)}, f32[1024,256]{1,0:T(8,128)}, f32[16,128]{1,0:T(8,128)}) custom-call(f32[64,64]{1,0:T(8,128)} %wp_ref.1, f32[64,512]{1,0:T(8,128)} %wf_ref.1, f32[1,512]{1,0:T(1,128)} %bitcast.30, f32[1,512]{1,0:T(1,128)} %bitcast.31, ...), custom_call_target="tpu_custom_call" | custom-call | flops 1207959552 | bytes 8695808 | tf_op jit(solution)/shard_map/taps/pallas_call | solution.py:463
  23.7 0.0 collective-permute-done.peer_cot_hbm
  23.7 0.0 copy-start.9
  23.7 1.4 %all-to-all-done.recv_hbm = bf16[32,16,640]{2,1,0:T(8,128)(2,1)S(1)} async-done(((bf16[32,16,640]{2,1,0:T(8,128)(2,1)}), bf16[32,16,640]{2,1,0:T(8,128)(2,1)S(1)}, u32[]{:S(2)}, u32[]{:S(2)}) %all-to-all-start) | async-done | bytes 655392 | tf_op jit(solution)/shard_map/all_to_all | solution.py:480
  25.1 0.0 copy-start.6
  25.1 0.9 copy-done.6
  25.9 6.3 %forward.1 = (bf16[32,16,384]{2,1,0:T(8,128)(2,1)}, f32[1024,128]{1,0:T(8,128)}, f32[1024,256]{1,0:T(8,128)}, f32[16,128]{1,0:T(8,128)}) custom-call(bf16[32,16,640]{2,1,0:T(8,128)(2,1)} %copy-done.6, f32[1024,256]{1,0:T(8,128)} %get-tuple-element.29.tspec_hbm.rest_2_, f32[16,128]{1,0:T(8,128)} %get-tuple-element.30.par_hbm.rest_3_, ...), custom_call_target="tpu_custom_call" | custom-call | flops 1207959552 | bytes 4358144 | tf_op jit(solution)/shard_map/forward/pallas_call | solution.py:463
  32.2 6.9 %all-to-all-start.1 = ((bf16[32,16,384]{2,1,0:T(8,128)(2,1)}), bf16[32,16,384]{2,1,0:T(8,128)(2,1)S(1)}, u32[]{:S(2)}, u32[]{:S(2)}) async-start(bf16[32,16,384]{2,1,0:T(8,128)(2,1)} %get-tuple-element.31), calls=%async_computation.1 | async-start | bytes 786432 | tf_op jit(solution)/shard_map/all_to_all | solution.py:480
  39.1 8.7 %backward.1 = (bf16[32,16,256]{2,1,0:T(8,128)(2,1)}, f32[2,32,128]{2,1,0:T(8,128)}) custom-call(f32[1024,128]{1,0:T(8,128)} %get-tuple-element.32.rest_0_, f32[1024,256]{1,0:T(8,128)} %get-tuple-element.33.rest_1_, f32[1024,256]{1,0:T(8,128)} %get-tuple-element.29.tspec_hbm.rest_2_, f32[16,128]{1,0:T(8,128)} %get-tuple-element.30.par_hbm.rest_3_, ...), custom_call_target="tpu_custom_call" | custom-call | flops 2415919104 | bytes 10420224 | tf_op jit(solution)/shard_map/backward/pallas_call | solution.py:463
  47.9 0.0 copy-done.9
  47.9 0.2 all-to-all-done.1
  48.1 0.0 copy-start.2
  48.1 2.1 %collective-permute-start.1 = (bf16[512,384]{1,0:T(8,128)(2,1)S(1)}, bf16[512,384]{1,0:T(8,128)(2,1)S(1)}, u32[]{:S(2)}, u32[]{:S(2)}) collective-permute-start(bf16[512,384]{1,0:T(8,128)(2,1)S(1)} %bitcast.18), channel_id=1, source_target_pairs={{0,1},{1,0},{2,3},{3,2},{4,5},{5,4},{6,7},{7,6},{8,9},{9,8},{10,11... | collective-permute-start | bytes 1179656 | tf_op jit(solution)/shard_map/ppermute | solution.py:590
  50.2 0.0 collective-permute-start.2
  50.2 1.5 %collective-permute-done.2.peer_small_hbm = f32[2,32,128]{2,1,0:T(8,128)S(1)} collective-permute-done((f32[2,32,128]{2,1,0:T(8,128)}, f32[2,32,128]{2,1,0:T(8,128)S(1)}, u32[]{:S(2)}, u32[]{:S(2)}) %collective-permute-start.2) | collective-permute-done | bytes 32800 | tf_op jit(solution)/shard_map/ppermute | solution.py:591
  51.6 0.0 copy-start.10
  51.6 0.0 collective-permute-done.1.peer_act_hbm
  51.7 0.0 copy-start.8
  51.7 0.0 copy-done.2
  51.7 0.6 copy-done.10
  52.3 0.1 copy-done.8
  52.4 4.2 %conv_grad.1._ = bf16[512,1792]{1,0:T(8,128)(2,1)} custom-call(bf16[512,384]{1,0:T(8,128)(2,1)} %bitcast.19, bf16[512,384]{1,0:T(8,128)(2,1)} %copy-done.8, bf16[256,512]{1,0:T(8,128)(2,1)} %bitcast.26, bf16[256,512]{1,0:T(8,128)(2,1)} %copy-done.9, bf16[512,256]{1,0:T(8,128)(2,1)} %bitcast.28, f32[2,32,128]{2,1,0:T(8,128)} %get-tuple-element.43.small_hbm, ...), custom_call_target="tpu_custom_call" | custom-call | flops 1006632960 | bytes 3473408 | tf_op jit(solution)/shard_map/conv_grad/pallas_call | solution.py:463
  56.6 0.0 copy-start.3
  56.6 6.3 %all-to-all-start.2 = ((bf16[32,16,1792]{2,1,0:T(8,128)(2,1)}), bf16[32,16,1792]{2,1,0:T(8,128)(2,1)S(1)}, u32[]{:S(2)}, u32[]{:S(2)}) async-start(bf16[32,16,1792]{2,1,0:T(8,128)(2,1)} %bitcast.17), calls=%async_computation.2 | async-start | bytes 3670016 | tf_op jit(solution)/shard_map/all_to_all | solution.py:480
  62.9 0.0 copy-done.3
  62.9 0.0 copy-start
  62.9 1.7 %copy-done = bf16[512,5,512]{2,0,1:T(8,128)(2,1)S(1)} copy-done((bf16[512,5,512]{2,0,1:T(8,128)(2,1)S(1)}, bf16[512,5,512]{2,0,1:T(8,128)(2,1)}, u32[]{:S(2)}) %copy-start) | copy-done | bytes 2621464
  64.6 0.0 copy-start.1
  64.6 1.5 %copy-done.1 = bf16[512,1792]{1,0:T(8,128)(2,1)S(1)} copy-done((bf16[512,1792]{1,0:T(8,128)(2,1)S(1)}, bf16[512,1792]{1,0:T(8,128)(2,1)}, u32[]{:S(2)}) %copy-start.1) | copy-done | bytes 1835032
  66.1 1.7 %mixed.1._ = bf16[256,512]{1,0:T(8,128)(2,1)} custom-call(bf16[512,384]{1,0:T(8,128)(2,1)S(1)} %bitcast.20, bf16[5,512,512]{2,1,0:T(8,128)(2,1)S(1)} %bitcast.16, bf16[512,1792]{1,0:T(8,128)(2,1)S(1)} %copy-done.1), custom_call_target="tpu_custom_call" | custom-call | flops 713031680 | bytes 5111808 | tf_op jit(solution)/shard_map/mixed/pallas_call | solution.py:463
  67.9 20.0 %all-to-all-done.2.recv_ref = bf16[32,16,1792]{2,1,0:T(8,128)(2,1)S(1)} async-done(((bf16[32,16,1792]{2,1,0:T(8,128)(2,1)}), bf16[32,16,1792]{2,1,0:T(8,128)(2,1)S(1)}, u32[]{:S(2)}, u32[]{:S(2)}) %all-to-all-start.2) | async-done | bytes 1835040 | tf_op jit(solution)/shard_map/all_to_all | solution.py:480
  87.9 0.0 copy-start.4
  87.9 0.9 copy-done.4
  88.8 1.1 %gather.1._ = bf16[4,80,512]{2,1,0:T(8,128)(2,1)} custom-call(bf16[32,16,1792]{2,1,0:T(8,128)(2,1)S(1)} %all-to-all-done.2.recv_ref, bf16[256,512]{1,0:T(8,128)(2,1)S(1)} %copy-done.4), custom_call_target="tpu_custom_call" | custom-call | bytes 2424832 | tf_op jit(solution)/shard_map/gather/pallas_call | solution.py:463
  90.0 7.3 %all-to-all-start.3 = ((bf16[4,80,512]{2,1,0:T(8,128)(2,1)}), bf16[4,80,512]{2,1,0:T(8,128)(2,1)S(1)}, u32[]{:S(2)}, u32[]{:S(2)}) async-start(bf16[4,80,512]{2,1,0:T(8,128)(2,1)} %gather.1._), calls=%async_computation.3 | async-start | bytes 655360 | tf_op jit(solution)/shard_map/all_to_all | solution.py:635
  97.3 0.8 input.1._
  98.1 8.6 %all-to-all-done.3.recv_ref = bf16[4,80,512]{2,1,0:T(8,128)(2,1)S(1)} async-done(((bf16[4,80,512]{2,1,0:T(8,128)(2,1)}), bf16[4,80,512]{2,1,0:T(8,128)(2,1)S(1)}, u32[]{:S(2)}, u32[]{:S(2)}) %all-to-all-start.3) | async-done | bytes 327712 | tf_op jit(solution)/shard_map/all_to_all | solution.py:635
  106.8 0.0 copy-start.5
  106.8 0.9 copy-done.5
  107.8 4.0 %collective-permute-start.3 = (f32[80,512]{1,0:T(8,128)S(1)}, f32[80,512]{1,0:T(8,128)S(1)}, u32[]{:S(2)}, u32[]{:S(2)}) collective-permute-start(f32[80,512]{1,0:T(8,128)S(1)} %final.1.mine_ref), channel_id=1, source_target_pairs={{0,1},{1,0},{2,3},{3,2},{4,5},{5,4},{6,7},{7,6},{8,9},{9,8},{10,11... | collective-permute-start | bytes 491528 | tf_op jit(solution)/shard_map/ppermute | solution.py:644
  111.8 1.0 collective-permute-done.3.other_ref
  112.8 0.8 join.1
  (1 shorter events, 0.0 us)
Async XLA Ops:
  0.6 13.2 %copy-start.7 = (bf16[1,256,512]{2,1,0:T(8,128)(2,1)S(1)}, bf16[1,256,512]{2,1,0:T(8,128)(2,1)}, u32[]{:S(2)}) copy-start(bf16[1,256,512]{2,1,0:T(8,128)(2,1)} %param.17) | copy-start | bytes 786436
  4.6 20.4 %all-to-all-start = ((bf16[32,16,640]{2,1,0:T(8,128)(2,1)}), bf16[32,16,640]{2,1,0:T(8,128)(2,1)S(1)}, u32[]{:S(2)}, u32[]{:S(2)}) async-start(bf16[32,16,640]{2,1,0:T(8,128)(2,1)} %bitcast.23), calls=%async_computation | async-start | bytes 1310720 | tf_op jit(solution)/shard_map/all_to_all | solution.py:480
  13.9 9.8 %collective-permute-start = (bf16[256,512]{1,0:T(8,128)(2,1)S(1)}, bf16[256,512]{1,0:T(8,128)(2,1)S(1)}, u32[]{:S(2)}, u32[]{:S(2)}) collective-permute-start(bf16[256,512]{1,0:T(8,128)(2,1)S(1)} %bitcast.27), channel_id=1, source_target_pairs={{0,1},{1,0},{2,3},{3,2},{4,5},{5,4},{6,7},{7,6},{8,9},{9,8},{10,11... | collective-permute-start | bytes 786440 | tf_op jit(solution)/shard_map/ppermute | solution.py:511
  23.7 24.2 %copy-start.9 = (bf16[256,512]{1,0:T(8,128)(2,1)}, bf16[256,512]{1,0:T(8,128)(2,1)S(1)}, u32[]{:S(2)}) copy-start(bf16[256,512]{1,0:T(8,128)(2,1)S(1)} %collective-permute-done.peer_cot_hbm) | copy-start | bytes 786436
  25.1 0.9 copy-start.6
  32.2 15.8 %all-to-all-start.1 = ((bf16[32,16,384]{2,1,0:T(8,128)(2,1)}), bf16[32,16,384]{2,1,0:T(8,128)(2,1)S(1)}, u32[]{:S(2)}, u32[]{:S(2)}) async-start(bf16[32,16,384]{2,1,0:T(8,128)(2,1)} %get-tuple-element.31), calls=%async_computation.1 | async-start | bytes 786432 | tf_op jit(solution)/shard_map/all_to_all | solution.py:480
  48.1 3.6 %copy-start.2 = (bf16[32,16,384]{2,1,0:T(8,128)(2,1)}, bf16[32,16,384]{2,1,0:T(8,128)(2,1)S(1)}, u32[]{:S(2)}) copy-start(bf16[32,16,384]{2,1,0:T(8,128)(2,1)S(1)} %all-to-all-done.1) | copy-start | bytes 1179652
  48.1 3.6 %collective-permute-start.1 = (bf16[512,384]{1,0:T(8,128)(2,1)S(1)}, bf16[512,384]{1,0:T(8,128)(2,1)S(1)}, u32[]{:S(2)}, u32[]{:S(2)}) collective-permute-start(bf16[512,384]{1,0:T(8,128)(2,1)S(1)} %bitcast.18), channel_id=1, source_target_pairs={{0,1},{1,0},{2,3},{3,2},{4,5},{5,4},{6,7},{7,6},{8,9},{9,8},{10,11... | collective-permute-start | bytes 1179656 | tf_op jit(solution)/shard_map/ppermute | solution.py:590
  50.2 1.5 %collective-permute-start.2 = (f32[2,32,128]{2,1,0:T(8,128)}, f32[2,32,128]{2,1,0:T(8,128)S(1)}, u32[]{:S(2)}, u32[]{:S(2)}) collective-permute-start(f32[2,32,128]{2,1,0:T(8,128)} %get-tuple-element.43.small_hbm), channel_id=1, source_target_pairs={{0,1},{1,0},{2,3},{3,2},{4,5},{5,4},{6,7},{7,6},{8,9},{9,8},{10,11... | collective-permute-start | bytes 98312 | tf_op jit(solution)/shard_map/ppermute | solution.py:591
  51.6 0.6 copy-start.10
  51.7 0.8 copy-start.8
  56.6 6.3 %copy-start.3 = (bf16[32,16,384]{2,1,0:T(8,128)(2,1)S(1)}, bf16[32,16,384]{2,1,0:T(8,128)(2,1)}, u32[]{:S(2)}) copy-start(bf16[32,16,384]{2,1,0:T(8,128)(2,1)} %copy-done.2) | copy-start | bytes 1179652
  56.6 31.3 %all-to-all-start.2 = ((bf16[32,16,1792]{2,1,0:T(8,128)(2,1)}), bf16[32,16,1792]{2,1,0:T(8,128)(2,1)S(1)}, u32[]{:S(2)}, u32[]{:S(2)}) async-start(bf16[32,16,1792]{2,1,0:T(8,128)(2,1)} %bitcast.17), calls=%async_computation.2 | async-start | bytes 3670016 | tf_op jit(solution)/shard_map/all_to_all | solution.py:480
  62.9 1.7 %copy-start = (bf16[512,5,512]{2,0,1:T(8,128)(2,1)S(1)}, bf16[512,5,512]{2,0,1:T(8,128)(2,1)}, u32[]{:S(2)}) copy-start(bf16[512,5,512]{2,0,1:T(8,128)(2,1)} %param.22) | copy-start | bytes 7864324
  64.6 1.5 %copy-start.1 = (bf16[512,1792]{1,0:T(8,128)(2,1)S(1)}, bf16[512,1792]{1,0:T(8,128)(2,1)}, u32[]{:S(2)}) copy-start(bf16[512,1792]{1,0:T(8,128)(2,1)} %conv_grad.1._) | copy-start | bytes 5505028
  87.9 1.0 copy-start.4
  90.0 16.8 %all-to-all-start.3 = ((bf16[4,80,512]{2,1,0:T(8,128)(2,1)}), bf16[4,80,512]{2,1,0:T(8,128)(2,1)S(1)}, u32[]{:S(2)}, u32[]{:S(2)}) async-start(bf16[4,80,512]{2,1,0:T(8,128)(2,1)} %gather.1._), calls=%async_computation.3 | async-start | bytes 655360 | tf_op jit(solution)/shard_map/all_to_all | solution.py:635
  106.8 1.0 copy-start.5
  107.8 5.0 %collective-permute-start.3 = (f32[80,512]{1,0:T(8,128)S(1)}, f32[80,512]{1,0:T(8,128)S(1)}, u32[]{:S(2)}, u32[]{:S(2)}) collective-permute-start(f32[80,512]{1,0:T(8,128)S(1)} %final.1.mine_ref), channel_id=1, source_target_pairs={{0,1},{1,0},{2,3},{3,2},{4,5},{5,4},{6,7},{7,6},{8,9},{9,8},{10,11... | collective-permute-start | bytes 491528 | tf_op jit(solution)/shard_map/ppermute | solution.py:644

commit v3 on v2

--- a/solution.py
+++ b/solution.py
@@ -25,8 +25,10 @@
 HALO = LANES
 SPAN = ROWS + HALO
 HALF = WIDTH // 2
+EDGE = 16
 CONV = KERNEL * HALF
 BLOCK = 1024
+SCALE = 1.0 / math.sqrt(8 * LENGTH)
 
 
 def split_table(values):
@@ -158,24 +160,24 @@
     w_copies = [pltpu.make_async_copy(w_hbm.at[i], w_ref.at[i], sems.at[2 + i]) for i in range(KERNEL)]
     for copy in w_copies:
         copy.start()
-    pad_ref[:HALO, :] = jnp.zeros((HALO, WIDTH), F32)
-    pad_ref[HALO + ROWS :, :] = jnp.zeros((8, WIDTH), F32)
+    pad_ref[:EDGE, :] = jnp.zeros((EDGE, WIDTH), F32)
+    pad_ref[EDGE + ROWS :, :] = jnp.zeros((8, WIDTH), F32)
     x_copy.wait()
     xt_ref[...] = jnp.transpose(x_ref[...].astype(F32)).astype(BF16)
     x_out = pltpu.make_async_copy(xt_ref, out_hbm.at[:, pl.ds(0, ROWS)], sems.at[2 + KERNEL])
     x_out.start()
     cot_copy.wait()
-    pad_ref[HALO : HALO + ROWS, :] = cot_ref[...].astype(F32)
+    pad_ref[EDGE : EDGE + ROWS, :] = cot_ref[...].astype(F32)
     for i in range(KERNEL):
-        shifted = pad_ref[i : i + SPAN, :].astype(BF16)
+        shifted = pad_ref[i : i + EDGE + ROWS, :].astype(BF16)
         w_copies[i].wait()
-        part = mul(w_ref[i], shifted, ((1,), (1,)))
+        part = mul(shifted, w_ref[i], ((1,), (1,)))
         if i == 0:
-            sum_ref[...] = part
-        elif i < KERNEL - 1:
-            sum_ref[...] += part
+            sum_ref[HALO - EDGE :, :] = part
         else:
-            ga_ref[...] = (sum_ref[...] + part).astype(BF16)
+            sum_ref[HALO - EDGE :, :] += part
+    sum_ref[: HALO - EDGE, :] = jnp.zeros((HALO - EDGE, WIDTH), F32)
+    ga_ref[...] = jnp.transpose(sum_ref[...]).astype(BF16)
     ga_out = pltpu.make_async_copy(ga_ref, out_hbm.at[:, pl.ds(ROWS, SPAN)], sems.at[3 + KERNEL])
     ga_out.start()
     x_out.wait()
@@ -184,7 +186,8 @@
 
 def taps_kernel(wp_ref, wf_ref, lr_ref, gain_ref, feat_ref, *rest):
     tabs = rest[:8]
-    hid_out, cos_out, taps_out, spec_ref, par_ref, hid_ref, cos_ref, taps_ref, stack_ref, vh_ref, vl_ref, sems = rest[8:]
+    hid_out, cos_out, taps_out, spec_out, par_out = rest[8:13]
+    hid_ref, cos_ref, taps_ref, spec_ref, par_ref, stack_ref, vh_ref, vl_ref, sems = rest[13:]
     first = lax.axis_index("tm") * OWN
     lane = lax.broadcasted_iota(jnp.int32, (OWN, WIDTH), 1)
     chosen = lane == first + lax.broadcasted_iota(jnp.int32, (OWN, WIDTH), 0)
@@ -221,23 +224,32 @@
             stack_ref[row : row + OWN, :] = rounded[:, j * LANES : (j + 1) * LANES]
     saves = [
         pltpu.make_async_copy(source, target, sems.at[k])
-        for k, (source, target) in enumerate(((hid_ref, hid_out), (cos_ref, cos_out), (taps_ref, taps_out)))
+        for k, (source, target) in enumerate(((hid_ref, hid_out), (cos_ref, cos_out), (taps_ref, taps_out), (par_ref, par_out)))
     ]
     for save in saves:
         save.start()
     spec_ref[...] = spectrum(stack_ref, vh_ref, vl_ref, tabs)
+    saves.append(pltpu.make_async_copy(spec_ref, spec_out, sems.at[4]))
+    saves[-1].start()
     for save in saves:
         save.wait()
 
 
+def gelu_parts(before):
+    root = math.sqrt(2.0 / math.pi)
+    square = before * before
+    th = jnp.tanh(root * (before + 0.044715 * square * before))
+    half_cdf = 0.5 * (1.0 + th)
+    slope = half_cdf + 0.5 * before * (1.0 - th * th) * (root * (1.0 + 3.0 * 0.044715 * square))
+    return before * half_cdf, slope
+
+
 def forward_kernel(recv_hbm, tspec_hbm, par_hbm, *rest):
     tabs_hbm = rest[:8]
-    act_hbm, gb_hbm, xspec_hbm, skip_ref = rest[8:12]
-    xin_ref, gain_ref, tspec_ref, spec_ref, act_ref, gb_ref = rest[12:18]
-    tabs = rest[18:26]
-    x_ref, y_ref, vh_ref, vl_ref, par_ref, sems = rest[26:]
-    par_load = pltpu.make_async_copy(par_hbm, par_ref, sems.at[14])
-    par_load.start()
+    act_hbm, before_hbm, xspec_hbm = rest[8:11]
+    xin_ref, tspec_ref, spec_ref, act_ref = rest[11:15]
+    tabs = rest[15:23]
+    x_ref, y_ref, vh_ref, vl_ref, par_ref, sems = rest[23:]
     x_load = pltpu.make_async_copy(recv_hbm.at[:, :, pl.ds(0, ROWS)], xin_ref, sems.at[0])
     x_load.start()
     loads = [pltpu.make_async_copy(tabs_hbm[k], tabs[k], sems.at[1 + k]) for k in range(8)]
@@ -245,8 +257,8 @@
         loads[k].start()
     tspec_load = pltpu.make_async_copy(tspec_hbm, tspec_ref, sems.at[9])
     tspec_load.start()
-    ga_load = pltpu.make_async_copy(recv_hbm.at[:, :, pl.ds(ROWS, SPAN)], gain_ref, sems.at[10])
-    ga_load.start()
+    par_load = pltpu.make_async_copy(par_hbm, par_ref, sems.at[10])
+    par_load.start()
     x_load.wait()
     for h in range(2):
         part = xin_ref[:, :, h * LANES : (h + 1) * LANES].astype(F32)
@@ -259,52 +271,46 @@
     from_spectrum(product(tspec_ref[...], spec, False), y_ref, tabs, loads)
     par_load.wait()
     gain = par_ref[:, FEAT + 1 : FEAT + 2][None]
-    x = x_ref[...].reshape(STEPS, OWN, LANES)
-    before = y_ref[...].reshape(STEPS, OWN, LANES) + gain * x
-    root = math.sqrt(2.0 / math.pi)
-    square = before * before
-    th = jnp.tanh(root * (before + 0.044715 * square * before))
-    half_cdf = 0.5 * (1.0 + th)
-    active = (before * half_cdf).astype(BF16)
-    first, second = active[:SHARDS], active[SHARDS:]
-    act_ref[:, :, HALO : HALO + LANES] = first
-    act_ref[:, :, HALO + LANES :] = second
-    act_ref[:, :, :HALO] = jnp.concatenate([jnp.zeros((1, OWN, LANES), BF16), second[:-1]], axis=0)
-    act_save = pltpu.make_async_copy(act_ref, act_hbm, sems.at[12])
+    before = y_ref[...].reshape(STEPS, OWN, LANES) + gain * x_ref[...].reshape(STEPS, OWN, LANES)
+    y_ref[...] = before.reshape(STACK, LANES)
+    before_save = pltpu.make_async_copy(y_ref, before_hbm, sems.at[12])
+    before_save.start()
+    active = gelu_parts(before)[0].astype(BF16)
+    act_ref[:, :, HALO : HALO + LANES] = active[:SHARDS]
+    act_ref[:, :, HALO + LANES :] = active[SHARDS:]
+    act_ref[:, :, :HALO] = jnp.concatenate([jnp.zeros((1, OWN, LANES), BF16), active[SHARDS:-1]], axis=0)
+    act_save = pltpu.make_async_copy(act_ref, act_hbm, sems.at[13])
     act_save.start()
-    slope = half_cdf + 0.5 * before * (1.0 - th * th) * (root * (1.0 + 3.0 * 0.044715 * square))
-    ga_load.wait()
-    early = gain_ref[:, :, HALO : HALO + LANES].astype(F32)
-    late = gain_ref[:, :, HALO + LANES :].astype(F32)
-    edge = gain_ref[:, :, :HALO].astype(F32)
+    spec_save.wait()
+    before_save.wait()
+    act_save.wait()
+
+
+def backward_kernel(*rest):
+    arrays_hbm, tabs_hbm = rest[:9], rest[9:17]
+    ig_hbm, small_hbm = rest[17:19]
+    arrays, tabs = rest[19:28], rest[28:36]
+    recv_ref, before_ref, xspec_ref, tspec_ref, par_ref, hid_ref, cos_ref, feat_ref, taps_ref = arrays
+    gb_ref, ig_ref, small_ref, y_ref, vh_ref, vl_ref, g_ref, sems = rest[36:]
+    first = [pltpu.make_async_copy(arrays_hbm[k], arrays[k], sems.at[k]) for k in range(9)]
+    table = [pltpu.make_async_copy(tabs_hbm[k], tabs[k], sems.at[9 + k]) for k in range(8)]
+    for copy in (*first[:2], *table, *first[2:]):
+        copy.start()
+    wait_for(first, 0, 1)
+    early = recv_ref[:, :, ROWS + HALO : ROWS + HALO + LANES].astype(F32)
+    late = recv_ref[:, :, ROWS + HALO + LANES :].astype(F32)
+    edge = recv_ref[:, :, ROWS : ROWS + HALO].astype(F32)
     edge = jnp.concatenate([edge[1:], jnp.zeros((1, OWN, LANES), F32)], axis=0)
     grad_active = jnp.concatenate([early, late + edge], axis=0)
-    grad_before = (grad_active * slope).astype(BF16).astype(F32)
-    gb_ref[...] = grad_before.reshape(STACK, LANES)
-    gb_save = pltpu.make_async_copy(gb_ref, gb_hbm, sems.at[13])
-    gb_save.start()
-    skip_ref[...] = jnp.sum(grad_before * x, axis=0)
-    spec_save.wait()
-    act_save.wait()
-    gb_save.wait()
-
-
-def backward_kernel(*rest):
-    arrays_hbm, tabs_hbm = rest[:9], rest[9:17]
-    ig_hbm, small_ref = rest[17:19]
-    arrays, tabs = rest[19:28], rest[28:36]
-    gb_ref, xspec_ref, tspec_ref, par_ref, skip_ref, hid_ref, cos_ref, feat_ref, taps_ref = arrays
-    ig_ref, y_ref, vh_ref, vl_ref, g_ref, sems = rest[36:]
-    first = [pltpu.make_async_copy(arrays_hbm[k], arrays[k], sems.at[k]) for k in range(9)]
-    table = [pltpu.make_async_copy(tabs_hbm[k], tabs[k], sems.at[9 + k]) for k in range(8)]
-    for copy in (first[0], *table, *first[1:]):
-        copy.start()
-    first[0].wait()
+    slope = gelu_parts(before_ref[...])[1].reshape(STEPS, OWN, LANES)
+    grad = (grad_active * slope).astype(BF16).astype(F32)
+    gb_ref[...] = grad.reshape(STACK, LANES)
+    x = jnp.concatenate([recv_ref[:, :, :LANES].astype(F32), recv_ref[:, :, LANES:ROWS].astype(F32)], axis=0)
+    skip = jnp.sum(jnp.sum(grad * x, axis=0), axis=1, keepdims=True)
     spec = spectrum(gb_ref, vh_ref, vl_ref, tabs, table)
-    wait_for(first, 1, 2, 3, 4)
+    wait_for(first, 2, 3, 4)
     from_spectrum(product(tspec_ref[...], spec, True), y_ref, tabs, table)
     gain = par_ref[:, FEAT + 1 : FEAT + 2][None]
-    grad = gb_ref[...].reshape(STEPS, OWN, LANES)
     result = (y_ref[...].reshape(STEPS, OWN, LANES) + gain * grad).astype(BF16)
     ig_ref[:, :, :LANES] = result[:SHARDS]
     ig_ref[:, :, LANES:] = result[SHARDS:]
@@ -332,14 +338,16 @@
         pos = pos + mul(feat_ref[:, cut], jnp.concatenate(split(inner), axis=0), ((1,), (1,)))
     filt = filt[:OWN, :FEAT] + filt[OWN:, :FEAT] + filt[:OWN, FEAT:]
     pos = pos[:FEAT, :FEAT] + pos[FEAT:, :FEAT] + pos[:FEAT, FEAT:]
-    skip = jnp.sum(skip_ref[...], axis=1, keepdims=True)
     small_ref[...] = jnp.zeros((2, 2 * OWN, LANES), F32)
     for e, stat in enumerate((rate, skip)):
         small_ref[e, :OWN, :32] = filt[:, 32 * e : 32 * e + 32]
         small_ref[e, :OWN, 32:33] = stat
         small_ref[e, OWN:, :FEAT] = pos[32 * e : 32 * e + 16]
         small_ref[e, OWN:, FEAT:] = pos[32 * e + 16 : 32 * e + 32]
+    small_save = pltpu.make_async_copy(small_ref, small_hbm, sems.at[18])
+    small_save.start()
     save.wait()
+    small_save.wait()
 
 
 def conv_kernel(
@@ -352,9 +360,9 @@
         (cot_hbm.at[:, half], cot_ref.at[0]),
         (peer_cot_hbm.at[:, half], cot_ref.at[1]),
         (act_hbm, act_ref.at[0]),
+        (peer_act_hbm, act_ref.at[1]),
         (ig_hbm, ig_ref),
         (small_hbm.at[core], small_ref.at[0]),
-        (peer_act_hbm, act_ref.at[1]),
         (peer_small_hbm.at[core], small_ref.at[1]),
     ]
     loads = [pltpu.make_async_copy(a, b, sems.at[k]) for k, (a, b) in enumerate(sources)]
@@ -364,17 +372,16 @@
     pad_ref[:, HALO + ROWS :, :] = jnp.zeros((2, 8, HALF), F32)
     wait_for(loads, 0, 1)
     pad_ref[:, HALO : HALO + ROWS, :] = cot_ref[...].astype(F32)
-    wait_for(loads, 2, 5)
+    wait_for(loads, 2, 3)
     copies = []
     for i in range(KERNEL):
         own = pad_ref[0, i : i + SPAN, :].astype(BF16)
         peer = pad_ref[1, i : i + SPAN, :].astype(BF16)
         part_ref[i] = (mul(act_ref[0], own) + mul(act_ref[1], peer)).astype(BF16)
-        copy = pltpu.make_async_copy(part_ref.at[i], out_hbm.at[:, pl.ds(i * HALF, HALF)], sems.at[7 + i])
-        copy.start()
-        copies.append(copy)
+        copies.append(pltpu.make_async_copy(part_ref.at[i], out_hbm.at[:, pl.ds(i * HALF, HALF)], sems.at[9 + i]))
+        copies[-1].start()
         if i == 0:
-            wait_for(loads, 3, 4, 6)
+            wait_for(loads, 4, 5, 6)
             tile_ref[:, :ROWS] = ig_ref[...]
             small = small_ref[0] + small_ref[1]
             high, low = split(small[:OWN])
@@ -382,78 +389,92 @@
             tile = jnp.concatenate([filt, small[OWN:]], axis=1).astype(BF16)
             for p in range(SHARDS):
                 tile_ref[p * OWN : (p + 1) * OWN, ROWS:] = tile
-            copy = pltpu.make_async_copy(tile_ref, out_hbm.at[:, pl.ds(CONV, ROWS + 2 * LANES)], sems.at[7 + KERNEL])
-            copy.start()
-            copies.append(copy)
+            target = out_hbm.at[:, pl.ds(CONV, ROWS + 2 * LANES)]
+            copies.append(pltpu.make_async_copy(tile_ref, target, sems.at[9 + KERNEL]))
+            copies[-1].start()
     for copy in copies:
         copy.wait()
 
 
-def mixed_kernel(act_ref, w_ref, _, out_ref, part_ref):
-    act = jnp.transpose(act_ref[...].astype(F32)).astype(BF16)[HALO - 16 :]
+def mixed_kernel(act_hbm, w_hbm, _, out_hbm, act_ref, w_ref, part_ref, out_ref, sems):
+    loads = [pltpu.make_async_copy(w_hbm.at[i], w_ref.at[i], sems.at[i]) for i in range(KERNEL)]
+    loads.append(pltpu.make_async_copy(act_hbm, act_ref, sems.at[KERNEL]))
+    for load in loads:
+        load.start()
+    wait_for(loads, KERNEL)
+    act = jnp.transpose(act_ref[...].astype(F32)).astype(BF16)[HALO - EDGE :]
     total = jnp.zeros((ROWS, WIDTH), F32)
     for i in range(KERNEL):
+        wait_for(loads, i)
         part_ref[...] = mul(act, w_ref[i])
-        total = total + part_ref[16 - i : 16 - i + ROWS, :]
+        total = total + part_ref[EDGE - i : EDGE - i + ROWS, :]
     out_ref[...] = total.astype(BF16)
-
-
-def gather_kernel(recv_ref, _, out_hbm, out_ref, sems):
-    conv = jnp.sum(recv_ref[:, :, :CONV].astype(F32), axis=0).astype(BF16)
-    for j in range(2):
-        out_ref[16 * j : 16 * j + 16, :] = conv[:, j * WIDTH : (j + 1) * WIDTH]
-    out_ref[32:48, :HALF] = conv[:, 2 * WIDTH :]
+    save = pltpu.make_async_copy(out_ref, out_hbm, sems.at[KERNEL + 1])
+    save.start()
+    save.wait()
+
+
+def fold(block):
+    return jnp.concatenate([block[:8], block[8:]], axis=1)
+
+
+def gather_kernel(recv_ref, out_ref):
+    conv = jnp.sum(recv_ref[:, :, :CONV].astype(F32), axis=0)
+    blocks = [conv[:, :WIDTH], conv[:, WIDTH : 2 * WIDTH], fold(conv[:, 2 * WIDTH :])]
     base = CONV + ROWS
     both = recv_ref[:, :, base : base + LANES].astype(F32).reshape(WIDTH, LANES)
     filt = jnp.transpose(both + pltpu.roll(both, FEAT, 1))
-    out_ref[48:80, :] = filt[:32].astype(BF16)
     pos = jnp.sum(recv_ref[:, :, base + LANES : base + 2 * LANES].astype(F32), axis=0)
-    out_ref[32:48, HALF : HALF + LANES] = pos.astype(BF16)
     stat = filt[32:33]
     pieces = [stat[:, j * LANES : (j + 1) * LANES] for j in range(4)]
-    stat = jnp.concatenate([*pieces, jnp.zeros((12, LANES), F32)], axis=0)
-    out_ref[32:48, HALF + LANES :] = stat.astype(BF16)
-    copies = [pltpu.make_async_copy(out_ref, out_hbm.at[z], sems.at[z]) for z in range(4)]
-    for copy in copies:
-        copy.start()
-    for copy in copies:
-        copy.wait()
-
-
-def input_kernel(recv_ref, _, out_ref):
+    stat = jnp.concatenate([*pieces, jnp.zeros((4, LANES), F32)], axis=0)
+    last = jnp.concatenate([fold(pos), stat, jnp.zeros((8, LANES), F32)], axis=1)
+    out_ref[...] = jnp.concatenate([*blocks, filt[:32], last], axis=0).astype(BF16)
+
+
+def final_kernel(own_ref, first_ref, second_ref, third_ref, out_ref):
+    across = own_ref[...].astype(F32) + second_ref[...].astype(F32)
+    beside = first_ref[...].astype(F32) + third_ref[...].astype(F32)
+    out_ref[...] = (across + beside) * SCALE
+
+
+def input_kernel(recv_ref, out_hbm, out_ref, sem):
     out_ref[...] = jnp.transpose(recv_ref[:, :, CONV : CONV + ROWS].astype(F32).reshape(WIDTH, ROWS)).astype(BF16)
-
-
-def final_kernel(recv_ref, _, out_ref):
-    out_ref[...] = jnp.sum(recv_ref[...].astype(F32), axis=0) * (1.0 / math.sqrt(8 * LENGTH))
-
-
-def join_kernel(core_ref, mine_ref, other_ref, conv_ref, pos_ref, filt_ref, rates_ref, skip_ref):
+    save = pltpu.make_async_copy(out_ref, out_hbm, sem)
+    save.start()
+    save.wait()
+
+
+def join_kernel(mine_ref, other_ref, conv_ref, pos_ref, filt_ref, rates_ref, skip_ref):
+    core = lax.axis_index("batch") % 2
+
     def write(low, high):
         for e, part in enumerate((low, high)):
-            for i in range(KERNEL):
+            lanes = slice(e * HALF, (e + 1) * HALF)
+            for i in range(KERNEL - 1):
                 row, lane = 16 * (i // 2), HALF * (i % 2)
-                conv_ref[i, :, e * HALF : (e + 1) * HALF] = part[row : row + 16, lane : lane + HALF]
-            pos = part[32:48, HALF : HALF + LANES]
-            pos_ref[32 * e : 32 * e + 16, :] = pos[:, :FEAT]
-            pos_ref[32 * e + 16 : 32 * e + 32, :] = pos[:, FEAT:]
-            filt_ref[32 * e : 32 * e + 32, :] = part[48:80, :]
-            stat_ref = (rates_ref, skip_ref)[e]
+                conv_ref[i, :, lanes] = part[row : row + 16, lane : lane + HALF]
+            conv_ref[KERNEL - 1, :8, lanes] = part[32:40, :HALF]
+            conv_ref[KERNEL - 1, 8:, lanes] = part[32:40, HALF:]
+            filt_ref[32 * e : 32 * e + 32, :] = part[40:72, :]
+            for j in range(2):
+                pos = part[72:80, j * LANES : (j + 1) * LANES]
+                pos_ref[32 * e + 8 * j : 32 * e + 8 * j + 8, :] = pos[:, :FEAT]
+                pos_ref[32 * e + 16 + 8 * j : 32 * e + 24 + 8 * j, :] = pos[:, FEAT:]
             for j in range(4):
-                stat_ref[:, j * LANES : (j + 1) * LANES] = part[32 + j : 33 + j, HALF + LANES :]
-
-    @pl.when(core_ref[0] == 0)
+                (rates_ref, skip_ref)[e][:, j * LANES : (j + 1) * LANES] = part[72 + j : 73 + j, HALF : HALF + LANES]
+
+    @pl.when(core == 0)
     def _():
         write(mine_ref, other_ref)
 
-    @pl.when(core_ref[0] == 1)
+    @pl.when(core == 1)
     def _():
         write(other_ref, mine_ref)
 
 
 VMEM = pl.BlockSpec(memory_space=pltpu.VMEM)
-SMEM = pl.BlockSpec(memory_space=pltpu.SMEM)
-ANY = pl.BlockSpec(memory_space=pl.ANY)
+HBM = pl.BlockSpec(memory_space=pltpu.HBM)
 
 
 def call(kernel, out_shape, args, scratch=(), flops=0, name=None, specs=None, out_specs=None, limit=60):
@@ -481,7 +502,6 @@
 
 
 def on_device(inputs, cotangent, w_pos, w_filt, log_rates, skip_gain, w_conv):
-    core = lax.axis_index("batch") % 2
     swap = [(i, i ^ 1) for i in range(lax.axis_size("batch"))]
     signal, upstream = inputs[0], cotangent[0]
     w_taps = jnp.transpose(w_conv, (1, 0, 2))
@@ -496,16 +516,16 @@
             pltpu.VMEM((ROWS, WIDTH), BF16),
             pltpu.VMEM((ROWS, WIDTH), BF16),
             pltpu.VMEM((KERNEL, WIDTH, WIDTH), BF16),
-            pltpu.VMEM((HALO + ROWS + 8, WIDTH), F32),
-            pltpu.VMEM((WIDTH, SPAN), F32),
+            pltpu.VMEM((EDGE + ROWS + 8, WIDTH), F32),
+            pltpu.VMEM((SPAN, WIDTH), F32),
             pltpu.VMEM((WIDTH, ROWS), BF16),
             pltpu.VMEM((WIDTH, SPAN), BF16),
             pltpu.SemaphoreType.DMA((4 + KERNEL,)),
         ],
-        flops=2 * KERNEL * WIDTH * WIDTH * SPAN,
+        flops=2 * KERNEL * WIDTH * WIDTH * (ROWS + EDGE),
         name="prep",
-        specs=[ANY] * 3,
-        out_specs=ANY,
+        specs=[HBM] * 3,
+        out_specs=HBM,
     )
     received = regroup(message.reshape(SHARDS, OWN, ROWS + SPAN))
     cot_peer = lax.ppermute(upstream, "batch", swap)
@@ -525,66 +545,61 @@
             shape((OWN, LANES)),
         ],
         (w_pos, w_filt, log_rates[None], skip_gain[None], feat, *tabs),
-        [*saved, stack, wide, wide, pltpu.SemaphoreType.DMA((3,))],
+        [*saved, pltpu.VMEM((STACK, 2 * LANES), F32), pltpu.VMEM((OWN, LANES), F32), stack, wide, wide, pltpu.SemaphoreType.DMA((5,))],
         flops=flops * 2,
         name="taps",
-        out_specs=[ANY, ANY, ANY, VMEM, VMEM],
-    )
-    act_message, grad_before, sig_spec, skip_part = call(
+        out_specs=[HBM] * 5,
+    )
+    act_message, before, sig_spec = call(
         forward_kernel,
-        [
-            shape((SHARDS, OWN, SPAN), BF16),
-            shape((STACK, LANES)),
-            shape((STACK, 2 * LANES)),
-            shape((OWN, LANES)),
-        ],
+        [shape((SHARDS, OWN, SPAN), BF16), shape((STACK, LANES)), shape((STACK, 2 * LANES))],
         (received, tap_spec, par, *tabs),
         [
             pltpu.VMEM((SHARDS, OWN, ROWS), BF16),
-            pltpu.VMEM((SHARDS, OWN, SPAN), BF16),
             pltpu.VMEM((STACK, 2 * LANES), F32),
             pltpu.VMEM((STACK, 2 * LANES), F32),
             pltpu.VMEM((SHARDS, OWN, SPAN), BF16),
-            stack,
             *[pltpu.VMEM(t.shape, t.dtype) for t in tabs],
             stack,
             stack,
             wide,
             wide,
             pltpu.VMEM((OWN, LANES), F32),
-            pltpu.SemaphoreType.DMA((15,)),
+            pltpu.SemaphoreType.DMA((14,)),
         ],
         flops=flops * 2,
         name="forward",
-        specs=[ANY] * 11,
-        out_specs=[ANY, ANY, ANY, VMEM],
+        specs=[HBM] * 11,
+        out_specs=[HBM] * 3,
     )
     act = regroup(act_message).reshape(WIDTH, SPAN)
     ig_message, small = call(
         backward_kernel,
         [shape((SHARDS, OWN, ROWS), BF16), shape((2, 2 * OWN, LANES))],
-        (grad_before, sig_spec, tap_spec, par, skip_part, hidden, cosines, feat, taps, *tabs),
+        (received, before, sig_spec, tap_spec, par, hidden, cosines, feat, taps, *tabs),
         [
+            pltpu.VMEM((SHARDS, OWN, ROWS + SPAN), BF16),
             stack,
             pltpu.VMEM((STACK, 2 * LANES), F32),
             pltpu.VMEM((STACK, 2 * LANES), F32),
-            pltpu.VMEM((OWN, LANES), F32),
             pltpu.VMEM((OWN, LANES), F32),
             *saved[:2],
             saved[0],
             saved[2],
             *[pltpu.VMEM(t.shape, t.dtype) for t in tabs],
+            stack,
             pltpu.VMEM((SHARDS, OWN, ROWS), BF16),
+            pltpu.VMEM((2, 2 * OWN, LANES), F32),
             stack,
             wide,
             wide,
             pltpu.VMEM((OWN, LENGTH), F32),
-            pltpu.SemaphoreType.DMA((18,)),
+            pltpu.SemaphoreType.DMA((19,)),
         ],
         flops=flops * 4,
         name="backward",
-        specs=[ANY] * 17,
-        out_specs=[ANY, VMEM],
+        specs=[HBM] * 17,
+        out_specs=[HBM] * 2,
     )
     act, ig_message, small = lax.optimization_barrier((act, ig_message, small))
     act_peer = lax.ppermute(act, "batch", swap)
@@ -602,46 +617,47 @@
             pltpu.VMEM((2, HALO + ROWS + 8, HALF), F32),
             pltpu.VMEM((KERNEL, WIDTH, HALF), BF16),
             pltpu.VMEM((WIDTH, ROWS + 2 * LANES), BF16),
-            pltpu.SemaphoreType.DMA((8 + KERNEL,)),
+            pltpu.SemaphoreType.DMA((10 + KERNEL,)),
         ],
-        flops=2 * KERNEL * WIDTH * HALF * 2 * SPAN,
+        flops=2 * KERNEL * WIDTH * HALF * 2 * ROWS,
         name="conv_grad",
-        specs=[ANY] * 7,
-        out_specs=ANY,
+        specs=[HBM] * 7,
+        out_specs=HBM,
     )
     spread = regroup(sums.reshape(SHARDS, OWN, lanes))
     mixed = call(
         mixed_kernel,
         shape((ROWS, WIDTH), BF16),
         (act, w_taps, sums),
-        [pltpu.VMEM((ROWS + 16, WIDTH), F32)],
-        flops=2 * KERNEL * WIDTH * WIDTH * (ROWS + 16),
+        [
+            pltpu.VMEM((WIDTH, SPAN), BF16),
+            pltpu.VMEM((KERNEL, WIDTH, WIDTH), BF16),
+            pltpu.VMEM((ROWS + EDGE, WIDTH), F32),
+            pltpu.VMEM((ROWS, WIDTH), BF16),
+            pltpu.SemaphoreType.DMA((2 + KERNEL,)),
+        ],
+        flops=2 * KERNEL * WIDTH * WIDTH * (ROWS + EDGE),
         name="mixed",
-        specs=[VMEM, VMEM, ANY],
-        limit=16,
-    )
-    payload = call(
-        gather_kernel,
-        shape((4, 80, WIDTH), BF16),
-        (spread, mixed),
-        [pltpu.VMEM((80, WIDTH), BF16), pltpu.SemaphoreType.DMA((4,))],
-        name="gather",
-        specs=[VMEM, ANY],
-        out_specs=ANY,
+        specs=[HBM] * 3,
+        out_specs=HBM,
+    )
+    spread, mixed = lax.optimization_barrier((spread, mixed))
+    payload = call(gather_kernel, shape((80, WIDTH), BF16), (spread,), name="gather", limit=12)
+    rounds = [[(i, (i + 2 * d) % 8) for i in range(8)] for d in range(1, 4)]
+    others = [lax.ppermute(payload, "batch", route) for route in rounds]
+    spread, payload = lax.optimization_barrier((spread, payload))
+    input_grad = call(
+        input_kernel,
+        shape((ROWS, WIDTH), BF16),
+        (spread,),
+        [pltpu.VMEM((ROWS, WIDTH), BF16), pltpu.SemaphoreType.DMA],
+        name="input",
+        out_specs=HBM,
         limit=12,
     )
-    input_grad = call(input_kernel, shape((ROWS, WIDTH), BF16), (spread, payload), name="input", specs=[VMEM, ANY], limit=12)
-    groups = [[2 * z + e for z in range(4)] for e in range(2)]
-    parts = lax.all_to_all(
-        payload,
-        "batch",
-        split_axis=0,
-        concat_axis=0,
-        tiled=True,
-        axis_index_groups=groups,
-    )
-    total = call(final_kernel, shape((80, WIDTH)), (parts, input_grad), name="final", specs=[VMEM, ANY], limit=12)
-    other = lax.ppermute(total, "batch", swap)
+    payload, input_grad = lax.optimization_barrier((payload, input_grad))
+    mine = call(final_kernel, shape((80, WIDTH)), (payload, *others), name="final", limit=12)
+    other = lax.ppermute(mine, "batch", swap)
     conv_grad, pos_grad, filt_grad, rates_grad, skip_grad = call(
         join_kernel,
         [
@@ -651,9 +667,8 @@
             shape((1, WIDTH)),
             shape((1, WIDTH)),
         ],
-        (core.astype(jnp.int32)[None], total, other),
+        (mine, other),
         name="join",
-        specs=[SMEM, VMEM, VMEM],
         limit=12,
     )
     return (

time: 114 us -> 107 us (0.939)
  local copies, waits for them, and re-layouts: 6.76 us -> 1.62 us
  waiting for transfers between devices: 32.7 us -> 29 us
    all_to_all x1 -> x0, waiting for transfers between devices: 8.65 us -> none  [on_device(): lax.all_to_all(payload, 'batch', split_axis=0, concat_axis=0, tiled=True,...]
    ppermute x1 -> x4, starting transfers between devices: 4.01 us -> 12.5 us  [the longest x3 8.44 us: on_device(): others = [lax.ppermute(payload, 'batch', route) for route in rounds]]
    all_to_all x1 -> x0, starting transfers between devices: 7.29 us -> none  [on_device(): lax.all_to_all(payload, 'batch', split_axis=0, concat_axis=0, tiled=True,...]
    unnamed x22 -> x12, local copies, waits for them, and re-layouts: 6.76 us -> 1.62 us
    ppermute x1 -> x4, waiting for transfers between devices: 1.03 us -> 5 us  [the longest x3 3.97 us: on_device(): others = [lax.ppermute(payload, 'batch', route) for route in rounds]]
  transfers between devices with their start and end apart: 8 -> 10, of which waited for: 6 -> 6; matrix products, arithmetic and copies ran while one was open for 0% -> 0% of each run, Pallas kernels for 18% -> 22%
where the time goes in v3:
time: 107 us; the launch traced here: 106 us
  starting transfers between devices  37.7 us (35%)
  Pallas kernels  37.2 us (35%)
  waiting for transfers between devices  29 us (27%)
  local copies, waits for them, and re-layouts  1.62 us (2%)
    pallas_call x10, Pallas kernels, call(): pl.pallas_call(kernel, out_shape=out_shape, in_specs=specs or [VMEM] * le...  37.2 us
    all_to_all x3, starting transfers between devices, regroup(): return lax.all_to_all(blocks, 'tm', split_axis=0, concat_axis=0, tiled=True)  22.9 us
    all_to_all x3, waiting for transfers between devices, regroup(): return lax.all_to_all(blocks, 'tm', split_axis=0, concat_axis=0, tiled=True)  22.6 us
    ppermute x3, starting transfers between devices, on_device(): others = [lax.ppermute(payload, 'batch', route) for route in rounds]  8.44 us
    ppermute x1, starting transfers between devices, on_device(): other = lax.ppermute(mine, 'batch', swap)  4.05 us
    ppermute x3, waiting for transfers between devices, on_device(): others = [lax.ppermute(payload, 'batch', route) for route in rounds]  3.97 us
  transfers between devices with their start and end apart: 10, of which 6 were waited for; matrix products, arithmetic and copies ran while one was open for 0% of the time, Pallas kernels for 22%

profile of v3, /device:TPU:1, one launch (start us, length us, event | category | flops | bytes accessed | tf_op | source)
XLA Modules:
  0.0 106.4 jit_solution(5990947678003881071)
XLA Ops:
  0.6 0.0 copy-start.2
  0.6 3.6 %prep.1 = bf16[512,640]{1,0:T(8,128)(2,1)} custom-call(bf16[256,512]{1,0:T(8,128)(2,1)} %bitcast.27, bf16[256,512]{1,0:T(8,128)(2,1)} %bitcast.21, bf16[5,512,512]{2,1,0:T(8,128)(2,1)} %bitcast.15), custom_call_target="tpu_custom_call" | custom-call | flops 713031680 | bytes 3801088 | tf_op jit(solution)/shard_map/prep/pallas_call | solution.py:484
  4.2 9.2 %all-to-all-start = ((bf16[32,16,640]{2,1,0:T(8,128)(2,1)}), bf16[32,16,640]{2,1,0:T(8,128)(2,1)S(1)}, u32[]{:S(2)}, u32[]{:S(2)}) async-start(bf16[32,16,640]{2,1,0:T(8,128)(2,1)} %bitcast.20), calls=%async_computation | async-start | bytes 1310720 | tf_op jit(solution)/shard_map/all_to_all | solution.py:501
  13.5 0.0 copy-done.2
  13.5 1.0 collective-permute-start
  14.5 8.2 %taps.1 = (bf16[128,8192]{1,0:T(8,128)(2,1)}, f32[64,8192]{1,0:T(8,128)}, f32[16,8192]{1,0:T(8,128)}, f32[1024,256]{1,0:T(8,128)}, f32[16,128]{1,0:T(8,128)}) custom-call(f32[64,64]{1,0:T(8,128)} %wp_ref.1, f32[64,512]{1,0:T(8,128)} %wf_ref.1, f32[1,512]{1,0:T(1,128)} %bitcast.29, f32[1,512]{1,0:T(1,128)} %bitcast.30, ...), custom_call_target="tpu_custom_call" | custom-call | flops 1207959552 | bytes 8695808 | tf_op jit(solution)/shard_map/taps/pallas_call | solution.py:484
  22.7 0.0 collective-permute-done.peer_cot_hbm
  22.7 0.0 copy-start.4
  22.7 1.9 %all-to-all-done.recv_hbm.rest_0_ = bf16[32,16,640]{2,1,0:T(8,128)(2,1)S(1)} async-done(((bf16[32,16,640]{2,1,0:T(8,128)(2,1)}), bf16[32,16,640]{2,1,0:T(8,128)(2,1)S(1)}, u32[]{:S(2)}, u32[]{:S(2)}) %all-to-all-start) | async-done | bytes 655392 | tf_op jit(solution)/shard_map/all_to_all | solution.py:501
  24.7 0.0 copy-start.1
  24.7 0.9 copy-done.1
  25.5 5.2 %forward.1 = (bf16[32,16,384]{2,1,0:T(8,128)(2,1)}, f32[1024,128]{1,0:T(8,128)}, f32[1024,256]{1,0:T(8,128)}) custom-call(bf16[32,16,640]{2,1,0:T(8,128)(2,1)} %copy-done.1, f32[1024,256]{1,0:T(8,128)} %get-tuple-element.34.tspec_hbm.rest_3_, f32[16,128]{1,0:T(8,128)} %get-tuple-element.35.par_hbm.rest_4_, bf16[128,128]{1,0:T(8,128)(2,1)} %constant.18.clone.rest_0_.rest_9_, ...), custom_call_target="tpu_custom_call" | custom-call | flops 1207959552 | bytes 4349952 | tf_op jit(solution)/shard_map/forward/pallas_call | solution.py:484
  30.8 6.3 %all-to-all-start.1 = ((bf16[32,16,384]{2,1,0:T(8,128)(2,1)}), bf16[32,16,384]{2,1,0:T(8,128)(2,1)S(1)}, u32[]{:S(2)}, u32[]{:S(2)}) async-start(bf16[32,16,384]{2,1,0:T(8,128)(2,1)} %get-tuple-element.36), calls=%async_computation.1 | async-start | bytes 786432 | tf_op jit(solution)/shard_map/all_to_all | solution.py:501
  37.1 9.8 %backward.1 = (bf16[32,16,256]{2,1,0:T(8,128)(2,1)}, f32[2,32,128]{2,1,0:T(8,128)}) custom-call(bf16[32,16,640]{2,1,0:T(8,128)(2,1)} %copy-done.1, f32[1024,128]{1,0:T(8,128)} %get-tuple-element.37.rest_1_, f32[1024,256]{1,0:T(8,128)} %get-tuple-element.38.rest_2_, f32[1024,256]{1,0:T(8,128)} %get-tuple-element.34.tspec_hbm.rest_3_, ...), custom_call_target="tpu_custom_call" | custom-call | flops 2415919104 | bytes 11067392 | tf_op jit(solution)/shard_map/backward/pallas_call | solution.py:484
  46.9 0.0 copy-done.4
  46.9 0.0 all-to-all-done.1
  46.9 0.0 copy-start
  46.9 1.2 %collective-permute-start.1 = (bf16[512,384]{1,0:T(8,128)(2,1)S(1)}, bf16[512,384]{1,0:T(8,128)(2,1)S(1)}, u32[]{:S(2)}, u32[]{:S(2)}) collective-permute-start(bf16[512,384]{1,0:T(8,128)(2,1)S(1)} %bitcast.17), channel_id=1, source_target_pairs={{0,1},{1,0},{2,3},{3,2},{4,5},{5,4},{6,7},{7,6},{8,9},{9,8},{10,11... | collective-permute-start | bytes 1179656 | tf_op jit(solution)/shard_map/ppermute | solution.py:605
  48.2 0.0 collective-permute-start.2
  48.2 1.5 %collective-permute-done.2.peer_small_hbm = f32[2,32,128]{2,1,0:T(8,128)S(1)} collective-permute-done((f32[2,32,128]{2,1,0:T(8,128)}, f32[2,32,128]{2,1,0:T(8,128)S(1)}, u32[]{:S(2)}, u32[]{:S(2)}) %collective-permute-start.2) | collective-permute-done | bytes 32800 | tf_op jit(solution)/shard_map/ppermute | solution.py:606
  49.6 0.0 copy-start.5
  49.6 0.0 collective-permute-done.1.peer_act_hbm
  49.6 0.0 copy-start.3
  49.6 0.0 copy-done
  49.6 0.6 copy-done.5
  50.2 0.1 copy-done.3
  50.4 4.1 %conv_grad.1._ = bf16[512,1792]{1,0:T(8,128)(2,1)} custom-call(bf16[512,384]{1,0:T(8,128)(2,1)} %bitcast.18, bf16[512,384]{1,0:T(8,128)(2,1)} %copy-done.3, bf16[256,512]{1,0:T(8,128)(2,1)} %bitcast.22, bf16[256,512]{1,0:T(8,128)(2,1)} %copy-done.4, bf16[512,256]{1,0:T(8,128)(2,1)} %bitcast.25, f32[2,32,128]{2,1,0:T(8,128)} %get-tuple-element.47.small_hbm, ...), custom_call_target="tpu_custom_call" | custom-call | flops 671088640 | bytes 3473408 | tf_op jit(solution)/shard_map/conv_grad/pallas_call | solution.py:484
  54.5 7.3 %all-to-all-start.2 = ((bf16[32,16,1792]{2,1,0:T(8,128)(2,1)}), bf16[32,16,1792]{2,1,0:T(8,128)(2,1)S(1)}, u32[]{:S(2)}, u32[]{:S(2)}) async-start(bf16[32,16,1792]{2,1,0:T(8,128)(2,1)} %bitcast.14), calls=%async_computation.2 | async-start | bytes 3670016 | tf_op jit(solution)/shard_map/all_to_all | solution.py:501
  61.9 4.3 %mixed.1 = bf16[256,512]{1,0:T(8,128)(2,1)} custom-call(bf16[512,384]{1,0:T(8,128)(2,1)} %bitcast.19, bf16[5,512,512]{2,1,0:T(8,128)(2,1)} %bitcast.16, bf16[512,1792]{1,0:T(8,128)(2,1)} %conv_grad.1._), custom_call_target="tpu_custom_call" | custom-call | flops 713031680 | bytes 5111808 | tf_op jit(solution)/shard_map/mixed/pallas_call | solution.py:484
  66.2 20.6 %all-to-all-done.2.recv_ref = bf16[32,16,1792]{2,1,0:T(8,128)(2,1)S(1)} async-done(((bf16[32,16,1792]{2,1,0:T(8,128)(2,1)}), bf16[32,16,1792]{2,1,0:T(8,128)(2,1)S(1)}, u32[]{:S(2)}, u32[]{:S(2)}) %all-to-all-start.2) | async-done | bytes 1835040 | tf_op jit(solution)/shard_map/all_to_all | solution.py:501
  86.8 0.3 gather.1.own_ref
  87.2 5.2 %collective-permute-start.5 = (bf16[80,512]{1,0:T(8,128)(2,1)S(1)}, bf16[80,512]{1,0:T(8,128)(2,1)S(1)}, u32[]{:S(2)}, u32[]{:S(2)}) collective-permute-start(bf16[80,512]{1,0:T(8,128)(2,1)S(1)} %gather.1.own_ref), channel_id=1, source_target_pairs={{0,6},{1,7},{2,0},{3,1},{4,2},{5,3},{6,4},{7,5},{8,14},{9,15},{10,... | collective-permute-start | bytes 245768 | tf_op jit(solution)/shard_map/ppermute | solution.py:647
  92.4 1.2 %collective-permute-start.4 = (bf16[80,512]{1,0:T(8,128)(2,1)S(1)}, bf16[80,512]{1,0:T(8,128)(2,1)S(1)}, u32[]{:S(2)}, u32[]{:S(2)}) collective-permute-start(bf16[80,512]{1,0:T(8,128)(2,1)S(1)} %gather.1.own_ref), channel_id=1, source_target_pairs={{0,4},{1,5},{2,6},{3,7},{4,0},{5,1},{6,2},{7,3},{8,12},{9,13},{10,... | collective-permute-start | bytes 245768 | tf_op jit(solution)/shard_map/ppermute | solution.py:647
  93.5 2.1 %collective-permute-start.3 = (bf16[80,512]{1,0:T(8,128)(2,1)S(1)}, bf16[80,512]{1,0:T(8,128)(2,1)S(1)}, u32[]{:S(2)}, u32[]{:S(2)}) collective-permute-start(bf16[80,512]{1,0:T(8,128)(2,1)S(1)} %gather.1.own_ref), channel_id=1, source_target_pairs={{0,2},{1,3},{2,4},{3,5},{4,6},{5,7},{6,0},{7,1},{8,10},{9,11},{10,... | collective-permute-start | bytes 245768 | tf_op jit(solution)/shard_map/ppermute | solution.py:647
  95.6 0.8 input.1
  96.5 0.0 collective-permute-done.5.third_ref
  96.5 3.1 %collective-permute-done.4.second_ref = bf16[80,512]{1,0:T(8,128)(2,1)S(1)} collective-permute-done((bf16[80,512]{1,0:T(8,128)(2,1)S(1)}, bf16[80,512]{1,0:T(8,128)(2,1)S(1)}, u32[]{:S(2)}, u32[]{:S(2)}) %collective-permute-start.4) | collective-permute-done | bytes 81952 | tf_op jit(solution)/shard_map/ppermute | solution.py:647
  99.6 0.9 collective-permute-done.3.first_ref
  100.5 4.0 %collective-permute-start.6 = (f32[80,512]{1,0:T(8,128)S(1)}, f32[80,512]{1,0:T(8,128)S(1)}, u32[]{:S(2)}, u32[]{:S(2)}) collective-permute-start(f32[80,512]{1,0:T(8,128)S(1)} %final.1.mine_ref), channel_id=1, source_target_pairs={{0,1},{1,0},{2,3},{3,2},{4,5},{5,4},{6,7},{7,6},{8,9},{9,8},{10,11... | collective-permute-start | bytes 491528 | tf_op jit(solution)/shard_map/ppermute | solution.py:660
  104.5 1.0 collective-permute-done.6.other_ref
  105.6 0.8 join.1
  (1 shorter events, 0.0 us)
Async XLA Ops:
  0.6 12.8 %copy-start.2 = (bf16[1,256,512]{2,1,0:T(8,128)(2,1)S(1)}, bf16[1,256,512]{2,1,0:T(8,128)(2,1)}, u32[]{:S(2)}) copy-start(bf16[1,256,512]{2,1,0:T(8,128)(2,1)} %param.17) | copy-start | bytes 786436
  4.2 20.5 %all-to-all-start = ((bf16[32,16,640]{2,1,0:T(8,128)(2,1)}), bf16[32,16,640]{2,1,0:T(8,128)(2,1)S(1)}, u32[]{:S(2)}, u32[]{:S(2)}) async-start(bf16[32,16,640]{2,1,0:T(8,128)(2,1)} %bitcast.20), calls=%async_computation | async-start | bytes 1310720 | tf_op jit(solution)/shard_map/all_to_all | solution.py:501
  13.5 9.2 %collective-permute-start = (bf16[256,512]{1,0:T(8,128)(2,1)S(1)}, bf16[256,512]{1,0:T(8,128)(2,1)S(1)}, u32[]{:S(2)}, u32[]{:S(2)}) collective-permute-start(bf16[256,512]{1,0:T(8,128)(2,1)S(1)} %bitcast.23), channel_id=1, source_target_pairs={{0,1},{1,0},{2,3},{3,2},{4,5},{5,4},{6,7},{7,6},{8,9},{9,8},{10,11... | collective-permute-start | bytes 786440 | tf_op jit(solution)/shard_map/ppermute | solution.py:531
  22.7 24.1 %copy-start.4 = (bf16[256,512]{1,0:T(8,128)(2,1)}, bf16[256,512]{1,0:T(8,128)(2,1)S(1)}, u32[]{:S(2)}) copy-start(bf16[256,512]{1,0:T(8,128)(2,1)S(1)} %collective-permute-done.peer_cot_hbm) | copy-start | bytes 786436
  24.7 0.9 copy-start.1
  30.8 16.1 %all-to-all-start.1 = ((bf16[32,16,384]{2,1,0:T(8,128)(2,1)}), bf16[32,16,384]{2,1,0:T(8,128)(2,1)S(1)}, u32[]{:S(2)}, u32[]{:S(2)}) async-start(bf16[32,16,384]{2,1,0:T(8,128)(2,1)} %get-tuple-element.36), calls=%async_computation.1 | async-start | bytes 786432 | tf_op jit(solution)/shard_map/all_to_all | solution.py:501
  46.9 2.7 %copy-start = (bf16[32,16,384]{2,1,0:T(8,128)(2,1)}, bf16[32,16,384]{2,1,0:T(8,128)(2,1)S(1)}, u32[]{:S(2)}) copy-start(bf16[32,16,384]{2,1,0:T(8,128)(2,1)S(1)} %all-to-all-done.1) | copy-start | bytes 1179652
  46.9 2.7 %collective-permute-start.1 = (bf16[512,384]{1,0:T(8,128)(2,1)S(1)}, bf16[512,384]{1,0:T(8,128)(2,1)S(1)}, u32[]{:S(2)}, u32[]{:S(2)}) collective-permute-start(bf16[512,384]{1,0:T(8,128)(2,1)S(1)} %bitcast.17), channel_id=1, source_target_pairs={{0,1},{1,0},{2,3},{3,2},{4,5},{5,4},{6,7},{7,6},{8,9},{9,8},{10,11... | collective-permute-start | bytes 1179656 | tf_op jit(solution)/shard_map/ppermute | solution.py:605
  48.2 1.5 %collective-permute-start.2 = (f32[2,32,128]{2,1,0:T(8,128)}, f32[2,32,128]{2,1,0:T(8,128)S(1)}, u32[]{:S(2)}, u32[]{:S(2)}) collective-permute-start(f32[2,32,128]{2,1,0:T(8,128)} %get-tuple-element.47.small_hbm), channel_id=1, source_target_pairs={{0,1},{1,0},{2,3},{3,2},{4,5},{5,4},{6,7},{7,6},{8,9},{9,8},{10,11... | collective-permute-start | bytes 98312 | tf_op jit(solution)/shard_map/ppermute | solution.py:606
  49.6 0.6 copy-start.5
  49.6 0.8 copy-start.3
  54.5 32.3 %all-to-all-start.2 = ((bf16[32,16,1792]{2,1,0:T(8,128)(2,1)}), bf16[32,16,1792]{2,1,0:T(8,128)(2,1)S(1)}, u32[]{:S(2)}, u32[]{:S(2)}) async-start(bf16[32,16,1792]{2,1,0:T(8,128)(2,1)} %bitcast.14), calls=%async_computation.2 | async-start | bytes 3670016 | tf_op jit(solution)/shard_map/all_to_all | solution.py:501
  87.2 9.3 %collective-permute-start.5 = (bf16[80,512]{1,0:T(8,128)(2,1)S(1)}, bf16[80,512]{1,0:T(8,128)(2,1)S(1)}, u32[]{:S(2)}, u32[]{:S(2)}) collective-permute-start(bf16[80,512]{1,0:T(8,128)(2,1)S(1)} %gather.1.own_ref), channel_id=1, source_target_pairs={{0,6},{1,7},{2,0},{3,1},{4,2},{5,3},{6,4},{7,5},{8,14},{9,15},{10,... | collective-permute-start | bytes 245768 | tf_op jit(solution)/shard_map/ppermute | solution.py:647
  92.4 7.2 %collective-permute-start.4 = (bf16[80,512]{1,0:T(8,128)(2,1)S(1)}, bf16[80,512]{1,0:T(8,128)(2,1)S(1)}, u32[]{:S(2)}, u32[]{:S(2)}) collective-permute-start(bf16[80,512]{1,0:T(8,128)(2,1)S(1)} %gather.1.own_ref), channel_id=1, source_target_pairs={{0,4},{1,5},{2,6},{3,7},{4,0},{5,1},{6,2},{7,3},{8,12},{9,13},{10,... | collective-permute-start | bytes 245768 | tf_op jit(solution)/shard_map/ppermute | solution.py:647
  93.5 6.9 %collective-permute-start.3 = (bf16[80,512]{1,0:T(8,128)(2,1)S(1)}, bf16[80,512]{1,0:T(8,128)(2,1)S(1)}, u32[]{:S(2)}, u32[]{:S(2)}) collective-permute-start(bf16[80,512]{1,0:T(8,128)(2,1)S(1)} %gather.1.own_ref), channel_id=1, source_target_pairs={{0,2},{1,3},{2,4},{3,5},{4,6},{5,7},{6,0},{7,1},{8,10},{9,11},{10,... | collective-permute-start | bytes 245768 | tf_op jit(solution)/shard_map/ppermute | solution.py:647
  100.5 5.1 %collective-permute-start.6 = (f32[80,512]{1,0:T(8,128)S(1)}, f32[80,512]{1,0:T(8,128)S(1)}, u32[]{:S(2)}, u32[]{:S(2)}) collective-permute-start(f32[80,512]{1,0:T(8,128)S(1)} %final.1.mine_ref), channel_id=1, source_target_pairs={{0,1},{1,0},{2,3},{3,2},{4,5},{5,4},{6,7},{7,6},{8,9},{9,8},{10,11... | collective-permute-start | bytes 491528 | tf_op jit(solution)/shard_map/ppermute | solution.py:660

commit v4 on v3

--- a/solution.py
+++ b/solution.py
@@ -432,10 +432,12 @@
     out_ref[...] = jnp.concatenate([*blocks, filt[:32], last], axis=0).astype(BF16)
 
 
-def final_kernel(own_ref, first_ref, second_ref, third_ref, out_ref):
-    across = own_ref[...].astype(F32) + second_ref[...].astype(F32)
-    beside = first_ref[...].astype(F32) + third_ref[...].astype(F32)
-    out_ref[...] = (across + beside) * SCALE
+def pair_kernel(own_ref, other_ref, out_ref):
+    out_ref[...] = (own_ref[...].astype(F32) + other_ref[...].astype(F32)).astype(BF16)
+
+
+def final_kernel(own_ref, other_ref, out_ref):
+    out_ref[...] = (own_ref[...].astype(F32) + other_ref[...].astype(F32)) * SCALE
 
 
 def input_kernel(recv_ref, out_hbm, out_ref, sem):
@@ -643,9 +645,10 @@
     )
     spread, mixed = lax.optimization_barrier((spread, mixed))
     payload = call(gather_kernel, shape((80, WIDTH), BF16), (spread,), name="gather", limit=12)
-    rounds = [[(i, (i + 2 * d) % 8) for i in range(8)] for d in range(1, 4)]
-    others = [lax.ppermute(payload, "batch", route) for route in rounds]
-    spread, payload = lax.optimization_barrier((spread, payload))
+    met = lax.ppermute(payload, "batch", [(i, i ^ 2) for i in range(8)])
+    pair = call(pair_kernel, shape((80, WIDTH), BF16), (payload, met), name="pair", limit=12)
+    met = lax.ppermute(pair, "batch", [(i, i ^ 6) for i in range(8)])
+    spread, pair = lax.optimization_barrier((spread, pair))
     input_grad = call(
         input_kernel,
         shape((ROWS, WIDTH), BF16),
@@ -655,8 +658,8 @@
         out_specs=HBM,
         limit=12,
     )
-    payload, input_grad = lax.optimization_barrier((payload, input_grad))
-    mine = call(final_kernel, shape((80, WIDTH)), (payload, *others), name="final", limit=12)
+    pair, input_grad = lax.optimization_barrier((pair, input_grad))
+    mine = call(final_kernel, shape((80, WIDTH)), (pair, met), name="final", limit=12)
     other = lax.ppermute(mine, "batch", swap)
     conv_grad, pos_grad, filt_grad, rates_grad, skip_grad = call(
         join_kernel,

time: 107 us -> 105 us (0.981)
  starting transfers between devices: 37.7 us -> 33.9 us
  waiting for transfers between devices: 29 us -> 30.8 us
    ppermute x3 -> x2, starting transfers between devices: 8.44 us -> 5.79 us  [the longest x1 3.08 us: on_device(): met = lax.ppermute(payload, 'batch', [(i, i ^ 2) for i in range(8)])]
    ppermute x3 -> x2, waiting for transfers between devices: 3.97 us -> 5.64 us  [the longest x1 3.71 us: on_device(): met = lax.ppermute(payload, 'batch', [(i, i ^ 2) for i in range(8)])]
    ppermute x1, starting transfers between devices: 4.05 us -> 2.93 us  [on_device(): other = lax.ppermute(mine, 'batch', swap)]
    pallas_call x10 -> x11, Pallas kernels: 37.2 us -> 37.2 us  [call(): pl.pallas_call(kernel, out_shape=out_shape, in_specs=specs or [VMEM] * le...]
  transfers between devices with their start and end apart: 10 -> 9, of which waited for: 6 -> 6; matrix products, arithmetic and copies ran while one was open for 0% -> 0% of each run, Pallas kernels for 22% -> 22%
where the time goes in v4:
time: 105 us; the launch traced here: 104 us
  Pallas kernels  37.2 us (35%)
  starting transfers between devices  33.9 us (32%)
  waiting for transfers between devices  30.8 us (29%)
  local copies, waits for them, and re-layouts  1.62 us (2%)
    pallas_call x11, Pallas kernels, call(): pl.pallas_call(kernel, out_shape=out_shape, in_specs=specs or [VMEM] * le...  37.2 us
    all_to_all x3, starting transfers between devices, regroup(): return lax.all_to_all(blocks, 'tm', split_axis=0, concat_axis=0, tiled=True)  22.9 us
    all_to_all x3, waiting for transfers between devices, regroup(): return lax.all_to_all(blocks, 'tm', split_axis=0, concat_axis=0, tiled=True)  22.6 us
    ppermute x1, waiting for transfers between devices, on_device(): met = lax.ppermute(payload, 'batch', [(i, i ^ 2) for i in range(8)])  3.71 us
    ppermute x1, starting transfers between devices, on_device(): met = lax.ppermute(payload, 'batch', [(i, i ^ 2) for i in range(8)])  3.08 us
    ppermute x1, starting transfers between devices, on_device(): other = lax.ppermute(mine, 'batch', swap)  2.93 us
    ppermute x1, starting transfers between devices, on_device(): met = lax.ppermute(pair, 'batch', [(i, i ^ 6) for i in range(8)])  2.71 us
  transfers between devices with their start and end apart: 9, of which 6 were waited for; matrix products, arithmetic and copies ran while one was open for 0% of the time, Pallas kernels for 22%

profile of v4, /device:TPU:1, one launch (start us, length us, event | category | flops | bytes accessed | tf_op | source)
XLA Modules:
  0.0 104.3 jit_solution(9675628509640547503)
XLA Ops:
  0.6 0.0 copy-start.2
  0.6 3.6 %prep.1 = bf16[512,640]{1,0:T(8,128)(2,1)} custom-call(bf16[256,512]{1,0:T(8,128)(2,1)} %bitcast.27, bf16[256,512]{1,0:T(8,128)(2,1)} %bitcast.21, bf16[5,512,512]{2,1,0:T(8,128)(2,1)} %bitcast.15), custom_call_target="tpu_custom_call" | custom-call | flops 713031680 | bytes 3801088 | tf_op jit(solution)/shard_map/prep/pallas_call | solution.py:486
  4.2 9.2 %all-to-all-start = ((bf16[32,16,640]{2,1,0:T(8,128)(2,1)}), bf16[32,16,640]{2,1,0:T(8,128)(2,1)S(1)}, u32[]{:S(2)}, u32[]{:S(2)}) async-start(bf16[32,16,640]{2,1,0:T(8,128)(2,1)} %bitcast.20), calls=%async_computation | async-start | bytes 1310720 | tf_op jit(solution)/shard_map/all_to_all | solution.py:503
  13.5 0.0 copy-done.2
  13.5 1.0 collective-permute-start
  14.5 8.2 %taps.1 = (bf16[128,8192]{1,0:T(8,128)(2,1)}, f32[64,8192]{1,0:T(8,128)}, f32[16,8192]{1,0:T(8,128)}, f32[1024,256]{1,0:T(8,128)}, f32[16,128]{1,0:T(8,128)}) custom-call(f32[64,64]{1,0:T(8,128)} %wp_ref.1, f32[64,512]{1,0:T(8,128)} %wf_ref.1, f32[1,512]{1,0:T(1,128)} %bitcast.29, f32[1,512]{1,0:T(1,128)} %bitcast.30, ...), custom_call_target="tpu_custom_call" | custom-call | flops 1207959552 | bytes 8695808 | tf_op jit(solution)/shard_map/taps/pallas_call | solution.py:486
  22.7 0.0 collective-permute-done.peer_cot_hbm
  22.7 0.0 copy-start.4
  22.7 1.9 %all-to-all-done.recv_hbm.rest_0_ = bf16[32,16,640]{2,1,0:T(8,128)(2,1)S(1)} async-done(((bf16[32,16,640]{2,1,0:T(8,128)(2,1)}), bf16[32,16,640]{2,1,0:T(8,128)(2,1)S(1)}, u32[]{:S(2)}, u32[]{:S(2)}) %all-to-all-start) | async-done | bytes 655392 | tf_op jit(solution)/shard_map/all_to_all | solution.py:503
  24.7 0.0 copy-start.1
  24.7 0.9 copy-done.1
  25.5 5.2 %forward.1 = (bf16[32,16,384]{2,1,0:T(8,128)(2,1)}, f32[1024,128]{1,0:T(8,128)}, f32[1024,256]{1,0:T(8,128)}) custom-call(bf16[32,16,640]{2,1,0:T(8,128)(2,1)} %copy-done.1, f32[1024,256]{1,0:T(8,128)} %get-tuple-element.34.tspec_hbm.rest_3_, f32[16,128]{1,0:T(8,128)} %get-tuple-element.35.par_hbm.rest_4_, bf16[128,128]{1,0:T(8,128)(2,1)} %constant.18.clone.rest_0_.rest_9_, ...), custom_call_target="tpu_custom_call" | custom-call | flops 1207959552 | bytes 4349952 | tf_op jit(solution)/shard_map/forward/pallas_call | solution.py:486
  30.8 6.3 %all-to-all-start.1 = ((bf16[32,16,384]{2,1,0:T(8,128)(2,1)}), bf16[32,16,384]{2,1,0:T(8,128)(2,1)S(1)}, u32[]{:S(2)}, u32[]{:S(2)}) async-start(bf16[32,16,384]{2,1,0:T(8,128)(2,1)} %get-tuple-element.36), calls=%async_computation.1 | async-start | bytes 786432 | tf_op jit(solution)/shard_map/all_to_all | solution.py:503
  37.1 9.8 %backward.1 = (bf16[32,16,256]{2,1,0:T(8,128)(2,1)}, f32[2,32,128]{2,1,0:T(8,128)}) custom-call(bf16[32,16,640]{2,1,0:T(8,128)(2,1)} %copy-done.1, f32[1024,128]{1,0:T(8,128)} %get-tuple-element.37.rest_1_, f32[1024,256]{1,0:T(8,128)} %get-tuple-element.38.rest_2_, f32[1024,256]{1,0:T(8,128)} %get-tuple-element.34.tspec_hbm.rest_3_, ...), custom_call_target="tpu_custom_call" | custom-call | flops 2415919104 | bytes 11067392 | tf_op jit(solution)/shard_map/backward/pallas_call | solution.py:486
  46.9 0.0 copy-done.4
  46.9 0.0 all-to-all-done.1
  46.9 0.0 copy-start
  46.9 1.2 %collective-permute-start.1 = (bf16[512,384]{1,0:T(8,128)(2,1)S(1)}, bf16[512,384]{1,0:T(8,128)(2,1)S(1)}, u32[]{:S(2)}, u32[]{:S(2)}) collective-permute-start(bf16[512,384]{1,0:T(8,128)(2,1)S(1)} %bitcast.17), channel_id=1, source_target_pairs={{0,1},{1,0},{2,3},{3,2},{4,5},{5,4},{6,7},{7,6},{8,9},{9,8},{10,11... | collective-permute-start | bytes 1179656 | tf_op jit(solution)/shard_map/ppermute | solution.py:607
  48.1 0.0 collective-permute-start.2
  48.1 1.5 %collective-permute-done.2.peer_small_hbm = f32[2,32,128]{2,1,0:T(8,128)S(1)} collective-permute-done((f32[2,32,128]{2,1,0:T(8,128)}, f32[2,32,128]{2,1,0:T(8,128)S(1)}, u32[]{:S(2)}, u32[]{:S(2)}) %collective-permute-start.2) | collective-permute-done | bytes 32800 | tf_op jit(solution)/shard_map/ppermute | solution.py:608
  49.6 0.0 copy-start.5
  49.6 0.0 collective-permute-done.1.peer_act_hbm
  49.6 0.0 copy-start.3
  49.6 0.0 copy-done
  49.6 0.6 copy-done.5
  50.2 0.1 copy-done.3
  50.4 4.1 %conv_grad.1._ = bf16[512,1792]{1,0:T(8,128)(2,1)} custom-call(bf16[512,384]{1,0:T(8,128)(2,1)} %bitcast.18, bf16[512,384]{1,0:T(8,128)(2,1)} %copy-done.3, bf16[256,512]{1,0:T(8,128)(2,1)} %bitcast.22, bf16[256,512]{1,0:T(8,128)(2,1)} %copy-done.4, bf16[512,256]{1,0:T(8,128)(2,1)} %bitcast.25, f32[2,32,128]{2,1,0:T(8,128)} %get-tuple-element.47.small_hbm, ...), custom_call_target="tpu_custom_call" | custom-call | flops 671088640 | bytes 3473408 | tf_op jit(solution)/shard_map/conv_grad/pallas_call | solution.py:486
  54.5 7.4 %all-to-all-start.2 = ((bf16[32,16,1792]{2,1,0:T(8,128)(2,1)}), bf16[32,16,1792]{2,1,0:T(8,128)(2,1)S(1)}, u32[]{:S(2)}, u32[]{:S(2)}) async-start(bf16[32,16,1792]{2,1,0:T(8,128)(2,1)} %bitcast.14), calls=%async_computation.2 | async-start | bytes 3670016 | tf_op jit(solution)/shard_map/all_to_all | solution.py:503
  61.9 4.3 %mixed.1 = bf16[256,512]{1,0:T(8,128)(2,1)} custom-call(bf16[512,384]{1,0:T(8,128)(2,1)} %bitcast.19, bf16[5,512,512]{2,1,0:T(8,128)(2,1)} %bitcast.16, bf16[512,1792]{1,0:T(8,128)(2,1)} %conv_grad.1._), custom_call_target="tpu_custom_call" | custom-call | flops 713031680 | bytes 5111808 | tf_op jit(solution)/shard_map/mixed/pallas_call | solution.py:486
  66.2 20.7 %all-to-all-done.2.recv_ref = bf16[32,16,1792]{2,1,0:T(8,128)(2,1)S(1)} async-done(((bf16[32,16,1792]{2,1,0:T(8,128)(2,1)}), bf16[32,16,1792]{2,1,0:T(8,128)(2,1)S(1)}, u32[]{:S(2)}, u32[]{:S(2)}) %all-to-all-start.2) | async-done | bytes 1835040 | tf_op jit(solution)/shard_map/all_to_all | solution.py:503
  86.9 0.3 gather.1.own_ref
  87.2 3.1 %collective-permute-start.3 = (bf16[80,512]{1,0:T(8,128)(2,1)S(1)}, bf16[80,512]{1,0:T(8,128)(2,1)S(1)}, u32[]{:S(2)}, u32[]{:S(2)}) collective-permute-start(bf16[80,512]{1,0:T(8,128)(2,1)S(1)} %gather.1.own_ref), channel_id=1, source_target_pairs={{0,2},{1,3},{2,0},{3,1},{4,6},{5,7},{6,4},{7,5},{8,10},{9,11},{10,... | collective-permute-start | bytes 245768 | tf_op jit(solution)/shard_map/ppermute | solution.py:648
  90.3 3.7 %collective-permute-done.3.other_ref = bf16[80,512]{1,0:T(8,128)(2,1)S(1)} collective-permute-done((bf16[80,512]{1,0:T(8,128)(2,1)S(1)}, bf16[80,512]{1,0:T(8,128)(2,1)S(1)}, u32[]{:S(2)}, u32[]{:S(2)}) %collective-permute-start.3) | collective-permute-done | bytes 81952 | tf_op jit(solution)/shard_map/ppermute | solution.py:648
  94.0 2.7 %collective-permute-start.4 = (bf16[80,512]{1,0:T(8,128)(2,1)S(1)}, bf16[80,512]{1,0:T(8,128)(2,1)S(1)}, u32[]{:S(2)}, u32[]{:S(2)}) collective-permute-start(bf16[80,512]{1,0:T(8,128)(2,1)S(1)} %pair.1.own_ref), channel_id=1, source_target_pairs={{0,6},{1,7},{2,4},{3,5},{4,2},{5,3},{6,0},{7,1},{8,14},{9,15},{10,... | collective-permute-start | bytes 245768 | tf_op jit(solution)/shard_map/ppermute | solution.py:650
  96.7 0.8 input.1
  97.6 1.9 %collective-permute-done.4.other_ref = bf16[80,512]{1,0:T(8,128)(2,1)S(1)} collective-permute-done((bf16[80,512]{1,0:T(8,128)(2,1)S(1)}, bf16[80,512]{1,0:T(8,128)(2,1)S(1)}, u32[]{:S(2)}, u32[]{:S(2)}) %collective-permute-start.4) | collective-permute-done | bytes 81952 | tf_op jit(solution)/shard_map/ppermute | solution.py:650
  99.6 2.9 %collective-permute-start.5 = (f32[80,512]{1,0:T(8,128)S(1)}, f32[80,512]{1,0:T(8,128)S(1)}, u32[]{:S(2)}, u32[]{:S(2)}) collective-permute-start(f32[80,512]{1,0:T(8,128)S(1)} %final.1.mine_ref), channel_id=1, source_target_pairs={{0,1},{1,0},{2,3},{3,2},{4,5},{5,4},{6,7},{7,6},{8,9},{9,8},{10,11... | collective-permute-start | bytes 491528 | tf_op jit(solution)/shard_map/ppermute | solution.py:663
  102.5 1.0 collective-permute-done.5.other_ref
  103.5 0.8 join.1
  (2 shorter events, 0.0 us)
Async XLA Ops:
  0.6 12.8 %copy-start.2 = (bf16[1,256,512]{2,1,0:T(8,128)(2,1)S(1)}, bf16[1,256,512]{2,1,0:T(8,128)(2,1)}, u32[]{:S(2)}) copy-start(bf16[1,256,512]{2,1,0:T(8,128)(2,1)} %param.17) | copy-start | bytes 786436
  4.2 20.5 %all-to-all-start = ((bf16[32,16,640]{2,1,0:T(8,128)(2,1)}), bf16[32,16,640]{2,1,0:T(8,128)(2,1)S(1)}, u32[]{:S(2)}, u32[]{:S(2)}) async-start(bf16[32,16,640]{2,1,0:T(8,128)(2,1)} %bitcast.20), calls=%async_computation | async-start | bytes 1310720 | tf_op jit(solution)/shard_map/all_to_all | solution.py:503
  13.5 9.2 %collective-permute-start = (bf16[256,512]{1,0:T(8,128)(2,1)S(1)}, bf16[256,512]{1,0:T(8,128)(2,1)S(1)}, u32[]{:S(2)}, u32[]{:S(2)}) collective-permute-start(bf16[256,512]{1,0:T(8,128)(2,1)S(1)} %bitcast.23), channel_id=1, source_target_pairs={{0,1},{1,0},{2,3},{3,2},{4,5},{5,4},{6,7},{7,6},{8,9},{9,8},{10,11... | collective-permute-start | bytes 786440 | tf_op jit(solution)/shard_map/ppermute | solution.py:533
  22.7 24.1 %copy-start.4 = (bf16[256,512]{1,0:T(8,128)(2,1)}, bf16[256,512]{1,0:T(8,128)(2,1)S(1)}, u32[]{:S(2)}) copy-start(bf16[256,512]{1,0:T(8,128)(2,1)S(1)} %collective-permute-done.peer_cot_hbm) | copy-start | bytes 786436
  24.7 0.9 copy-start.1
  30.8 16.1 %all-to-all-start.1 = ((bf16[32,16,384]{2,1,0:T(8,128)(2,1)}), bf16[32,16,384]{2,1,0:T(8,128)(2,1)S(1)}, u32[]{:S(2)}, u32[]{:S(2)}) async-start(bf16[32,16,384]{2,1,0:T(8,128)(2,1)} %get-tuple-element.36), calls=%async_computation.1 | async-start | bytes 786432 | tf_op jit(solution)/shard_map/all_to_all | solution.py:503
  46.9 2.7 %copy-start = (bf16[32,16,384]{2,1,0:T(8,128)(2,1)}, bf16[32,16,384]{2,1,0:T(8,128)(2,1)S(1)}, u32[]{:S(2)}) copy-start(bf16[32,16,384]{2,1,0:T(8,128)(2,1)S(1)} %all-to-all-done.1) | copy-start | bytes 1179652
  46.9 2.7 %collective-permute-start.1 = (bf16[512,384]{1,0:T(8,128)(2,1)S(1)}, bf16[512,384]{1,0:T(8,128)(2,1)S(1)}, u32[]{:S(2)}, u32[]{:S(2)}) collective-permute-start(bf16[512,384]{1,0:T(8,128)(2,1)S(1)} %bitcast.17), channel_id=1, source_target_pairs={{0,1},{1,0},{2,3},{3,2},{4,5},{5,4},{6,7},{7,6},{8,9},{9,8},{10,11... | collective-permute-start | bytes 1179656 | tf_op jit(solution)/shard_map/ppermute | solution.py:607
  48.1 1.5 %collective-permute-start.2 = (f32[2,32,128]{2,1,0:T(8,128)}, f32[2,32,128]{2,1,0:T(8,128)S(1)}, u32[]{:S(2)}, u32[]{:S(2)}) collective-permute-start(f32[2,32,128]{2,1,0:T(8,128)} %get-tuple-element.47.small_hbm), channel_id=1, source_target_pairs={{0,1},{1,0},{2,3},{3,2},{4,5},{5,4},{6,7},{7,6},{8,9},{9,8},{10,11... | collective-permute-start | bytes 98312 | tf_op jit(solution)/shard_map/ppermute | solution.py:608
  49.6 0.6 copy-start.5
  49.6 0.8 copy-start.3
  54.5 32.4 %all-to-all-start.2 = ((bf16[32,16,1792]{2,1,0:T(8,128)(2,1)}), bf16[32,16,1792]{2,1,0:T(8,128)(2,1)S(1)}, u32[]{:S(2)}, u32[]{:S(2)}) async-start(bf16[32,16,1792]{2,1,0:T(8,128)(2,1)} %bitcast.14), calls=%async_computation.2 | async-start | bytes 3670016 | tf_op jit(solution)/shard_map/all_to_all | solution.py:503
  87.2 6.8 %collective-permute-start.3 = (bf16[80,512]{1,0:T(8,128)(2,1)S(1)}, bf16[80,512]{1,0:T(8,128)(2,1)S(1)}, u32[]{:S(2)}, u32[]{:S(2)}) collective-permute-start(bf16[80,512]{1,0:T(8,128)(2,1)S(1)} %gather.1.own_ref), channel_id=1, source_target_pairs={{0,2},{1,3},{2,0},{3,1},{4,6},{5,7},{6,4},{7,5},{8,10},{9,11},{10,... | collective-permute-start | bytes 245768 | tf_op jit(solution)/shard_map/ppermute | solution.py:648
  94.0 5.5 %collective-permute-start.4 = (bf16[80,512]{1,0:T(8,128)(2,1)S(1)}, bf16[80,512]{1,0:T(8,128)(2,1)S(1)}, u32[]{:S(2)}, u32[]{:S(2)}) collective-permute-start(bf16[80,512]{1,0:T(8,128)(2,1)S(1)} %pair.1.own_ref), channel_id=1, source_target_pairs={{0,6},{1,7},{2,4},{3,5},{4,2},{5,3},{6,0},{7,1},{8,14},{9,15},{10,... | collective-permute-start | bytes 245768 | tf_op jit(solution)/shard_map/ppermute | solution.py:650
  99.6 4.0 %collective-permute-start.5 = (f32[80,512]{1,0:T(8,128)S(1)}, f32[80,512]{1,0:T(8,128)S(1)}, u32[]{:S(2)}, u32[]{:S(2)}) collective-permute-start(f32[80,512]{1,0:T(8,128)S(1)} %final.1.mine_ref), channel_id=1, source_target_pairs={{0,1},{1,0},{2,3},{3,2},{4,5},{5,4},{6,7},{7,6},{8,9},{9,8},{10,11... | collective-permute-start | bytes 491528 | tf_op jit(solution)/shard_map/ppermute | solution.py:663

commit v5 on v4

--- a/solution.py
+++ b/solution.py
@@ -27,7 +27,8 @@
 HALF = WIDTH // 2
 EDGE = 16
 CONV = KERNEL * HALF
-BLOCK = 1024
+BLOCK = 4096
+CHUNK = 128
 SCALE = 1.0 / math.sqrt(8 * LENGTH)
 
 
@@ -102,14 +103,17 @@
             high_ref[(c + k) * STEPS : (c + k + 1) * STEPS, :] = high
             low_ref[(c + k) * STEPS : (c + k + 1) * STEPS, :] = low
     wait_for(loads, 4, 5)
-    return mul3((high_ref[...], low_ref[...]), (ahead_high[...], ahead_low[...]))
+    table = (ahead_high[...], ahead_low[...])
+    parts = [mul3((high_ref[r : r + CHUNK, :], low_ref[r : r + CHUNK, :]), table) for r in range(0, STACK, CHUNK)]
+    return jnp.concatenate(parts, axis=0)
 
 
 def from_spectrum(values, stack_ref, tabs, loads=None):
     _, last, tc_ref, ts_ref, _, _, behind_high, behind_low = tabs
     wait_for(loads, 6, 7, 1)
     tc, ts = tc_ref[...], ts_ref[...]
-    q = mul3(split(values), (behind_high[...], behind_low[...]))
+    table = (behind_high[...], behind_low[...])
+    q = jnp.concatenate([mul3(split(values[r : r + CHUNK]), table) for r in range(0, STACK, CHUNK)], axis=0)
     for c in range(0, OWN, 2):
         pair = []
         for k in range(2):
@@ -377,7 +381,11 @@
     for i in range(KERNEL):
         own = pad_ref[0, i : i + SPAN, :].astype(BF16)
         peer = pad_ref[1, i : i + SPAN, :].astype(BF16)
-        part_ref[i] = (mul(act_ref[0], own) + mul(act_ref[1], peer)).astype(BF16)
+        both = jnp.concatenate([own, peer], axis=0)
+        for r in range(0, WIDTH, CHUNK):
+            rows = slice(r, r + CHUNK)
+            wide = jnp.concatenate([act_ref[0, rows, :], act_ref[1, rows, :]], axis=1)
+            part_ref[i, rows, :] = mul(wide, both).astype(BF16)
         copies.append(pltpu.make_async_copy(part_ref.at[i], out_hbm.at[:, pl.ds(i * HALF, HALF)], sems.at[9 + i]))
         copies[-1].start()
         if i == 0:
@@ -418,6 +426,11 @@
     return jnp.concatenate([block[:8], block[8:]], axis=1)
 
 
+def two_parts(rows):
+    high, low = split(rows)
+    return jnp.concatenate([high.astype(F32), low.astype(F32)], axis=0)
+
+
 def gather_kernel(recv_ref, out_ref):
     conv = jnp.sum(recv_ref[:, :, :CONV].astype(F32), axis=0)
     blocks = [conv[:, :WIDTH], conv[:, WIDTH : 2 * WIDTH], fold(conv[:, 2 * WIDTH :])]
@@ -427,13 +440,16 @@
     pos = jnp.sum(recv_ref[:, :, base + LANES : base + 2 * LANES].astype(F32), axis=0)
     stat = filt[32:33]
     pieces = [stat[:, j * LANES : (j + 1) * LANES] for j in range(4)]
-    stat = jnp.concatenate([*pieces, jnp.zeros((4, LANES), F32)], axis=0)
-    last = jnp.concatenate([fold(pos), stat, jnp.zeros((8, LANES), F32)], axis=1)
+    last = jnp.concatenate([fold(pos), two_parts(jnp.concatenate(pieces, axis=0)), jnp.zeros((8, LANES), F32)], axis=1)
     out_ref[...] = jnp.concatenate([*blocks, filt[:32], last], axis=0).astype(BF16)
 
 
 def pair_kernel(own_ref, other_ref, out_ref):
-    out_ref[...] = (own_ref[...].astype(F32) + other_ref[...].astype(F32)).astype(BF16)
+    total = own_ref[...].astype(F32) + other_ref[...].astype(F32)
+    last = total[72:]
+    stat = last[:4, HALF : HALF + LANES] + last[4:, HALF : HALF + LANES]
+    last = jnp.concatenate([last[:, :HALF], two_parts(stat), last[:, HALF + LANES :]], axis=1)
+    out_ref[...] = jnp.concatenate([total[:72], last], axis=0).astype(BF16)
 
 
 def final_kernel(own_ref, other_ref, out_ref):
@@ -464,7 +480,8 @@
                 pos_ref[32 * e + 8 * j : 32 * e + 8 * j + 8, :] = pos[:, :FEAT]
                 pos_ref[32 * e + 16 + 8 * j : 32 * e + 24 + 8 * j, :] = pos[:, FEAT:]
             for j in range(4):
-                (rates_ref, skip_ref)[e][:, j * LANES : (j + 1) * LANES] = part[72 + j : 73 + j, HALF : HALF + LANES]
+                stat = part[72 + j : 73 + j, HALF : HALF + LANES] + part[76 + j : 77 + j, HALF : HALF + LANES]
+                (rates_ref, skip_ref)[e][:, j * LANES : (j + 1) * LANES] = stat
 
     @pl.when(core == 0)
     def _():

time: 105 us -> 102 us (0.971)
  Pallas kernels: 37.2 us -> 33.8 us
  starting transfers between devices: 33.9 us -> 35.4 us
  waiting for transfers between devices: 30.8 us -> 29.5 us
    pallas_call x11, Pallas kernels: 37.2 us -> 33.8 us  [call(): pl.pallas_call(kernel, out_shape=out_shape, in_specs=specs or [VMEM] * le...]
    all_to_all x3, starting transfers between devices: 22.9 us -> 20.9 us  [regroup(): return lax.all_to_all(blocks, 'tm', split_axis=0, concat_axis=0, tiled=True)]
    ppermute x1, waiting for transfers between devices: 3.71 us -> 2.38 us  [on_device(): met = lax.ppermute(payload, 'batch', [(i, i ^ 2) for i in range(8)])]
    ppermute x1, starting transfers between devices: 2.71 us -> 4.04 us  [on_device(): met = lax.ppermute(pair, 'batch', [(i, i ^ 6) for i in range(8)])]
    ppermute x1, starting transfers between devices: 1.25 us -> 2.46 us  [on_device(): act_peer = lax.ppermute(act, 'batch', swap)]
  transfers between devices with their start and end apart: 9 -> 9, of which waited for: 6 -> 7; matrix products, arithmetic and copies ran while one was open for 0% -> 0% of each run, Pallas kernels for 22% -> 21%
where the time goes in v5:
time: 102 us; the launch traced here: 101 us
  starting transfers between devices  35.4 us (35%)
  Pallas kernels  33.8 us (33%)
  waiting for transfers between devices  29.5 us (29%)
  local copies, waits for them, and re-layouts  1.62 us (2%)
    pallas_call x11, Pallas kernels, call(): pl.pallas_call(kernel, out_shape=out_shape, in_specs=specs or [VMEM] * le...  33.8 us
    all_to_all x3, waiting for transfers between devices, regroup(): return lax.all_to_all(blocks, 'tm', split_axis=0, concat_axis=0, tiled=True)  23.5 us
    all_to_all x3, starting transfers between devices, regroup(): return lax.all_to_all(blocks, 'tm', split_axis=0, concat_axis=0, tiled=True)  20.9 us
    ppermute x1, starting transfers between devices, on_device(): met = lax.ppermute(pair, 'batch', [(i, i ^ 6) for i in range(8)])  4.04 us
    ppermute x1, starting transfers between devices, on_device(): other = lax.ppermute(mine, 'batch', swap)  3.83 us
    ppermute x1, starting transfers between devices, on_device(): met = lax.ppermute(payload, 'batch', [(i, i ^ 2) for i in range(8)])  3.11 us
    ppermute x1, starting transfers between devices, on_device(): act_peer = lax.ppermute(act, 'batch', swap)  2.46 us
    ppermute x1, waiting for transfers between devices, on_device(): met = lax.ppermute(payload, 'batch', [(i, i ^ 2) for i in range(8)])  2.38 us
  transfers between devices with their start and end apart: 9, of which 7 were waited for; matrix products, arithmetic and copies ran while one was open for 0% of the time, Pallas kernels for 21%

profile of v5, /device:TPU:1, one launch (start us, length us, event | category | flops | bytes accessed | tf_op | source)
XLA Modules:
  0.0 101.1 jit_solution(13427605028939293765)
XLA Ops:
  0.6 0.0 copy-start.2
  0.6 3.6 %prep.1 = bf16[512,640]{1,0:T(8,128)(2,1)} custom-call(bf16[256,512]{1,0:T(8,128)(2,1)} %bitcast.27, bf16[256,512]{1,0:T(8,128)(2,1)} %bitcast.21, bf16[5,512,512]{2,1,0:T(8,128)(2,1)} %bitcast.15), custom_call_target="tpu_custom_call" | custom-call | flops 713031680 | bytes 3801088 | tf_op jit(solution)/shard_map/prep/pallas_call | solution.py:503
  4.2 9.2 %all-to-all-start = ((bf16[32,16,640]{2,1,0:T(8,128)(2,1)}), bf16[32,16,640]{2,1,0:T(8,128)(2,1)S(1)}, u32[]{:S(2)}, u32[]{:S(2)}) async-start(bf16[32,16,640]{2,1,0:T(8,128)(2,1)} %bitcast.20), calls=%async_computation | async-start | bytes 1310720 | tf_op jit(solution)/shard_map/all_to_all | solution.py:520
  13.5 0.0 copy-done.2
  13.5 1.0 %collective-permute-start = (bf16[256,512]{1,0:T(8,128)(2,1)S(1)}, bf16[256,512]{1,0:T(8,128)(2,1)S(1)}, u32[]{:S(2)}, u32[]{:S(2)}) collective-permute-start(bf16[256,512]{1,0:T(8,128)(2,1)S(1)} %bitcast.23), channel_id=1, source_target_pairs={{0,1},{1,0},{2,3},{3,2},{4,5},{5,4},{6,7},{7,6},{8,9},{9,8},{10,11... | collective-permute-start | bytes 786440 | tf_op jit(solution)/shard_map/ppermute | solution.py:550
  14.5 8.0 %taps.1 = (bf16[128,8192]{1,0:T(8,128)(2,1)}, f32[64,8192]{1,0:T(8,128)}, f32[16,8192]{1,0:T(8,128)}, f32[1024,256]{1,0:T(8,128)}, f32[16,128]{1,0:T(8,128)}) custom-call(f32[64,64]{1,0:T(8,128)} %wp_ref.1, f32[64,512]{1,0:T(8,128)} %wf_ref.1, f32[1,512]{1,0:T(1,128)} %bitcast.29, f32[1,512]{1,0:T(1,128)} %bitcast.30, ...), custom_call_target="tpu_custom_call" | custom-call | flops 1207959552 | bytes 8695808 | tf_op jit(solution)/shard_map/taps/pallas_call | solution.py:503
  22.5 0.0 collective-permute-done.peer_cot_hbm
  22.5 0.0 copy-start.4
  22.5 2.1 %all-to-all-done.recv_hbm.rest_0_ = bf16[32,16,640]{2,1,0:T(8,128)(2,1)S(1)} async-done(((bf16[32,16,640]{2,1,0:T(8,128)(2,1)}), bf16[32,16,640]{2,1,0:T(8,128)(2,1)S(1)}, u32[]{:S(2)}, u32[]{:S(2)}) %all-to-all-start) | async-done | bytes 655392 | tf_op jit(solution)/shard_map/all_to_all | solution.py:520
  24.7 0.0 copy-start.1
  24.7 0.9 copy-done.1
  25.5 4.6 %forward.1 = (bf16[32,16,384]{2,1,0:T(8,128)(2,1)}, f32[1024,128]{1,0:T(8,128)}, f32[1024,256]{1,0:T(8,128)}) custom-call(bf16[32,16,640]{2,1,0:T(8,128)(2,1)} %copy-done.1, f32[1024,256]{1,0:T(8,128)} %get-tuple-element.34.tspec_hbm.rest_3_, f32[16,128]{1,0:T(8,128)} %get-tuple-element.35.par_hbm.rest_4_, bf16[128,128]{1,0:T(8,128)(2,1)} %constant.18.clone.rest_0_.rest_9_, ...), custom_call_target="tpu_custom_call" | custom-call | flops 1207959552 | bytes 4349952 | tf_op jit(solution)/shard_map/forward/pallas_call | solution.py:503
  30.1 6.1 %all-to-all-start.1 = ((bf16[32,16,384]{2,1,0:T(8,128)(2,1)}), bf16[32,16,384]{2,1,0:T(8,128)(2,1)S(1)}, u32[]{:S(2)}, u32[]{:S(2)}) async-start(bf16[32,16,384]{2,1,0:T(8,128)(2,1)} %get-tuple-element.36), calls=%async_computation.1 | async-start | bytes 786432 | tf_op jit(solution)/shard_map/all_to_all | solution.py:520
  36.2 7.8 %backward.1 = (bf16[32,16,256]{2,1,0:T(8,128)(2,1)}, f32[2,32,128]{2,1,0:T(8,128)}) custom-call(bf16[32,16,640]{2,1,0:T(8,128)(2,1)} %copy-done.1, f32[1024,128]{1,0:T(8,128)} %get-tuple-element.37.rest_1_, f32[1024,256]{1,0:T(8,128)} %get-tuple-element.38.rest_2_, f32[1024,256]{1,0:T(8,128)} %get-tuple-element.34.tspec_hbm.rest_3_, ...), custom_call_target="tpu_custom_call" | custom-call | flops 2415919104 | bytes 11067392 | tf_op jit(solution)/shard_map/backward/pallas_call | solution.py:503
  44.1 0.0 copy-done.4
  44.1 0.8 all-to-all-done.1
  44.8 0.0 copy-start
  44.8 2.5 %collective-permute-start.1 = (bf16[512,384]{1,0:T(8,128)(2,1)S(1)}, bf16[512,384]{1,0:T(8,128)(2,1)S(1)}, u32[]{:S(2)}, u32[]{:S(2)}) collective-permute-start(bf16[512,384]{1,0:T(8,128)(2,1)S(1)} %bitcast.17), channel_id=1, source_target_pairs={{0,1},{1,0},{2,3},{3,2},{4,5},{5,4},{6,7},{7,6},{8,9},{9,8},{10,11... | collective-permute-start | bytes 1179656 | tf_op jit(solution)/shard_map/ppermute | solution.py:624
  47.3 0.0 collective-permute-start.2
  47.3 1.5 %collective-permute-done.2.peer_small_hbm = f32[2,32,128]{2,1,0:T(8,128)S(1)} collective-permute-done((f32[2,32,128]{2,1,0:T(8,128)}, f32[2,32,128]{2,1,0:T(8,128)S(1)}, u32[]{:S(2)}, u32[]{:S(2)}) %collective-permute-start.2) | collective-permute-done | bytes 32800 | tf_op jit(solution)/shard_map/ppermute | solution.py:625
  48.8 0.0 copy-start.5
  48.8 0.0 collective-permute-done.1.peer_act_hbm
  48.8 0.0 copy-start.3
  48.8 0.0 copy-done
  48.8 0.6 copy-done.5
  49.4 0.1 copy-done.3
  49.5 3.5 %conv_grad.1._ = bf16[512,1792]{1,0:T(8,128)(2,1)} custom-call(bf16[512,384]{1,0:T(8,128)(2,1)} %bitcast.18, bf16[512,384]{1,0:T(8,128)(2,1)} %copy-done.3, bf16[256,512]{1,0:T(8,128)(2,1)} %bitcast.22, bf16[256,512]{1,0:T(8,128)(2,1)} %copy-done.4, bf16[512,256]{1,0:T(8,128)(2,1)} %bitcast.25, f32[2,32,128]{2,1,0:T(8,128)} %get-tuple-element.47.small_hbm, ...), custom_call_target="tpu_custom_call" | custom-call | flops 671088640 | bytes 3473408 | tf_op jit(solution)/shard_map/conv_grad/pallas_call | solution.py:503
  53.0 5.6 %all-to-all-start.2 = ((bf16[32,16,1792]{2,1,0:T(8,128)(2,1)}), bf16[32,16,1792]{2,1,0:T(8,128)(2,1)S(1)}, u32[]{:S(2)}, u32[]{:S(2)}) async-start(bf16[32,16,1792]{2,1,0:T(8,128)(2,1)} %bitcast.14), calls=%async_computation.2 | async-start | bytes 3670016 | tf_op jit(solution)/shard_map/all_to_all | solution.py:520
  58.6 4.3 %mixed.1 = bf16[256,512]{1,0:T(8,128)(2,1)} custom-call(bf16[512,384]{1,0:T(8,128)(2,1)} %bitcast.19, bf16[5,512,512]{2,1,0:T(8,128)(2,1)} %bitcast.16, bf16[512,1792]{1,0:T(8,128)(2,1)} %conv_grad.1._), custom_call_target="tpu_custom_call" | custom-call | flops 713031680 | bytes 5111808 | tf_op jit(solution)/shard_map/mixed/pallas_call | solution.py:503
  63.0 20.6 %all-to-all-done.2.recv_ref = bf16[32,16,1792]{2,1,0:T(8,128)(2,1)S(1)} async-done(((bf16[32,16,1792]{2,1,0:T(8,128)(2,1)}), bf16[32,16,1792]{2,1,0:T(8,128)(2,1)S(1)}, u32[]{:S(2)}, u32[]{:S(2)}) %all-to-all-start.2) | async-done | bytes 1835040 | tf_op jit(solution)/shard_map/all_to_all | solution.py:520
  83.6 0.3 gather.1.own_ref
  84.0 3.1 %collective-permute-start.3 = (bf16[80,512]{1,0:T(8,128)(2,1)S(1)}, bf16[80,512]{1,0:T(8,128)(2,1)S(1)}, u32[]{:S(2)}, u32[]{:S(2)}) collective-permute-start(bf16[80,512]{1,0:T(8,128)(2,1)S(1)} %gather.1.own_ref), channel_id=1, source_target_pairs={{0,2},{1,3},{2,0},{3,1},{4,6},{5,7},{6,4},{7,5},{8,10},{9,11},{10,... | collective-permute-start | bytes 245768 | tf_op jit(solution)/shard_map/ppermute | solution.py:665
  87.1 2.4 %collective-permute-done.3.other_ref = bf16[80,512]{1,0:T(8,128)(2,1)S(1)} collective-permute-done((bf16[80,512]{1,0:T(8,128)(2,1)S(1)}, bf16[80,512]{1,0:T(8,128)(2,1)S(1)}, u32[]{:S(2)}, u32[]{:S(2)}) %collective-permute-start.3) | collective-permute-done | bytes 81952 | tf_op jit(solution)/shard_map/ppermute | solution.py:665
  89.5 4.0 %collective-permute-start.4 = (bf16[80,512]{1,0:T(8,128)(2,1)S(1)}, bf16[80,512]{1,0:T(8,128)(2,1)S(1)}, u32[]{:S(2)}, u32[]{:S(2)}) collective-permute-start(bf16[80,512]{1,0:T(8,128)(2,1)S(1)} %pair.1.own_ref), channel_id=1, source_target_pairs={{0,6},{1,7},{2,4},{3,5},{4,2},{5,3},{6,0},{7,1},{8,14},{9,15},{10,... | collective-permute-start | bytes 245768 | tf_op jit(solution)/shard_map/ppermute | solution.py:667
  93.5 0.8 input.1
  94.4 1.1 %collective-permute-done.4.other_ref = bf16[80,512]{1,0:T(8,128)(2,1)S(1)} collective-permute-done((bf16[80,512]{1,0:T(8,128)(2,1)S(1)}, bf16[80,512]{1,0:T(8,128)(2,1)S(1)}, u32[]{:S(2)}, u32[]{:S(2)}) %collective-permute-start.4) | collective-permute-done | bytes 81952 | tf_op jit(solution)/shard_map/ppermute | solution.py:667
  95.5 3.8 %collective-permute-start.5 = (f32[80,512]{1,0:T(8,128)S(1)}, f32[80,512]{1,0:T(8,128)S(1)}, u32[]{:S(2)}, u32[]{:S(2)}) collective-permute-start(f32[80,512]{1,0:T(8,128)S(1)} %final.1.mine_ref), channel_id=1, source_target_pairs={{0,1},{1,0},{2,3},{3,2},{4,5},{5,4},{6,7},{7,6},{8,9},{9,8},{10,11... | collective-permute-start | bytes 491528 | tf_op jit(solution)/shard_map/ppermute | solution.py:680
  99.3 1.0 %collective-permute-done.5.other_ref = f32[80,512]{1,0:T(8,128)S(1)} collective-permute-done((f32[80,512]{1,0:T(8,128)S(1)}, f32[80,512]{1,0:T(8,128)S(1)}, u32[]{:S(2)}, u32[]{:S(2)}) %collective-permute-start.5) | collective-permute-done | bytes 163872 | tf_op jit(solution)/shard_map/ppermute | solution.py:680
  100.3 0.8 join.1
  (2 shorter events, 0.1 us)
Async XLA Ops:
  0.6 12.8 %copy-start.2 = (bf16[1,256,512]{2,1,0:T(8,128)(2,1)S(1)}, bf16[1,256,512]{2,1,0:T(8,128)(2,1)}, u32[]{:S(2)}) copy-start(bf16[1,256,512]{2,1,0:T(8,128)(2,1)} %param.17) | copy-start | bytes 786436
  4.2 20.5 %all-to-all-start = ((bf16[32,16,640]{2,1,0:T(8,128)(2,1)}), bf16[32,16,640]{2,1,0:T(8,128)(2,1)S(1)}, u32[]{:S(2)}, u32[]{:S(2)}) async-start(bf16[32,16,640]{2,1,0:T(8,128)(2,1)} %bitcast.20), calls=%async_computation | async-start | bytes 1310720 | tf_op jit(solution)/shard_map/all_to_all | solution.py:520
  13.5 9.0 %collective-permute-start = (bf16[256,512]{1,0:T(8,128)(2,1)S(1)}, bf16[256,512]{1,0:T(8,128)(2,1)S(1)}, u32[]{:S(2)}, u32[]{:S(2)}) collective-permute-start(bf16[256,512]{1,0:T(8,128)(2,1)S(1)} %bitcast.23), channel_id=1, source_target_pairs={{0,1},{1,0},{2,3},{3,2},{4,5},{5,4},{6,7},{7,6},{8,9},{9,8},{10,11... | collective-permute-start | bytes 786440 | tf_op jit(solution)/shard_map/ppermute | solution.py:550
  22.5 21.5 %copy-start.4 = (bf16[256,512]{1,0:T(8,128)(2,1)}, bf16[256,512]{1,0:T(8,128)(2,1)S(1)}, u32[]{:S(2)}) copy-start(bf16[256,512]{1,0:T(8,128)(2,1)S(1)} %collective-permute-done.peer_cot_hbm) | copy-start | bytes 786436
  24.7 0.9 copy-start.1
  30.1 14.7 %all-to-all-start.1 = ((bf16[32,16,384]{2,1,0:T(8,128)(2,1)}), bf16[32,16,384]{2,1,0:T(8,128)(2,1)S(1)}, u32[]{:S(2)}, u32[]{:S(2)}) async-start(bf16[32,16,384]{2,1,0:T(8,128)(2,1)} %get-tuple-element.36), calls=%async_computation.1 | async-start | bytes 786432 | tf_op jit(solution)/shard_map/all_to_all | solution.py:520
  44.8 3.9 %copy-start = (bf16[32,16,384]{2,1,0:T(8,128)(2,1)}, bf16[32,16,384]{2,1,0:T(8,128)(2,1)S(1)}, u32[]{:S(2)}) copy-start(bf16[32,16,384]{2,1,0:T(8,128)(2,1)S(1)} %all-to-all-done.1) | copy-start | bytes 1179652
  44.8 3.9 %collective-permute-start.1 = (bf16[512,384]{1,0:T(8,128)(2,1)S(1)}, bf16[512,384]{1,0:T(8,128)(2,1)S(1)}, u32[]{:S(2)}, u32[]{:S(2)}) collective-permute-start(bf16[512,384]{1,0:T(8,128)(2,1)S(1)} %bitcast.17), channel_id=1, source_target_pairs={{0,1},{1,0},{2,3},{3,2},{4,5},{5,4},{6,7},{7,6},{8,9},{9,8},{10,11... | collective-permute-start | bytes 1179656 | tf_op jit(solution)/shard_map/ppermute | solution.py:624
  47.3 1.5 %collective-permute-start.2 = (f32[2,32,128]{2,1,0:T(8,128)}, f32[2,32,128]{2,1,0:T(8,128)S(1)}, u32[]{:S(2)}, u32[]{:S(2)}) collective-permute-start(f32[2,32,128]{2,1,0:T(8,128)} %get-tuple-element.47.small_hbm), channel_id=1, source_target_pairs={{0,1},{1,0},{2,3},{3,2},{4,5},{5,4},{6,7},{7,6},{8,9},{9,8},{10,11... | collective-permute-start | bytes 98312 | tf_op jit(solution)/shard_map/ppermute | solution.py:625
  48.8 0.6 copy-start.5
  48.8 0.8 copy-start.3
  53.0 30.6 %all-to-all-start.2 = ((bf16[32,16,1792]{2,1,0:T(8,128)(2,1)}), bf16[32,16,1792]{2,1,0:T(8,128)(2,1)S(1)}, u32[]{:S(2)}, u32[]{:S(2)}) async-start(bf16[32,16,1792]{2,1,0:T(8,128)(2,1)} %bitcast.14), calls=%async_computation.2 | async-start | bytes 3670016 | tf_op jit(solution)/shard_map/all_to_all | solution.py:520
  84.0 5.5 %collective-permute-start.3 = (bf16[80,512]{1,0:T(8,128)(2,1)S(1)}, bf16[80,512]{1,0:T(8,128)(2,1)S(1)}, u32[]{:S(2)}, u32[]{:S(2)}) collective-permute-start(bf16[80,512]{1,0:T(8,128)(2,1)S(1)} %gather.1.own_ref), channel_id=1, source_target_pairs={{0,2},{1,3},{2,0},{3,1},{4,6},{5,7},{6,4},{7,5},{8,10},{9,11},{10,... | collective-permute-start | bytes 245768 | tf_op jit(solution)/shard_map/ppermute | solution.py:665
  89.5 6.0 %collective-permute-start.4 = (bf16[80,512]{1,0:T(8,128)(2,1)S(1)}, bf16[80,512]{1,0:T(8,128)(2,1)S(1)}, u32[]{:S(2)}, u32[]{:S(2)}) collective-permute-start(bf16[80,512]{1,0:T(8,128)(2,1)S(1)} %pair.1.own_ref), channel_id=1, source_target_pairs={{0,6},{1,7},{2,4},{3,5},{4,2},{5,3},{6,0},{7,1},{8,14},{9,15},{10,... | collective-permute-start | bytes 245768 | tf_op jit(solution)/shard_map/ppermute | solution.py:667
  95.5 4.9 %collective-permute-start.5 = (f32[80,512]{1,0:T(8,128)S(1)}, f32[80,512]{1,0:T(8,128)S(1)}, u32[]{:S(2)}, u32[]{:S(2)}) collective-permute-start(f32[80,512]{1,0:T(8,128)S(1)} %final.1.mine_ref), channel_id=1, source_target_pairs={{0,1},{1,0},{2,3},{3,2},{4,5},{5,4},{6,7},{7,6},{8,9},{9,8},{10,11... | collective-permute-start | bytes 491528 | tf_op jit(solution)/shard_map/ppermute | solution.py:680

commit v6 on v5

--- a/solution.py
+++ b/solution.py
@@ -29,6 +29,7 @@
 CONV = KERNEL * HALF
 BLOCK = 4096
 CHUNK = 128
+SLICE = 8
 SCALE = 1.0 / math.sqrt(8 * LENGTH)
 
 
@@ -275,14 +276,19 @@
     from_spectrum(product(tspec_ref[...], spec, False), y_ref, tabs, loads)
     par_load.wait()
     gain = par_ref[:, FEAT + 1 : FEAT + 2][None]
-    before = y_ref[...].reshape(STEPS, OWN, LANES) + gain * x_ref[...].reshape(STEPS, OWN, LANES)
-    y_ref[...] = before.reshape(STACK, LANES)
+    act_ref[0, :, :HALO] = jnp.zeros((OWN, LANES), BF16)
+    for p in range(0, STEPS, SLICE):
+        rows = slice(p * OWN, (p + SLICE) * OWN)
+        before = y_ref[rows, :].reshape(SLICE, OWN, LANES) + gain * x_ref[rows, :].reshape(SLICE, OWN, LANES)
+        y_ref[rows, :] = before.reshape(SLICE * OWN, LANES)
+        active = gelu_parts(before)[0].astype(BF16)
+        h, at = divmod(p, SHARDS)
+        act_ref[at : at + SLICE, :, HALO + h * LANES : HALO + (h + 1) * LANES] = active
+        if h == 1:
+            kept = min(SLICE, SHARDS - 1 - at)
+            act_ref[at + 1 : at + 1 + kept, :, :HALO] = active[:kept]
     before_save = pltpu.make_async_copy(y_ref, before_hbm, sems.at[12])
     before_save.start()
-    active = gelu_parts(before)[0].astype(BF16)
-    act_ref[:, :, HALO : HALO + LANES] = active[:SHARDS]
-    act_ref[:, :, HALO + LANES :] = active[SHARDS:]
-    act_ref[:, :, :HALO] = jnp.concatenate([jnp.zeros((1, OWN, LANES), BF16), active[SHARDS:-1]], axis=0)
     act_save = pltpu.make_async_copy(act_ref, act_hbm, sems.at[13])
     act_save.start()
     spec_save.wait()
@@ -301,23 +307,31 @@
     for copy in (*first[:2], *table, *first[2:]):
         copy.start()
     wait_for(first, 0, 1)
-    early = recv_ref[:, :, ROWS + HALO : ROWS + HALO + LANES].astype(F32)
-    late = recv_ref[:, :, ROWS + HALO + LANES :].astype(F32)
-    edge = recv_ref[:, :, ROWS : ROWS + HALO].astype(F32)
-    edge = jnp.concatenate([edge[1:], jnp.zeros((1, OWN, LANES), F32)], axis=0)
-    grad_active = jnp.concatenate([early, late + edge], axis=0)
-    slope = gelu_parts(before_ref[...])[1].reshape(STEPS, OWN, LANES)
-    grad = (grad_active * slope).astype(BF16).astype(F32)
-    gb_ref[...] = grad.reshape(STACK, LANES)
-    x = jnp.concatenate([recv_ref[:, :, :LANES].astype(F32), recv_ref[:, :, LANES:ROWS].astype(F32)], axis=0)
-    skip = jnp.sum(jnp.sum(grad * x, axis=0), axis=1, keepdims=True)
+    skip = jnp.zeros((OWN, LANES), F32)
+    for p in range(0, STEPS, SLICE):
+        rows = slice(p * OWN, (p + SLICE) * OWN)
+        h, at = divmod(p, SHARDS)
+        part = slice(at, at + SLICE)
+        grad = recv_ref[part, :, ROWS + HALO + h * LANES : ROWS + HALO + (h + 1) * LANES].astype(F32)
+        if h == 1:
+            edge = recv_ref[at + 1 : min(at + 1 + SLICE, SHARDS), :, ROWS : ROWS + HALO].astype(F32)
+            if at + SLICE == SHARDS:
+                edge = jnp.concatenate([edge, jnp.zeros((1, OWN, LANES), F32)], axis=0)
+            grad = grad + edge
+        grad = grad * gelu_parts(before_ref[rows, :].reshape(SLICE, OWN, LANES))[1]
+        grad = grad.astype(BF16).astype(F32)
+        gb_ref[rows, :] = grad.reshape(SLICE * OWN, LANES)
+        skip = skip + jnp.sum(grad * recv_ref[part, :, h * LANES : (h + 1) * LANES].astype(F32), axis=0)
+    skip = jnp.sum(skip, axis=1, keepdims=True)
     spec = spectrum(gb_ref, vh_ref, vl_ref, tabs, table)
     wait_for(first, 2, 3, 4)
     from_spectrum(product(tspec_ref[...], spec, True), y_ref, tabs, table)
     gain = par_ref[:, FEAT + 1 : FEAT + 2][None]
-    result = (y_ref[...].reshape(STEPS, OWN, LANES) + gain * grad).astype(BF16)
-    ig_ref[:, :, :LANES] = result[:SHARDS]
-    ig_ref[:, :, LANES:] = result[SHARDS:]
+    for p in range(0, STEPS, SLICE):
+        rows = slice(p * OWN, (p + SLICE) * OWN)
+        h, at = divmod(p, SHARDS)
+        result = y_ref[rows, :].reshape(SLICE, OWN, LANES) + gain * gb_ref[rows, :].reshape(SLICE, OWN, LANES)
+        ig_ref[at : at + SLICE, :, h * LANES : (h + 1) * LANES] = result.astype(BF16)
     save = pltpu.make_async_copy(ig_ref, ig_hbm, sems.at[17])
     save.start()
     from_spectrum(product(xspec_ref[...], spec, True), y_ref, tabs)
@@ -506,7 +520,7 @@
         in_specs=specs or [VMEM] * len(args),
         out_specs=out_specs or (VMEM if single else [VMEM] * len(outs)),
         scratch_shapes=list(scratch),
-        compiler_params=pltpu.CompilerParams(vmem_limit_bytes=limit * 1024 * 1024),
+        compiler_params=pltpu.CompilerParams(vmem_limit_bytes=int(limit * 1024 * 1024)),
         cost_estimate=pl.CostEstimate(flops=flops, bytes_accessed=moved, transcendentals=0),
         name=name,
     )(*args)
@@ -568,6 +582,7 @@
         flops=flops * 2,
         name="taps",
         out_specs=[HBM] * 5,
+        limit=63.5,
     )
     act_message, before, sig_spec = call(
         forward_kernel,
@@ -619,6 +634,7 @@
         name="backward",
         specs=[HBM] * 17,
         out_specs=[HBM] * 2,
+        limit=63.75,
     )
     act, ig_message, small = lax.optimization_barrier((act, ig_message, small))
     act_peer = lax.ppermute(act, "batch", swap)

time: 102 us -> 101 us (level)
  waiting for transfers between devices: 29.5 us -> 31.1 us
  starting transfers between devices: 35.4 us -> 34.2 us
where the time goes in v6:
time: 101 us; the launch traced here: 100 us
  starting transfers between devices  34.2 us (34%)
  Pallas kernels  33.4 us (33%)
  waiting for transfers between devices  31.1 us (31%)
    pallas_call x11, Pallas kernels, call(): pl.pallas_call(kernel, out_shape=out_shape, in_specs=specs or [VMEM] * le...  33.4 us
    all_to_all x3, waiting for transfers between devices, regroup(): return lax.all_to_all(blocks, 'tm', split_axis=0, concat_axis=0, tiled=True)  23.8 us
    all_to_all x3, starting transfers between devices, regroup(): return lax.all_to_all(blocks, 'tm', split_axis=0, concat_axis=0, tiled=True)  20.9 us
    ppermute x1, starting transfers between devices, on_device(): other = lax.ppermute(mine, 'batch', swap)  3.41 us
    ppermute x1, waiting for transfers between devices, on_device(): met = lax.ppermute(payload, 'batch', [(i, i ^ 2) for i in range(8)])  3.26 us
    ppermute x1, starting transfers between devices, on_device(): met = lax.ppermute(pair, 'batch', [(i, i ^ 6) for i in range(8)])  3.16 us
    ppermute x1, starting transfers between devices, on_device(): met = lax.ppermute(payload, 'batch', [(i, i ^ 2) for i in range(8)])  3.08 us
    ppermute x1, starting transfers between devices, on_device(): act_peer = lax.ppermute(act, 'batch', swap)  2.58 us
  transfers between devices with their start and end apart: 9, of which 7 were waited for; matrix products, arithmetic and copies ran while one was open for 0% of the time, Pallas kernels for 21%

profile of v6, /device:TPU:1, one launch (start us, length us, event | category | flops | bytes accessed | tf_op | source)
XLA Modules:
  0.0 100.3 jit_solution(15707545170558864809)
XLA Ops:
  0.6 0.0 copy-start
  0.6 3.6 %prep.1 = bf16[512,640]{1,0:T(8,128)(2,1)} custom-call(bf16[256,512]{1,0:T(8,128)(2,1)} %bitcast.24, bf16[256,512]{1,0:T(8,128)(2,1)} %bitcast.18, bf16[5,512,512]{2,1,0:T(8,128)(2,1)} %bitcast.15), custom_call_target="tpu_custom_call" | custom-call | flops 713031680 | bytes 3801088 | tf_op jit(solution)/shard_map/prep/pallas_call | solution.py:517
  4.2 9.3 %all-to-all-start = ((bf16[32,16,640]{2,1,0:T(8,128)(2,1)}), bf16[32,16,640]{2,1,0:T(8,128)(2,1)}, u32[]{:S(2)}, u32[]{:S(2)}) async-start(bf16[32,16,640]{2,1,0:T(8,128)(2,1)} %bitcast.17), calls=%async_computation | async-start | bytes 1310720 | tf_op jit(solution)/shard_map/all_to_all | solution.py:534
  13.6 0.0 copy-done
  13.6 1.0 %collective-permute-start = (bf16[256,512]{1,0:T(8,128)(2,1)S(1)}, bf16[256,512]{1,0:T(8,128)(2,1)}, u32[]{:S(2)}, u32[]{:S(2)}) collective-permute-start(bf16[256,512]{1,0:T(8,128)(2,1)S(1)} %bitcast.20), channel_id=1, source_target_pairs={{0,1},{1,0},{2,3},{3,2},{4,5},{5,4},{6,7},{7,6},{8,9},{9,8},{10,11... | collective-permute-start | bytes 786440 | tf_op jit(solution)/shard_map/ppermute | solution.py:564
  14.6 8.0 %taps.1 = (bf16[128,8192]{1,0:T(8,128)(2,1)}, f32[64,8192]{1,0:T(8,128)}, f32[16,8192]{1,0:T(8,128)}, f32[1024,256]{1,0:T(8,128)}, f32[16,128]{1,0:T(8,128)}) custom-call(f32[64,64]{1,0:T(8,128)} %wp_ref.1, f32[64,512]{1,0:T(8,128)} %wf_ref.1, f32[1,512]{1,0:T(1,128)} %bitcast.26, f32[1,512]{1,0:T(1,128)} %bitcast.27, ...), custom_call_target="tpu_custom_call" | custom-call | flops 1207959552 | bytes 8695808 | tf_op jit(solution)/shard_map/taps/pallas_call | solution.py:517
  22.6 0.0 collective-permute-done.peer_cot_hbm
  22.6 2.1 %all-to-all-done.recv_hbm.rest_0_ = bf16[32,16,640]{2,1,0:T(8,128)(2,1)} async-done(((bf16[32,16,640]{2,1,0:T(8,128)(2,1)}), bf16[32,16,640]{2,1,0:T(8,128)(2,1)}, u32[]{:S(2)}, u32[]{:S(2)}) %all-to-all-start) | async-done | bytes 655392 | tf_op jit(solution)/shard_map/all_to_all | solution.py:534
  24.8 4.5 %forward.1 = (bf16[32,16,384]{2,1,0:T(8,128)(2,1)}, f32[1024,128]{1,0:T(8,128)}, f32[1024,256]{1,0:T(8,128)}) custom-call(bf16[32,16,640]{2,1,0:T(8,128)(2,1)} %all-to-all-done.recv_hbm.rest_0_, f32[1024,256]{1,0:T(8,128)} %get-tuple-element.34.tspec_hbm.rest_3_, f32[16,128]{1,0:T(8,128)} %get-tuple-element.35.par_hbm.rest_4_, ...), custom_call_target="tpu_custom_call" | custom-call | flops 1207959552 | bytes 4349952 | tf_op jit(solution)/shard_map/forward/pallas_call | solution.py:517
  29.3 6.1 %all-to-all-start.1 = ((bf16[32,16,384]{2,1,0:T(8,128)(2,1)}), bf16[32,16,384]{2,1,0:T(8,128)(2,1)}, u32[]{:S(2)}, u32[]{:S(2)}) async-start(bf16[32,16,384]{2,1,0:T(8,128)(2,1)} %get-tuple-element.36), calls=%async_computation.1 | async-start | bytes 786432 | tf_op jit(solution)/shard_map/all_to_all | solution.py:534
  35.4 7.5 %backward.1 = (bf16[32,16,256]{2,1,0:T(8,128)(2,1)}, f32[2,32,128]{2,1,0:T(8,128)}) custom-call(bf16[32,16,640]{2,1,0:T(8,128)(2,1)} %all-to-all-done.recv_hbm.rest_0_, f32[1024,128]{1,0:T(8,128)} %get-tuple-element.37.rest_1_, f32[1024,256]{1,0:T(8,128)} %get-tuple-element.38.rest_2_, f32[1024,256]{1,0:T(8,128)} %get-tuple-element.34.tspec_hbm.rest_3_, ...), custom_call_target="tpu_custom_call" | custom-call | flops 2415919104 | bytes 11067392 | tf_op jit(solution)/shard_map/backward/pallas_call | solution.py:517
  42.9 1.0 all-to-all-done.1
  43.9 2.6 %collective-permute-start.1 = (bf16[512,384]{1,0:T(8,128)(2,1)}, bf16[512,384]{1,0:T(8,128)(2,1)S(1)}, u32[]{:S(2)}, u32[]{:S(2)}) collective-permute-start(bf16[512,384]{1,0:T(8,128)(2,1)} %bitcast.6.act_hbm), channel_id=1, source_target_pairs={{0,1},{1,0},{2,3},{3,2},{4,5},{5,4},{6,7},{7,6},{8,9},{9,8},{10,11... | collective-permute-start | bytes 1179656 | tf_op jit(solution)/shard_map/ppermute | solution.py:640
  46.5 0.0 collective-permute-start.2
  46.5 1.6 %collective-permute-done.2.peer_small_hbm = f32[2,32,128]{2,1,0:T(8,128)S(1)} collective-permute-done((f32[2,32,128]{2,1,0:T(8,128)}, f32[2,32,128]{2,1,0:T(8,128)S(1)}, u32[]{:S(2)}, u32[]{:S(2)}) %collective-permute-start.2) | collective-permute-done | bytes 32800 | tf_op jit(solution)/shard_map/ppermute | solution.py:641
  48.1 0.0 copy-start.2
  48.1 0.0 collective-permute-done.1.peer_act_hbm
  48.1 0.0 copy-start.1
  48.1 0.6 copy-done.2
  48.7 0.1 copy-done.1
  48.8 3.5 %conv_grad.1._ = bf16[512,1792]{1,0:T(8,128)(2,1)} custom-call(bf16[512,384]{1,0:T(8,128)(2,1)} %bitcast.6.act_hbm, bf16[512,384]{1,0:T(8,128)(2,1)} %copy-done.1, bf16[256,512]{1,0:T(8,128)(2,1)} %bitcast.19, bf16[256,512]{1,0:T(8,128)(2,1)} %collective-permute-done.peer_cot_hbm, bf16[512,256]{1,0:T(8,128)(2,1)} %bitcast.22, ...), custom_call_target="tpu_custom_call" | custom-call | flops 671088640 | bytes 3473408 | tf_op jit(solution)/shard_map/conv_grad/pallas_call | solution.py:517
  52.4 5.4 %all-to-all-start.2 = ((bf16[32,16,1792]{2,1,0:T(8,128)(2,1)}), bf16[32,16,1792]{2,1,0:T(8,128)(2,1)S(1)}, u32[]{:S(2)}, u32[]{:S(2)}) async-start(bf16[32,16,1792]{2,1,0:T(8,128)(2,1)} %bitcast.14), calls=%async_computation.2 | async-start | bytes 3670016 | tf_op jit(solution)/shard_map/all_to_all | solution.py:534
  57.8 4.3 %mixed.1 = bf16[256,512]{1,0:T(8,128)(2,1)} custom-call(bf16[512,384]{1,0:T(8,128)(2,1)} %bitcast.6.act_hbm, bf16[5,512,512]{2,1,0:T(8,128)(2,1)} %bitcast.16, bf16[512,1792]{1,0:T(8,128)(2,1)} %conv_grad.1._), custom_call_target="tpu_custom_call" | custom-call | flops 713031680 | bytes 5111808 | tf_op jit(solution)/shard_map/mixed/pallas_call | solution.py:517
  62.2 20.7 %all-to-all-done.2.recv_ref = bf16[32,16,1792]{2,1,0:T(8,128)(2,1)S(1)} async-done(((bf16[32,16,1792]{2,1,0:T(8,128)(2,1)}), bf16[32,16,1792]{2,1,0:T(8,128)(2,1)S(1)}, u32[]{:S(2)}, u32[]{:S(2)}) %all-to-all-start.2) | async-done | bytes 1835040 | tf_op jit(solution)/shard_map/all_to_all | solution.py:534
  82.8 0.3 gather.1.own_ref
  83.2 3.1 %collective-permute-start.3 = (bf16[80,512]{1,0:T(8,128)(2,1)S(1)}, bf16[80,512]{1,0:T(8,128)(2,1)S(1)}, u32[]{:S(2)}, u32[]{:S(2)}) collective-permute-start(bf16[80,512]{1,0:T(8,128)(2,1)S(1)} %gather.1.own_ref), channel_id=1, source_target_pairs={{0,2},{1,3},{2,0},{3,1},{4,6},{5,7},{6,4},{7,5},{8,10},{9,11},{10,... | collective-permute-start | bytes 245768 | tf_op jit(solution)/shard_map/ppermute | solution.py:681
  86.3 3.3 %collective-permute-done.3.other_ref = bf16[80,512]{1,0:T(8,128)(2,1)S(1)} collective-permute-done((bf16[80,512]{1,0:T(8,128)(2,1)S(1)}, bf16[80,512]{1,0:T(8,128)(2,1)S(1)}, u32[]{:S(2)}, u32[]{:S(2)}) %collective-permute-start.3) | collective-permute-done | bytes 81952 | tf_op jit(solution)/shard_map/ppermute | solution.py:681
  89.6 3.2 %collective-permute-start.4 = (bf16[80,512]{1,0:T(8,128)(2,1)S(1)}, bf16[80,512]{1,0:T(8,128)(2,1)S(1)}, u32[]{:S(2)}, u32[]{:S(2)}) collective-permute-start(bf16[80,512]{1,0:T(8,128)(2,1)S(1)} %pair.1.own_ref), channel_id=1, source_target_pairs={{0,6},{1,7},{2,4},{3,5},{4,2},{5,3},{6,0},{7,1},{8,14},{9,15},{10,... | collective-permute-start | bytes 245768 | tf_op jit(solution)/shard_map/ppermute | solution.py:683
  92.7 0.8 input.1
  93.6 1.5 %collective-permute-done.4.other_ref = bf16[80,512]{1,0:T(8,128)(2,1)S(1)} collective-permute-done((bf16[80,512]{1,0:T(8,128)(2,1)S(1)}, bf16[80,512]{1,0:T(8,128)(2,1)S(1)}, u32[]{:S(2)}, u32[]{:S(2)}) %collective-permute-start.4) | collective-permute-done | bytes 81952 | tf_op jit(solution)/shard_map/ppermute | solution.py:683
  95.1 3.4 %collective-permute-start.5 = (f32[80,512]{1,0:T(8,128)S(1)}, f32[80,512]{1,0:T(8,128)S(1)}, u32[]{:S(2)}, u32[]{:S(2)}) collective-permute-start(f32[80,512]{1,0:T(8,128)S(1)} %final.1.mine_ref), channel_id=1, source_target_pairs={{0,1},{1,0},{2,3},{3,2},{4,5},{5,4},{6,7},{7,6},{8,9},{9,8},{10,11... | collective-permute-start | bytes 491528 | tf_op jit(solution)/shard_map/ppermute | solution.py:696
  98.5 1.0 %collective-permute-done.5.other_ref = f32[80,512]{1,0:T(8,128)S(1)} collective-permute-done((f32[80,512]{1,0:T(8,128)S(1)}, f32[80,512]{1,0:T(8,128)S(1)}, u32[]{:S(2)}, u32[]{:S(2)}) %collective-permute-start.5) | collective-permute-done | bytes 163872 | tf_op jit(solution)/shard_map/ppermute | solution.py:696
  99.5 0.8 join.1
  (2 shorter events, 0.1 us)
Async XLA Ops:
  0.6 12.9 %copy-start = (bf16[1,256,512]{2,1,0:T(8,128)(2,1)S(1)}, bf16[1,256,512]{2,1,0:T(8,128)(2,1)}, u32[]{:S(2)}) copy-start(bf16[1,256,512]{2,1,0:T(8,128)(2,1)} %param.17) | copy-start | bytes 786436
  4.2 20.6 %all-to-all-start = ((bf16[32,16,640]{2,1,0:T(8,128)(2,1)}), bf16[32,16,640]{2,1,0:T(8,128)(2,1)}, u32[]{:S(2)}, u32[]{:S(2)}) async-start(bf16[32,16,640]{2,1,0:T(8,128)(2,1)} %bitcast.17), calls=%async_computation | async-start | bytes 1310720 | tf_op jit(solution)/shard_map/all_to_all | solution.py:534
  13.6 9.0 %collective-permute-start = (bf16[256,512]{1,0:T(8,128)(2,1)S(1)}, bf16[256,512]{1,0:T(8,128)(2,1)}, u32[]{:S(2)}, u32[]{:S(2)}) collective-permute-start(bf16[256,512]{1,0:T(8,128)(2,1)S(1)} %bitcast.20), channel_id=1, source_target_pairs={{0,1},{1,0},{2,3},{3,2},{4,5},{5,4},{6,7},{7,6},{8,9},{9,8},{10,11... | collective-permute-start | bytes 786440 | tf_op jit(solution)/shard_map/ppermute | solution.py:564
  29.3 14.6 %all-to-all-start.1 = ((bf16[32,16,384]{2,1,0:T(8,128)(2,1)}), bf16[32,16,384]{2,1,0:T(8,128)(2,1)}, u32[]{:S(2)}, u32[]{:S(2)}) async-start(bf16[32,16,384]{2,1,0:T(8,128)(2,1)} %get-tuple-element.36), calls=%async_computation.1 | async-start | bytes 786432 | tf_op jit(solution)/shard_map/all_to_all | solution.py:534
  43.9 4.2 %collective-permute-start.1 = (bf16[512,384]{1,0:T(8,128)(2,1)}, bf16[512,384]{1,0:T(8,128)(2,1)S(1)}, u32[]{:S(2)}, u32[]{:S(2)}) collective-permute-start(bf16[512,384]{1,0:T(8,128)(2,1)} %bitcast.6.act_hbm), channel_id=1, source_target_pairs={{0,1},{1,0},{2,3},{3,2},{4,5},{5,4},{6,7},{7,6},{8,9},{9,8},{10,11... | collective-permute-start | bytes 1179656 | tf_op jit(solution)/shard_map/ppermute | solution.py:640
  46.5 1.6 %collective-permute-start.2 = (f32[2,32,128]{2,1,0:T(8,128)}, f32[2,32,128]{2,1,0:T(8,128)S(1)}, u32[]{:S(2)}, u32[]{:S(2)}) collective-permute-start(f32[2,32,128]{2,1,0:T(8,128)} %get-tuple-element.47.small_hbm), channel_id=1, source_target_pairs={{0,1},{1,0},{2,3},{3,2},{4,5},{5,4},{6,7},{7,6},{8,9},{9,8},{10,11... | collective-permute-start | bytes 98312 | tf_op jit(solution)/shard_map/ppermute | solution.py:641
  48.1 0.6 copy-start.2
  48.1 0.8 copy-start.1
  52.4 30.5 %all-to-all-start.2 = ((bf16[32,16,1792]{2,1,0:T(8,128)(2,1)}), bf16[32,16,1792]{2,1,0:T(8,128)(2,1)S(1)}, u32[]{:S(2)}, u32[]{:S(2)}) async-start(bf16[32,16,1792]{2,1,0:T(8,128)(2,1)} %bitcast.14), calls=%async_computation.2 | async-start | bytes 3670016 | tf_op jit(solution)/shard_map/all_to_all | solution.py:534
  83.2 6.3 %collective-permute-start.3 = (bf16[80,512]{1,0:T(8,128)(2,1)S(1)}, bf16[80,512]{1,0:T(8,128)(2,1)S(1)}, u32[]{:S(2)}, u32[]{:S(2)}) collective-permute-start(bf16[80,512]{1,0:T(8,128)(2,1)S(1)} %gather.1.own_ref), channel_id=1, source_target_pairs={{0,2},{1,3},{2,0},{3,1},{4,6},{5,7},{6,4},{7,5},{8,10},{9,11},{10,... | collective-permute-start | bytes 245768 | tf_op jit(solution)/shard_map/ppermute | solution.py:681
  89.6 5.5 %collective-permute-start.4 = (bf16[80,512]{1,0:T(8,128)(2,1)S(1)}, bf16[80,512]{1,0:T(8,128)(2,1)S(1)}, u32[]{:S(2)}, u32[]{:S(2)}) collective-permute-start(bf16[80,512]{1,0:T(8,128)(2,1)S(1)} %pair.1.own_ref), channel_id=1, source_target_pairs={{0,6},{1,7},{2,4},{3,5},{4,2},{5,3},{6,0},{7,1},{8,14},{9,15},{10,... | collective-permute-start | bytes 245768 | tf_op jit(solution)/shard_map/ppermute | solution.py:683
  95.1 4.4 %collective-permute-start.5 = (f32[80,512]{1,0:T(8,128)S(1)}, f32[80,512]{1,0:T(8,128)S(1)}, u32[]{:S(2)}, u32[]{:S(2)}) collective-permute-start(f32[80,512]{1,0:T(8,128)S(1)} %final.1.mine_ref), channel_id=1, source_target_pairs={{0,1},{1,0},{2,3},{3,2},{4,5},{5,4},{6,7},{7,6},{8,9},{9,8},{10,11... | collective-permute-start | bytes 491528 | tf_op jit(solution)/shard_map/ppermute | solution.py:696

commit v7 on v6

--- a/solution.py
+++ b/solution.py
@@ -466,10 +466,6 @@
     out_ref[...] = jnp.concatenate([total[:72], last], axis=0).astype(BF16)
 
 
-def final_kernel(own_ref, other_ref, out_ref):
-    out_ref[...] = (own_ref[...].astype(F32) + other_ref[...].astype(F32)) * SCALE
-
-
 def input_kernel(recv_ref, out_hbm, out_ref, sem):
     out_ref[...] = jnp.transpose(recv_ref[:, :, CONV : CONV + ROWS].astype(F32).reshape(WIDTH, ROWS)).astype(BF16)
     save = pltpu.make_async_copy(out_ref, out_hbm, sem)
@@ -477,8 +473,12 @@
     save.wait()
 
 
-def join_kernel(mine_ref, other_ref, conv_ref, pos_ref, filt_ref, rates_ref, skip_ref):
+def join_kernel(
+    pair_ref, met_ref, peer_pair_ref, peer_met_ref, conv_ref, pos_ref, filt_ref, rates_ref, skip_ref, mine_ref, other_ref
+):
     core = lax.axis_index("batch") % 2
+    mine_ref[...] = (pair_ref[...].astype(F32) + met_ref[...].astype(F32)) * SCALE
+    other_ref[...] = (peer_pair_ref[...].astype(F32) + peer_met_ref[...].astype(F32)) * SCALE
 
     def write(low, high):
         for e, part in enumerate((low, high)):
@@ -691,9 +691,9 @@
         out_specs=HBM,
         limit=12,
     )
-    pair, input_grad = lax.optimization_barrier((pair, input_grad))
-    mine = call(final_kernel, shape((80, WIDTH)), (pair, met), name="final", limit=12)
-    other = lax.ppermute(mine, "batch", swap)
+    pair, met, input_grad = lax.optimization_barrier((pair, met, input_grad))
+    peer_met = lax.ppermute(met, "batch", swap)
+    peer_pair = lax.ppermute(pair, "batch", swap)
     conv_grad, pos_grad, filt_grad, rates_grad, skip_grad = call(
         join_kernel,
         [
@@ -703,7 +703,8 @@
             shape((1, WIDTH)),
             shape((1, WIDTH)),
         ],
-        (mine, other),
+        (pair, met, peer_pair, peer_met),
+        [pltpu.VMEM((80, WIDTH), F32)] * 2,
         name="join",
         limit=12,
     )

time: 101 us -> 101 us (level)
    ppermute x1 -> x2, starting transfers between devices: 3.41 us -> 3.32 us  [the longest x1 3.31 us: on_device(): peer_pair = lax.ppermute(pair, 'batch', swap)]
    pallas_call x11 -> x10, Pallas kernels: 33.4 us -> 33.5 us  [call(): pl.pallas_call(kernel, out_shape=out_shape, in_specs=specs or [VMEM] * le...]
  transfers between devices with their start and end apart: 9 -> 10, of which waited for: 7 -> 8; matrix products, arithmetic and copies ran while one was open for 0% -> 0% of each run, Pallas kernels for 21% -> 21%
where the time goes in v7:
time: 101 us
  starting transfers between devices  34.1 us (34%)
  Pallas kernels  33.5 us (33%)
  waiting for transfers between devices  31.4 us (31%)
    pallas_call x10, Pallas kernels, call(): pl.pallas_call(kernel, out_shape=out_shape, in_specs=specs or [VMEM] * le...  33.5 us
    all_to_all x3, waiting for transfers between devices, regroup(): return lax.all_to_all(blocks, 'tm', split_axis=0, concat_axis=0, tiled=True)  23.8 us
    all_to_all x3, starting transfers between devices, regroup(): return lax.all_to_all(blocks, 'tm', split_axis=0, concat_axis=0, tiled=True)  21 us
    ppermute x1, starting transfers between devices, on_device(): peer_pair = lax.ppermute(pair, 'batch', swap)  3.31 us
    ppermute x1, waiting for transfers between devices, on_device(): met = lax.ppermute(payload, 'batch', [(i, i ^ 2) for i in range(8)])  3.27 us
    ppermute x1, starting transfers between devices, on_device(): met = lax.ppermute(pair, 'batch', [(i, i ^ 6) for i in range(8)])  3.15 us
    ppermute x1, starting transfers between devices, on_device(): met = lax.ppermute(payload, 'batch', [(i, i ^ 2) for i in range(8)])  3.08 us
    ppermute x1, starting transfers between devices, on_device(): act_peer = lax.ppermute(act, 'batch', swap)  2.58 us
  transfers between devices with their start and end apart: 10, of which 8 were waited for; matrix products, arithmetic and copies ran while one was open for 0% of the time, Pallas kernels for 21%

profile of v7, /device:TPU:1, one launch (start us, length us, event | category | flops | bytes accessed | tf_op | source)
XLA Modules:
  0.0 100.5 jit_solution(12915617230713777779)
XLA Ops:
  0.6 0.0 copy-start
  0.6 3.6 %prep.1 = bf16[512,640]{1,0:T(8,128)(2,1)} custom-call(bf16[256,512]{1,0:T(8,128)(2,1)} %bitcast.24, bf16[256,512]{1,0:T(8,128)(2,1)} %bitcast.18, bf16[5,512,512]{2,1,0:T(8,128)(2,1)} %bitcast.15), custom_call_target="tpu_custom_call" | custom-call | flops 713031680 | bytes 3801088 | tf_op jit(solution)/shard_map/prep/pallas_call | solution.py:517
  4.2 9.3 %all-to-all-start = ((bf16[32,16,640]{2,1,0:T(8,128)(2,1)}), bf16[32,16,640]{2,1,0:T(8,128)(2,1)}, u32[]{:S(2)}, u32[]{:S(2)}) async-start(bf16[32,16,640]{2,1,0:T(8,128)(2,1)} %bitcast.17), calls=%async_computation | async-start | bytes 1310720 | tf_op jit(solution)/shard_map/all_to_all | solution.py:534
  13.6 0.0 copy-done
  13.6 1.0 %collective-permute-start = (bf16[256,512]{1,0:T(8,128)(2,1)S(1)}, bf16[256,512]{1,0:T(8,128)(2,1)}, u32[]{:S(2)}, u32[]{:S(2)}) collective-permute-start(bf16[256,512]{1,0:T(8,128)(2,1)S(1)} %bitcast.20), channel_id=1, source_target_pairs={{0,1},{1,0},{2,3},{3,2},{4,5},{5,4},{6,7},{7,6},{8,9},{9,8},{10,11... | collective-permute-start | bytes 786440 | tf_op jit(solution)/shard_map/ppermute | solution.py:564
  14.6 8.0 %taps.1 = (bf16[128,8192]{1,0:T(8,128)(2,1)}, f32[64,8192]{1,0:T(8,128)}, f32[16,8192]{1,0:T(8,128)}, f32[1024,256]{1,0:T(8,128)}, f32[16,128]{1,0:T(8,128)}) custom-call(f32[64,64]{1,0:T(8,128)} %wp_ref.1, f32[64,512]{1,0:T(8,128)} %wf_ref.1, f32[1,512]{1,0:T(1,128)} %bitcast.26, f32[1,512]{1,0:T(1,128)} %bitcast.27, ...), custom_call_target="tpu_custom_call" | custom-call | flops 1207959552 | bytes 8695808 | tf_op jit(solution)/shard_map/taps/pallas_call | solution.py:517
  22.6 0.0 collective-permute-done.peer_cot_hbm
  22.6 2.1 %all-to-all-done.recv_hbm.rest_0_ = bf16[32,16,640]{2,1,0:T(8,128)(2,1)} async-done(((bf16[32,16,640]{2,1,0:T(8,128)(2,1)}), bf16[32,16,640]{2,1,0:T(8,128)(2,1)}, u32[]{:S(2)}, u32[]{:S(2)}) %all-to-all-start) | async-done | bytes 655392 | tf_op jit(solution)/shard_map/all_to_all | solution.py:534
  24.8 4.5 %forward.1 = (bf16[32,16,384]{2,1,0:T(8,128)(2,1)}, f32[1024,128]{1,0:T(8,128)}, f32[1024,256]{1,0:T(8,128)}) custom-call(bf16[32,16,640]{2,1,0:T(8,128)(2,1)} %all-to-all-done.recv_hbm.rest_0_, f32[1024,256]{1,0:T(8,128)} %get-tuple-element.35.tspec_hbm.rest_3_, f32[16,128]{1,0:T(8,128)} %get-tuple-element.36.par_hbm.rest_4_, ...), custom_call_target="tpu_custom_call" | custom-call | flops 1207959552 | bytes 4349952 | tf_op jit(solution)/shard_map/forward/pallas_call | solution.py:517
  29.3 6.1 %all-to-all-start.1 = ((bf16[32,16,384]{2,1,0:T(8,128)(2,1)}), bf16[32,16,384]{2,1,0:T(8,128)(2,1)}, u32[]{:S(2)}, u32[]{:S(2)}) async-start(bf16[32,16,384]{2,1,0:T(8,128)(2,1)} %get-tuple-element.37), calls=%async_computation.1 | async-start | bytes 786432 | tf_op jit(solution)/shard_map/all_to_all | solution.py:534
  35.4 7.5 %backward.1 = (bf16[32,16,256]{2,1,0:T(8,128)(2,1)}, f32[2,32,128]{2,1,0:T(8,128)}) custom-call(bf16[32,16,640]{2,1,0:T(8,128)(2,1)} %all-to-all-done.recv_hbm.rest_0_, f32[1024,128]{1,0:T(8,128)} %get-tuple-element.38.rest_1_, f32[1024,256]{1,0:T(8,128)} %get-tuple-element.39.rest_2_, f32[1024,256]{1,0:T(8,128)} %get-tuple-element.35.tspec_hbm.rest_3_, ...), custom_call_target="tpu_custom_call" | custom-call | flops 2415919104 | bytes 11067392 | tf_op jit(solution)/shard_map/backward/pallas_call | solution.py:517
  42.9 1.0 all-to-all-done.1
  43.9 2.6 %collective-permute-start.1 = (bf16[512,384]{1,0:T(8,128)(2,1)}, bf16[512,384]{1,0:T(8,128)(2,1)S(1)}, u32[]{:S(2)}, u32[]{:S(2)}) collective-permute-start(bf16[512,384]{1,0:T(8,128)(2,1)} %bitcast.6.act_hbm), channel_id=1, source_target_pairs={{0,1},{1,0},{2,3},{3,2},{4,5},{5,4},{6,7},{7,6},{8,9},{9,8},{10,11... | collective-permute-start | bytes 1179656 | tf_op jit(solution)/shard_map/ppermute | solution.py:640
  46.5 0.0 collective-permute-start.2
  46.5 1.6 %collective-permute-done.2.peer_small_hbm = f32[2,32,128]{2,1,0:T(8,128)S(1)} collective-permute-done((f32[2,32,128]{2,1,0:T(8,128)}, f32[2,32,128]{2,1,0:T(8,128)S(1)}, u32[]{:S(2)}, u32[]{:S(2)}) %collective-permute-start.2) | collective-permute-done | bytes 32800 | tf_op jit(solution)/shard_map/ppermute | solution.py:641
  48.1 0.0 copy-start.2
  48.1 0.0 collective-permute-done.1.peer_act_hbm
  48.1 0.0 copy-start.1
  48.1 0.6 copy-done.2
  48.7 0.1 copy-done.1
  48.8 3.5 %conv_grad.1._ = bf16[512,1792]{1,0:T(8,128)(2,1)} custom-call(bf16[512,384]{1,0:T(8,128)(2,1)} %bitcast.6.act_hbm, bf16[512,384]{1,0:T(8,128)(2,1)} %copy-done.1, bf16[256,512]{1,0:T(8,128)(2,1)} %bitcast.19, bf16[256,512]{1,0:T(8,128)(2,1)} %collective-permute-done.peer_cot_hbm, bf16[512,256]{1,0:T(8,128)(2,1)} %bitcast.22, ...), custom_call_target="tpu_custom_call" | custom-call | flops 671088640 | bytes 3473408 | tf_op jit(solution)/shard_map/conv_grad/pallas_call | solution.py:517
  52.4 5.5 %all-to-all-start.2 = ((bf16[32,16,1792]{2,1,0:T(8,128)(2,1)}), bf16[32,16,1792]{2,1,0:T(8,128)(2,1)S(1)}, u32[]{:S(2)}, u32[]{:S(2)}) async-start(bf16[32,16,1792]{2,1,0:T(8,128)(2,1)} %bitcast.14), calls=%async_computation.2 | async-start | bytes 3670016 | tf_op jit(solution)/shard_map/all_to_all | solution.py:534
  57.9 4.3 %mixed.1 = bf16[256,512]{1,0:T(8,128)(2,1)} custom-call(bf16[512,384]{1,0:T(8,128)(2,1)} %bitcast.6.act_hbm, bf16[5,512,512]{2,1,0:T(8,128)(2,1)} %bitcast.16, bf16[512,1792]{1,0:T(8,128)(2,1)} %conv_grad.1._), custom_call_target="tpu_custom_call" | custom-call | flops 713031680 | bytes 5111808 | tf_op jit(solution)/shard_map/mixed/pallas_call | solution.py:517
  62.2 20.7 %all-to-all-done.2.recv_ref = bf16[32,16,1792]{2,1,0:T(8,128)(2,1)S(1)} async-done(((bf16[32,16,1792]{2,1,0:T(8,128)(2,1)}), bf16[32,16,1792]{2,1,0:T(8,128)(2,1)S(1)}, u32[]{:S(2)}, u32[]{:S(2)}) %all-to-all-start.2) | async-done | bytes 1835040 | tf_op jit(solution)/shard_map/all_to_all | solution.py:534
  82.9 0.3 gather.1.own_ref
  83.2 3.1 %collective-permute-start.3 = (bf16[80,512]{1,0:T(8,128)(2,1)S(1)}, bf16[80,512]{1,0:T(8,128)(2,1)S(1)}, u32[]{:S(2)}, u32[]{:S(2)}) collective-permute-start(bf16[80,512]{1,0:T(8,128)(2,1)S(1)} %gather.1.own_ref), channel_id=1, source_target_pairs={{0,2},{1,3},{2,0},{3,1},{4,6},{5,7},{6,4},{7,5},{8,10},{9,11},{10,... | collective-permute-start | bytes 245768 | tf_op jit(solution)/shard_map/ppermute | solution.py:681
  86.3 3.3 %collective-permute-done.3.other_ref = bf16[80,512]{1,0:T(8,128)(2,1)S(1)} collective-permute-done((bf16[80,512]{1,0:T(8,128)(2,1)S(1)}, bf16[80,512]{1,0:T(8,128)(2,1)S(1)}, u32[]{:S(2)}, u32[]{:S(2)}) %collective-permute-start.3) | collective-permute-done | bytes 81952 | tf_op jit(solution)/shard_map/ppermute | solution.py:681
  89.6 3.2 %collective-permute-start.4 = (bf16[80,512]{1,0:T(8,128)(2,1)S(1)}, bf16[80,512]{1,0:T(8,128)(2,1)S(1)}, u32[]{:S(2)}, u32[]{:S(2)}) collective-permute-start(bf16[80,512]{1,0:T(8,128)(2,1)S(1)} %pair.1.pair_ref), channel_id=1, source_target_pairs={{0,6},{1,7},{2,4},{3,5},{4,2},{5,3},{6,0},{7,1},{8,14},{9,15},{10,... | collective-permute-start | bytes 245768 | tf_op jit(solution)/shard_map/ppermute | solution.py:683
  92.7 0.8 input.1
  93.6 1.5 %collective-permute-done.4.met_ref = bf16[80,512]{1,0:T(8,128)(2,1)S(1)} collective-permute-done((bf16[80,512]{1,0:T(8,128)(2,1)S(1)}, bf16[80,512]{1,0:T(8,128)(2,1)S(1)}, u32[]{:S(2)}, u32[]{:S(2)}) %collective-permute-start.4) | collective-permute-done | bytes 81952 | tf_op jit(solution)/shard_map/ppermute | solution.py:683
  95.1 3.3 %collective-permute-start.5 = (bf16[80,512]{1,0:T(8,128)(2,1)S(1)}, bf16[80,512]{1,0:T(8,128)(2,1)S(1)}, u32[]{:S(2)}, u32[]{:S(2)}) collective-permute-start(bf16[80,512]{1,0:T(8,128)(2,1)S(1)} %pair.1.pair_ref), channel_id=1, source_target_pairs={{0,1},{1,0},{2,3},{3,2},{4,5},{5,4},{6,7},{7,6},{8,9},{9,8},{10,11... | collective-permute-start | bytes 245768 | tf_op jit(solution)/shard_map/ppermute | solution.py:696
  98.4 0.0 collective-permute-start.6
  98.4 0.9 collective-permute-done.5.peer_pair_ref
  99.3 0.4 collective-permute-done.6.peer_met_ref
  99.7 0.8 join.1
  (1 shorter events, 0.0 us)
Async XLA Ops:
  0.6 12.9 %copy-start = (bf16[1,256,512]{2,1,0:T(8,128)(2,1)S(1)}, bf16[1,256,512]{2,1,0:T(8,128)(2,1)}, u32[]{:S(2)}) copy-start(bf16[1,256,512]{2,1,0:T(8,128)(2,1)} %param.17) | copy-start | bytes 786436
  4.2 20.6 %all-to-all-start = ((bf16[32,16,640]{2,1,0:T(8,128)(2,1)}), bf16[32,16,640]{2,1,0:T(8,128)(2,1)}, u32[]{:S(2)}, u32[]{:S(2)}) async-start(bf16[32,16,640]{2,1,0:T(8,128)(2,1)} %bitcast.17), calls=%async_computation | async-start | bytes 1310720 | tf_op jit(solution)/shard_map/all_to_all | solution.py:534
  13.6 9.0 %collective-permute-start = (bf16[256,512]{1,0:T(8,128)(2,1)S(1)}, bf16[256,512]{1,0:T(8,128)(2,1)}, u32[]{:S(2)}, u32[]{:S(2)}) collective-permute-start(bf16[256,512]{1,0:T(8,128)(2,1)S(1)} %bitcast.20), channel_id=1, source_target_pairs={{0,1},{1,0},{2,3},{3,2},{4,5},{5,4},{6,7},{7,6},{8,9},{9,8},{10,11... | collective-permute-start | bytes 786440 | tf_op jit(solution)/shard_map/ppermute | solution.py:564
  29.3 14.6 %all-to-all-start.1 = ((bf16[32,16,384]{2,1,0:T(8,128)(2,1)}), bf16[32,16,384]{2,1,0:T(8,128)(2,1)}, u32[]{:S(2)}, u32[]{:S(2)}) async-start(bf16[32,16,384]{2,1,0:T(8,128)(2,1)} %get-tuple-element.37), calls=%async_computation.1 | async-start | bytes 786432 | tf_op jit(solution)/shard_map/all_to_all | solution.py:534
  43.9 4.2 %collective-permute-start.1 = (bf16[512,384]{1,0:T(8,128)(2,1)}, bf16[512,384]{1,0:T(8,128)(2,1)S(1)}, u32[]{:S(2)}, u32[]{:S(2)}) collective-permute-start(bf16[512,384]{1,0:T(8,128)(2,1)} %bitcast.6.act_hbm), channel_id=1, source_target_pairs={{0,1},{1,0},{2,3},{3,2},{4,5},{5,4},{6,7},{7,6},{8,9},{9,8},{10,11... | collective-permute-start | bytes 1179656 | tf_op jit(solution)/shard_map/ppermute | solution.py:640
  46.5 1.6 %collective-permute-start.2 = (f32[2,32,128]{2,1,0:T(8,128)}, f32[2,32,128]{2,1,0:T(8,128)S(1)}, u32[]{:S(2)}, u32[]{:S(2)}) collective-permute-start(f32[2,32,128]{2,1,0:T(8,128)} %get-tuple-element.48.small_hbm), channel_id=1, source_target_pairs={{0,1},{1,0},{2,3},{3,2},{4,5},{5,4},{6,7},{7,6},{8,9},{9,8},{10,11... | collective-permute-start | bytes 98312 | tf_op jit(solution)/shard_map/ppermute | solution.py:641
  48.1 0.6 copy-start.2
  48.1 0.7 copy-start.1
  52.4 30.5 %all-to-all-start.2 = ((bf16[32,16,1792]{2,1,0:T(8,128)(2,1)}), bf16[32,16,1792]{2,1,0:T(8,128)(2,1)S(1)}, u32[]{:S(2)}, u32[]{:S(2)}) async-start(bf16[32,16,1792]{2,1,0:T(8,128)(2,1)} %bitcast.14), calls=%async_computation.2 | async-start | bytes 3670016 | tf_op jit(solution)/shard_map/all_to_all | solution.py:534
  83.2 6.3 %collective-permute-start.3 = (bf16[80,512]{1,0:T(8,128)(2,1)S(1)}, bf16[80,512]{1,0:T(8,128)(2,1)S(1)}, u32[]{:S(2)}, u32[]{:S(2)}) collective-permute-start(bf16[80,512]{1,0:T(8,128)(2,1)S(1)} %gather.1.own_ref), channel_id=1, source_target_pairs={{0,2},{1,3},{2,0},{3,1},{4,6},{5,7},{6,4},{7,5},{8,10},{9,11},{10,... | collective-permute-start | bytes 245768 | tf_op jit(solution)/shard_map/ppermute | solution.py:681
  89.6 5.5 %collective-permute-start.4 = (bf16[80,512]{1,0:T(8,128)(2,1)S(1)}, bf16[80,512]{1,0:T(8,128)(2,1)S(1)}, u32[]{:S(2)}, u32[]{:S(2)}) collective-permute-start(bf16[80,512]{1,0:T(8,128)(2,1)S(1)} %pair.1.pair_ref), channel_id=1, source_target_pairs={{0,6},{1,7},{2,4},{3,5},{4,2},{5,3},{6,0},{7,1},{8,14},{9,15},{10,... | collective-permute-start | bytes 245768 | tf_op jit(solution)/shard_map/ppermute | solution.py:683
  95.1 4.2 %collective-permute-start.5 = (bf16[80,512]{1,0:T(8,128)(2,1)S(1)}, bf16[80,512]{1,0:T(8,128)(2,1)S(1)}, u32[]{:S(2)}, u32[]{:S(2)}) collective-permute-start(bf16[80,512]{1,0:T(8,128)(2,1)S(1)} %pair.1.pair_ref), channel_id=1, source_target_pairs={{0,1},{1,0},{2,3},{3,2},{4,5},{5,4},{6,7},{7,6},{8,9},{9,8},{10,11... | collective-permute-start | bytes 245768 | tf_op jit(solution)/shard_map/ppermute | solution.py:696
  98.4 1.3 %collective-permute-start.6 = (bf16[80,512]{1,0:T(8,128)(2,1)S(1)}, bf16[80,512]{1,0:T(8,128)(2,1)S(1)}, u32[]{:S(2)}, u32[]{:S(2)}) collective-permute-start(bf16[80,512]{1,0:T(8,128)(2,1)S(1)} %collective-permute-done.4.met_ref), channel_id=1, source_target_pairs={{0,1},{1,0},{2,3},{3,2},{4,5},{5,4},{6,7},{7,6},{8,9},{9,8},{10,11... | collective-permute-start | bytes 245768 | tf_op jit(solution)/shard_map/ppermute | solution.py:695
